TPU v7x, 256 devices: a whole 4x4x8 slice. The times are simulated.
256 devices in a mesh: dp: 16 (over z, core), expert: 16 (over x, y).
Axes of the slice: x: 4, y: 4, z: 8, core: 2. Of those that a mesh axis runs over, the one named last changes fastest.
Arguments:
- tokens: bfloat16 [32768, 2048], P(('dp', 'expert')), may hold values from -6 to 6
- expert_ids: int32 [32768, 2], P(('dp', 'expert')), may hold values from 0 to 15, as said below
- gate_weights: float32 [32768, 2], P(('dp', 'expert')), may hold values from 0.1 to 1
- w_gate: bfloat16 [16, 2048, 768], P('expert'), may hold values from -0.125 to 0.125
- w_up: bfloat16 [16, 2048, 768], P('expert'), may hold values from -0.125 to 0.125
- w_down: bfloat16 [16, 768, 2048], P('expert'), may hold values from -0.21875 to 0.21875
Outputs:
- mixed: bfloat16 [32768, 2048], P(('dp', 'expert'))
- aux_loss: float32 [], replicated
Inputs may be any that keep to these rules, and one draw needn't show every extreme that they name: `expert_ids`: each token names 2 different experts. Two experts, the same two on every device, are each named exactly 48 times by the rows of every device; among the rows of one device every other expert is named at most 12 times, possibly not at all, and some other expert exactly 12 times.
All inputs are finite; a program needn't handle non-finite values.
Results may differ from a plain program's by a relative error of at most 0.0025.
The roundings to bfloat16 on the way count: a program that leaves them out, or rounds other values in their place, can miss the bound.
Values may be sent and summed in bfloat16 or wider, within the bound.
No kernel may reach another device: no remote copies, remote signals or barrier semaphores. Data moves between devices by JAX's collectives and lax.ppermute only.
A program may use at most 128 MiB of HBM per device.

v0:
```python
import jax
import jax.numpy as jnp
from jax import lax
from jax.sharding import PartitionSpec as P


def on_device(tokens, expert_ids, gate_weights, w_gate, w_up, w_down):
    tok_rows, feature_width = tokens.shape
    pick_count = expert_ids.shape[1]
    local_experts = w_gate.shape[0]
    group_size = lax.axis_size("expert")
    experts = local_experts * group_size
    capacity = min(tok_rows * pick_count // 4, 3 * tok_rows * pick_count // experts)
    flat_ids = expert_ids.reshape(-1)
    flat_gates = gate_weights.reshape(-1)
    row_token = jnp.arange(tok_rows * pick_count, dtype=jnp.int32) // pick_count
    labels = jnp.arange(experts, dtype=jnp.int32)
    onehot = (flat_ids[:, None] == labels[None, :]).astype(jnp.int32)
    load_here = jnp.sum(onehot, 0).astype(jnp.float32)
    mass_here = jnp.sum(jnp.where(onehot > 0, flat_gates[:, None], jnp.float32(0.0)), 0)
    load_all, mass_all = lax.psum((load_here, mass_here), ("dp", "expert"))
    total_tokens = tok_rows * lax.axis_size("dp") * group_size
    aux_loss = experts * jnp.sum(load_all / (total_tokens * pick_count) * (mass_all / total_tokens))
    is_hot = jnp.zeros(flat_ids.shape, bool)
    rank = jnp.sum((jnp.cumsum(onehot, 0) - onehot) * onehot, 1)
    destination = flat_ids * capacity + rank
    slot_total = experts * capacity
    send_index = jnp.where(is_hot, slot_total, destination)
    outgoing = jnp.zeros((slot_total, feature_width), jnp.bfloat16)
    outgoing = outgoing.at[send_index].set(tokens[row_token], mode="drop")
    outgoing = outgoing.reshape(group_size, local_experts, capacity, feature_width)
    received = lax.all_to_all(outgoing, "expert", split_axis=0, concat_axis=0, tiled=True)
    gate_part = jnp.einsum("gend,edf->genf", received, w_gate, preferred_element_type=jnp.float32)
    up_part = jnp.einsum("gend,edf->genf", received, w_up, preferred_element_type=jnp.float32)
    hidden = (jax.nn.silu(gate_part) * up_part).astype(jnp.bfloat16)
    result = jnp.einsum("genf,efd->gend", hidden, w_down, preferred_element_type=jnp.float32)
    returned_rows = lax.all_to_all(
        result.astype(jnp.bfloat16), "expert", split_axis=0, concat_axis=0, tiled=True
    )
    returned_rows = returned_rows.reshape(slot_total, feature_width)
    slot_rows = returned_rows[jnp.minimum(destination, slot_total - 1)]
    weighted = jnp.where(
        is_hot[:, None], jnp.float32(0.0), flat_gates[:, None] * slot_rows.astype(jnp.float32)
    )
    mixed = jnp.sum(weighted.reshape(tok_rows, pick_count, feature_width), 1).astype(jnp.bfloat16)
    return (mixed, aux_loss)


def solution(mesh):
    in_specs = (
        P(("dp", "expert"), None),
        P(("dp", "expert"), None),
        P(("dp", "expert"), None),
        P("expert", None, None),
        P("expert", None, None),
        P("expert", None, None),
    )
    out_specs = (P(("dp", "expert"), None), P())
    return jax.shard_map(
        on_device, mesh=mesh, in_specs=in_specs, out_specs=out_specs, check_vma=False
    )
```

profile of v0, /device:TPU:1, one launch (start us, length us, event | category | flops | bytes accessed | tf_op | source)
XLA Modules:
  0.0 205.8 jit_solution(16969204139301911262)
XLA Ops:
  0.6 0.0 copy-start
  0.6 0.9 copy.17
  1.6 0.1 eq.29
  1.7 0.1 eq.25
  1.9 0.7 broadcast_multiply_fusion
  2.6 0.6 reduce-window.6
  3.2 0.2 slice_reduce_fusion
  3.4 0.1 copy.16
  3.5 0.1 mul.47
  3.7 0.1 convert_reduce_fusion
  3.8 7.8 %scatter_custom_fusion = bf16[768,2048]{1,0:T(8,128)(2,1)} fusion(s32[256]{0:T(256)S(1)} %bitcast.97, bf16[]{:T(256)} %constant.16.clone.1, bf16[128,2048]{1,0:T(8,128)(2,1)} %param.6, s32[1024]{0:T(1024)S(1)} %pad_clamp_fusion.1), kind=kCustom, calls=%fused_computation.20 | custom fusion | bytes 3146240 | tf_op jit(solution)/shard_map/scatter | solution.py:30
  11.6 0.0 copy-start.3
  11.6 45.8 %all_to_all.10 = bf16[16,1,48,2048]{3,2,1,0:T(8,128)(2,1)S(1)} all-to-all(bf16[16,1,48,2048]{3,2,1,0:T(8,128)(2,1)} %bitcast.93), channel_id=1, replica_groups=mesh['dp'=16,'expert'=16] {'expert'}, dimensions={0} | all-to-all | bytes 6291456 | tf_op jit(solution)/shard_map/all_to_all | solution.py:32
  57.3 0.0 copy-start.1
  57.4 1.7 copy-done.1
  59.1 0.0 copy-done.3
  59.1 4.0 %fusion.3 = f32[16,48,768]{2,1,0:T(8,128)} fusion(bf16[1,2048,768]{2,1,0:T(8,128)(2,1)S(1)} %copy-done.3, bf16[16,1,48,2048]{3,2,1,0:T(8,128)(2,1)S(1)} %all_to_all.10), kind=kOutput, calls=%fused_computation.7 | convolution fusion | flops 2415919104 | bytes 8650752 | tf_op jit(solution)/shard_map/gend,edf->genf/dot_general | solution.py:33
  63.1 0.0 copy-done
  63.1 11.0 %fusion.7 = bf16[16,1,48,2048]{3,2,1,0:T(8,128)(2,1)} fusion(bf16[1,768,2048]{2,1,0:T(8,128)(2,1)S(1)} %copy-done, bf16[1,2048,768]{2,1,0:T(8,128)(2,1)} %param.10, bf16[16,1,48,2048]{3,2,1,0:T(8,128)(2,1)} %copy-done.1, f32[16,48,768]{2,1,0:T(8,128)} %fusion.3), kind=kOutput, calls=%fused_computation.11 | convolution fusion | flops 4836950016 | bytes 14942208 | tf_op jit(solution)/shard_map/genf,efd->gend/dot_general | solution.py:36
  74.1 0.0 copy-start.2
  74.1 4.6 %all-to-all-start.1 = ((bf16[16,1,48,2048]{3,2,1,0:T(8,128)(2,1)}), bf16[16,1,48,2048]{3,2,1,0:T(8,128)(2,1)}, u32[]{:S(2)}, u32[]{:S(2)}) async-start(bf16[16,1,48,2048]{3,2,1,0:T(8,128)(2,1)} %fusion.7), calls=%async_computation.1 | async-start | bytes 6291456 | tf_op jit(solution)/shard_map/all_to_all | solution.py:37
  78.7 0.0 copy-done.2
  78.7 0.1 copy.15
  78.8 0.1 mul.52
  79.0 0.1 select_reduce_fusion
  79.1 109.7 %all-reduce = (f32[16]{0:T(128)S(1)}, f32[16]{0:T(128)S(1)}) all-reduce(f32[16]{0:T(128)S(1)} %select_reduce_fusion, f32[16]{0:T(128)S(1)} %convert_element_type.45), channel_id=1, replica_groups=mesh['dp'=16,'expert'=16] {'dp','expert'}, use_global_device_ids=true, to_apply=%region_8.9 | all-reduce | flops 32 | bytes 256 | tf_op jit(solution)/shard_map/psum | solution.py:21
  188.7 0.6 multiply_reduce_fusion.1
  190.0 0.0 all-to-all-done.1
  190.0 5.6 %gather_fusion = bf16[256,2048]{1,0:T(8,128)(2,1)} fusion(bf16[768,2048]{1,0:T(8,128)(2,1)} %bitcast.25, s32[1024]{0:T(1024)S(1)} %pad_clamp_fusion), kind=kCustom, calls=%fused_computation.1 | custom fusion | bytes 2098176 | tf_op jit(solution)/shard_map/gather | solution.py:41
  195.7 3.4 %reshape.160 = f32[128,2,2048]{2,1,0:T(2,128)} reshape(bf16[256,2048]{1,0:T(8,128)(2,1)} %gather_fusion) | data formatting | bytes 3145728 | tf_op jit(solution)/shard_map/convert_element_type | solution.py:43
  199.1 5.6 %multiply_reduce_fusion = bf16[128,2048]{1,0:T(8,128)(2,1)} fusion(f32[128,2,2048]{2,1,0:T(2,128)} %reshape.160, f32[128,2]{1,0:T(8,128)S(1)} %copy.15), kind=kLoop, calls=%fused_computation.19 | loop fusion | flops 786432 | bytes 2622464 | tf_op jit(solution)/shard_map/reduce_sum | solution.py:45
  (8 shorter events, 0.1 us)
Async XLA Ops:
  0.6 62.5 %copy-start = (bf16[1,768,2048]{2,1,0:T(8,128)(2,1)S(1)}, bf16[1,768,2048]{2,1,0:T(8,128)(2,1)}, u32[]{:S(2)}) copy-start(bf16[1,768,2048]{2,1,0:T(8,128)(2,1)} %param.11) | copy-start | bytes 9437188
  11.6 47.5 %copy-start.3 = (bf16[1,2048,768]{2,1,0:T(8,128)(2,1)S(1)}, bf16[1,2048,768]{2,1,0:T(8,128)(2,1)}, u32[]{:S(2)}) copy-start(bf16[1,2048,768]{2,1,0:T(8,128)(2,1)} %param.9) | copy-start | bytes 9437188
  57.3 1.7 copy-start.1
  74.1 4.6 %copy-start.2 = (f32[128,2]{0,1:T(2,128)S(1)}, f32[128,2]{0,1:T(2,128)}, u32[]{:S(2)}) copy-start(f32[128,2]{0,1:T(2,128)} %param.8) | copy-start | bytes 3076
  74.1 115.9 %all-to-all-start.1 = ((bf16[16,1,48,2048]{3,2,1,0:T(8,128)(2,1)}), bf16[16,1,48,2048]{3,2,1,0:T(8,128)(2,1)}, u32[]{:S(2)}, u32[]{:S(2)}) async-start(bf16[16,1,48,2048]{3,2,1,0:T(8,128)(2,1)} %fusion.7), calls=%async_computation.1 | async-start | bytes 6291456 | tf_op jit(solution)/shard_map/all_to_all | solution.py:37
where the time goes:
time: 206 us
  blocking collectives  155 us (75%)
  local copies, waits for them, and re-layouts  20.4 us (10%)
  matrix products  15 us (7%)
  other arithmetic  7.79 us (4%)
  starting transfers between devices  4.62 us (2%)
  between operations  2.5 us (1%)
    psum x1, blocking collectives, on_device(): load_all, mass_all = lax.psum((load_here, mass_here), ('dp', 'expert'))  110 us
    all_to_all x1, blocking collectives, on_device(): lax.all_to_all(outgoing, 'expert', split_axis=0, concat_axis=0, tiled=True)  45.8 us
    dot_general x1, matrix products, on_device(): jnp.einsum('genf,efd->gend', hidden, w_down, preferred_element_type=jnp.f...  11 us
    scatter x1, local copies, waits for them, and re-layouts, on_device(): outgoing = outgoing.at[send_index].set(tokens[row_token], mode='drop')  7.78 us
    gather x1, local copies, waits for them, and re-layouts, on_device(): slot_rows = returned_rows[jnp.minimum(destination, slot_total - 1)]  5.64 us
    reduce_sum x1, other arithmetic, on_device(): jnp.sum(weighted.reshape(tok_rows, pick_count, feature_width), 1)  5.59 us
    all_to_all x1, starting transfers between devices, on_device(): lax.all_to_all(result.astype(jnp.bfloat16), 'expert', split_axis=0, conca...  4.62 us
  transfers between devices with their start and end apart: 1, of which 0 were waited for; matrix products, arithmetic and copies ran while one was open for 0% of the time, Pallas kernels for 0%

commit v1 on v0

v1 whole, which is shorter than its diff:
```python
import functools

import jax
import jax.numpy as jnp
from jax import lax
from jax.experimental import pallas as pl
from jax.experimental.pallas import tpu as pltpu
from jax.sharding import PartitionSpec as P

F32 = jnp.float32
BF16 = jnp.bfloat16
PARTS = 4


def pack_kernel(cap, ids_ref, gates_ref, tok_ref, out_ref, meta_ref, stats_ref, dest_ref):
    experts = stats_ref.shape[0]
    rows, toks = out_ref.shape[0], tok_ref.shape[0]
    step = pl.program_id(0)

    @pl.when(step == 0)
    def _():
        ids = ids_ref[...]
        gates = gates_ref[...]
        labels = lax.broadcasted_iota(jnp.int32, (experts, toks), 0)
        first = (labels == ids[0:1, :]).astype(F32)
        second = (labels == ids[1:2, :]).astype(F32)
        before = lax.broadcasted_iota(jnp.int32, (toks, toks), 0)
        after = lax.broadcasted_iota(jnp.int32, (toks, toks), 1)
        earlier = (before < after).astype(F32).astype(BF16)
        first_rank = jnp.dot(first.astype(BF16), earlier, preferred_element_type=F32)
        second_rank = jnp.dot(second.astype(BF16), earlier, preferred_element_type=F32)
        first_count = jnp.sum(first, 1, keepdims=True)
        count = first_count + jnp.sum(second, 1, keepdims=True)
        mass = jnp.sum(first * gates[0:1, :] + second * gates[1:2, :], 1, keepdims=True)
        base = ids.astype(F32) * cap
        first_dest = base[0:1, :] + jnp.sum(first * first_rank, 0, keepdims=True)
        second_dest = base[1:2, :] + jnp.sum(second * (second_rank + first_count), 0, keepdims=True)
        lanes = lax.broadcasted_iota(jnp.int32, stats_ref.shape, 1)
        stats_ref[...] = jnp.where(lanes == 0, count, jnp.where(lanes == 1, mass, 0.0))
        sub = lax.broadcasted_iota(jnp.int32, (toks, toks), 0)
        rows_up = jnp.where(sub == 0, first_dest, jnp.where(sub == 1, second_dest, 0.0))
        rows_up = jnp.where(sub == 2, gates[0:1, :], jnp.where(sub == 3, gates[1:2, :], rows_up))
        meta_ref[...] = rows_up.T
        dest_ref[0:1, :] = first_dest.astype(jnp.int32)
        dest_ref[1:2, :] = second_dest.astype(jnp.int32)

    slots = lax.broadcasted_iota(jnp.int32, (rows, toks), 0) + step * rows
    dest = dest_ref[...]
    pick = (slots == dest[0:1, :]) | (slots == dest[1:2, :])
    pick = pick.astype(F32).astype(BF16)
    out_ref[...] = jnp.dot(pick, tok_ref[...], preferred_element_type=F32).astype(BF16)


def pack(ids, gates, tokens, experts, cap):
    toks, width = tokens.shape
    slots = experts * cap
    rows = slots // PARTS
    whole = lambda shape: pl.BlockSpec(shape, lambda i: (0, 0))
    return pl.pallas_call(
        functools.partial(pack_kernel, cap),
        grid=(PARTS,),
        in_specs=[whole(ids.shape), whole(gates.shape), whole(tokens.shape)],
        out_specs=[
            pl.BlockSpec((rows, width), lambda i: (i, 0)),
            whole((toks, toks)),
            whole((experts, 128)),
        ],
        out_shape=[
            jax.ShapeDtypeStruct((slots, width), BF16),
            jax.ShapeDtypeStruct((toks, toks), F32),
            jax.ShapeDtypeStruct((experts, 128), F32),
        ],
        scratch_shapes=[pltpu.VMEM((8, toks), jnp.int32)],
        compiler_params=pltpu.CompilerParams(vmem_limit_bytes=16 * 2**20),
        cost_estimate=pl.CostEstimate(
            flops=2 * slots * toks * width, bytes_accessed=4 * slots * width, transcendentals=0
        ),
        name="pack",
    )(ids, gates, tokens)


def hidden_kernel(x_ref, gate_ref, up_ref, out_ref):
    x = x_ref[...]
    gate = jnp.dot(x, gate_ref[0], preferred_element_type=F32)
    up = jnp.dot(x, up_ref[0], preferred_element_type=F32)
    out_ref[...] = (gate / (1.0 + jnp.exp(-gate)) * up).astype(BF16)


def down_kernel(x_ref, down_ref, out_ref):
    out_ref[...] = jnp.dot(x_ref[...], down_ref[0], preferred_element_type=F32).astype(BF16)


def rows_kernel(body, x, weights, out_width, block, name):
    rows, width = x.shape
    once = pl.Buffered(1)
    return pl.pallas_call(
        body,
        grid=(rows // block,),
        in_specs=[pl.BlockSpec((block, width), lambda i: (i, 0))]
        + [pl.BlockSpec(w.shape, lambda i: (0, 0, 0), pipeline_mode=once) for w in weights],
        out_specs=pl.BlockSpec((block, out_width), lambda i: (i, 0)),
        out_shape=jax.ShapeDtypeStruct((rows, out_width), BF16),
        compiler_params=pltpu.CompilerParams(vmem_limit_bytes=24 * 2**20),
        cost_estimate=pl.CostEstimate(
            flops=2 * rows * width * out_width * len(weights),
            bytes_accessed=2 * (rows * (width + out_width) + len(weights) * width * out_width),
            transcendentals=0,
        ),
        name=name,
    )(x, *weights)


def combine_kernel(meta_ref, rows_ref, out_ref, pick_ref):
    toks = out_ref.shape[0]
    slots = rows_ref.shape[0]

    @pl.when(pl.program_id(0) == 0)
    def _():
        dest = meta_ref[:, 0:2].astype(jnp.int32)
        lane = lax.broadcasted_iota(jnp.int32, (toks, slots), 1)
        pick_ref[:toks, :] = (lane == dest[:, 0:1]).astype(F32).astype(BF16)
        pick_ref[toks:, :] = (lane == dest[:, 1:2]).astype(F32).astype(BF16)

    both = jnp.dot(pick_ref[...], rows_ref[...], preferred_element_type=F32)
    weights = meta_ref[:, 2:4]
    out_ref[...] = (weights[:, 0:1] * both[:toks] + weights[:, 1:2] * both[toks:]).astype(BF16)


def combine(meta, rows):
    toks = meta.shape[0]
    slots, width = rows.shape
    block = width // PARTS
    return pl.pallas_call(
        combine_kernel,
        grid=(PARTS,),
        in_specs=[
            pl.BlockSpec(meta.shape, lambda i: (0, 0)),
            pl.BlockSpec((slots, block), lambda i: (0, i)),
        ],
        out_specs=pl.BlockSpec((toks, block), lambda i: (0, i)),
        out_shape=jax.ShapeDtypeStruct((toks, width), BF16),
        scratch_shapes=[pltpu.VMEM((2 * toks, slots), BF16)],
        compiler_params=pltpu.CompilerParams(vmem_limit_bytes=16 * 2**20),
        cost_estimate=pl.CostEstimate(
            flops=4 * toks * slots * width, bytes_accessed=2 * slots * width, transcendentals=0
        ),
        name="combine",
    )(meta, rows)


def radix_sum(value, axis, size, stride):
    total = value
    for turn in range(1, 4):
        pairs = []
        for i in range(size):
            digit = (i // stride) % 4
            pairs.append((i, i + ((digit + turn) % 4 - digit) * stride))
        total = total + lax.ppermute(value, axis, pairs)
    return total


def on_device(tokens, expert_ids, gate_weights, w_gate, w_up, w_down):
    toks, width = tokens.shape
    picks = expert_ids.shape[1]
    group = lax.axis_size("expert")
    copies = lax.axis_size("dp")
    experts = w_gate.shape[0] * group
    cap = min(toks * picks // 4, 3 * toks * picks // experts)
    all_tokens = toks * group * copies

    outgoing, meta, stats = pack(expert_ids.T, gate_weights.T, tokens, experts, cap)
    stats = radix_sum(stats, "expert", group, 1)
    received = lax.all_to_all(outgoing, "expert", split_axis=0, concat_axis=0, tiled=True)
    stats, received = lax.optimization_barrier((stats, received))
    stats = radix_sum(stats, "expert", group, 4)
    hidden = rows_kernel(hidden_kernel, received, (w_gate, w_up), w_gate.shape[2], 256, "hidden")
    stats, hidden = lax.optimization_barrier((stats, hidden))
    stats = radix_sum(stats, "dp", copies, 1)
    result = rows_kernel(down_kernel, hidden, (w_down,), width, 256, "down")
    stats, result = lax.optimization_barrier((stats, result))
    stats = radix_sum(stats, "dp", copies, 4)
    returned = lax.all_to_all(result, "expert", split_axis=0, concat_axis=0, tiled=True)
    stats, returned = lax.optimization_barrier((stats, returned))
    mixed = combine(meta, returned)
    load, mass = stats[:, 0], stats[:, 1]
    aux_loss = experts * jnp.sum(load / (all_tokens * picks) * (mass / all_tokens))
    return mixed, aux_loss


def solution(mesh):
    rows = P(("dp", "expert"), None)
    held = P("expert", None, None)
    return jax.shard_map(
        on_device,
        mesh=mesh,
        in_specs=(rows, rows, rows, held, held, held),
        out_specs=(rows, P()),
        check_vma=False,
    )
```

time: 206 us -> 135 us (0.66)
  the two profiles are of different devices: /device:TPU:1 before, /device:TPU:189 now
where the time goes in v1:
time: 135 us
  waiting for transfers between devices  81.5 us (60%)
  starting transfers between devices  27.8 us (21%)
  Pallas kernels  12.8 us (9%)
  local copies, waits for them, and re-layouts  9.45 us (7%)
  between operations  2.52 us (2%)
    all_to_all x1, waiting for transfers between devices, on_device(): lax.all_to_all(result, 'expert', split_axis=0, concat_axis=0, tiled=True)  37.2 us
    ppermute x12, waiting for transfers between devices, radix_sum(): total = total + lax.ppermute(value, axis, pairs)  27.6 us
    all_to_all x1, waiting for transfers between devices, on_device(): lax.all_to_all(outgoing, 'expert', split_axis=0, concat_axis=0, tiled=True)  16.6 us
    ppermute x12, starting transfers between devices, radix_sum(): total = total + lax.ppermute(value, axis, pairs)  13.7 us
    unnamed x16, local copies, waits for them, and re-layouts  9.45 us
    pallas_call x2, Pallas kernels, rows_kernel(): pl.pallas_call(body, grid=(rows // block,), in_specs=[pl.BlockSpec((block...  8.35 us
    all_to_all x1, starting transfers between devices, on_device(): lax.all_to_all(result, 'expert', split_axis=0, concat_axis=0, tiled=True)  7.6 us
    all_to_all x1, starting transfers between devices, on_device(): lax.all_to_all(outgoing, 'expert', split_axis=0, concat_axis=0, tiled=True)  6.55 us
  transfers between devices with their start and end apart: 14, of which 6 were waited for; matrix products, arithmetic and copies ran while one was open for 0% of the time, Pallas kernels for 6%

profile of v1, /device:TPU:189, one launch (start us, length us, event | category | flops | bytes accessed | tf_op | source)
XLA Modules:
  0.0 134.8 jit_solution(4831597856254819520)
XLA Ops:
  0.6 0.0 copy-start.5
  0.6 1.0 copy-done.5
  1.7 0.0 copy-start.6
  1.7 0.7 copy-done.6
  2.4 0.0 copy-start.7
  2.4 0.7 copy-done.7
  3.0 1.7 %pack.1 = (bf16[768,2048]{1,0:T(8,128)(2,1)S(1)}, f32[128,128]{1,0:T(8,128)S(1)}, f32[16,128]{1,0:T(8,128)S(1)}) custom-call(s32[2,128]{1,0:T(2,128)S(1)} %bitcast.10, f32[2,128]{1,0:T(2,128)S(1)} %bitcast.11, bf16[128,2048]{1,0:T(8,128)(2,1)S(1)} %copy-done.5), custom_call_target="tpu_custom_call" | custom-call | flops 402653184 | bytes 6291456 | tf_op jit(solution)/shard_map/pack/pallas_call | solution.py:59
  4.7 0.0 copy-start.1
  4.7 1.6 %copy-done.1 = bf16[768,2048]{1,0:T(8,128)(2,1)} copy-done((bf16[768,2048]{1,0:T(8,128)(2,1)}, bf16[768,2048]{1,0:T(8,128)(2,1)S(1)}, u32[]{:S(2)}) %copy-start.1) | copy-done | bytes 3145752
  6.4 6.6 %all-to-all-start = ((bf16[16,48,2048]{2,1,0:T(8,128)(2,1)}), bf16[16,48,2048]{2,1,0:T(8,128)(2,1)S(1)}, u32[]{:S(2)}, u32[]{:S(2)}) async-start(bf16[16,48,2048]{2,1,0:T(8,128)(2,1)} %bitcast.9), calls=%async_computation | async-start | bytes 6291456 | tf_op jit(solution)/shard_map/all_to_all | solution.py:173
  12.9 0.6 collective-permute-start.2
  13.5 0.9 collective-permute-start.1
  14.4 1.8 %collective-permute-start = (f32[16,128]{1,0:T(8,128)S(1)}, f32[16,128]{1,0:T(8,128)S(1)}, u32[]{:S(2)}, u32[]{:S(2)}) collective-permute-start(f32[16,128]{1,0:T(8,128)S(1)} %get-tuple-element.14), channel_id=1, source_target_pairs={{0,1},{1,2},{2,3},{3,0},{4,5},{5,6},{6,7},{7,4},{8,9},{9,10},{10,1... | collective-permute-start | bytes 24584 | tf_op jit(solution)/shard_map/ppermute | solution.py:158
  16.2 13.2 %collective-permute-done.2 = f32[16,128]{1,0:T(8,128)S(1)} collective-permute-done((f32[16,128]{1,0:T(8,128)S(1)}, f32[16,128]{1,0:T(8,128)S(1)}, u32[]{:S(2)}, u32[]{:S(2)}) %collective-permute-start.2) | collective-permute-done | bytes 8224 | tf_op jit(solution)/shard_map/ppermute | solution.py:158
  29.4 9.5 %collective-permute-done.1 = f32[16,128]{1,0:T(8,128)S(1)} collective-permute-done((f32[16,128]{1,0:T(8,128)S(1)}, f32[16,128]{1,0:T(8,128)S(1)}, u32[]{:S(2)}, u32[]{:S(2)}) %collective-permute-start.1) | collective-permute-done | bytes 8224 | tf_op jit(solution)/shard_map/ppermute | solution.py:158
  38.9 0.0 collective-permute-done
  38.9 16.6 %all-to-all-done = bf16[16,48,2048]{2,1,0:T(8,128)(2,1)S(1)} async-done(((bf16[16,48,2048]{2,1,0:T(8,128)(2,1)}), bf16[16,48,2048]{2,1,0:T(8,128)(2,1)S(1)}, u32[]{:S(2)}, u32[]{:S(2)}) %all-to-all-start) | async-done | bytes 3145760 | tf_op jit(solution)/shard_map/all_to_all | solution.py:173
  55.5 0.0 collective-permute-start.5
  55.5 0.0 collective-permute-start.4
  55.5 1.5 %collective-permute-start.3 = (f32[16,128]{1,0:T(8,128)S(1)}, f32[16,128]{1,0:T(8,128)S(1)}, u32[]{:S(2)}, u32[]{:S(2)}) collective-permute-start(f32[16,128]{1,0:T(8,128)S(1)} %add_add_fusion.3), channel_id=1, source_target_pairs={{0,4},{1,5},{2,6},{3,7},{4,8},{5,9},{6,10},{7,11},{8,12},{9,13},{1... | collective-permute-start | bytes 24584 | tf_op jit(solution)/shard_map/ppermute | solution.py:158
  57.0 0.0 copy-start.2
  57.0 1.9 %copy-done.2 = bf16[1,2048,768]{2,1,0:T(8,128)(2,1)S(1)} copy-done((bf16[1,2048,768]{2,1,0:T(8,128)(2,1)S(1)}, bf16[1,2048,768]{2,1,0:T(8,128)(2,1)}, u32[]{:S(2)}) %copy-start.2) | copy-done | bytes 3145752
  58.9 0.0 copy-start.3
  58.9 1.9 %copy-done.3 = bf16[1,2048,768]{2,1,0:T(8,128)(2,1)S(1)} copy-done((bf16[1,2048,768]{2,1,0:T(8,128)(2,1)S(1)}, bf16[1,2048,768]{2,1,0:T(8,128)(2,1)}, u32[]{:S(2)}) %copy-start.3) | copy-done | bytes 3145752
  60.8 0.0 copy-start.4
  60.8 5.4 %hidden.1.x_ref = bf16[768,768]{1,0:T(8,128)(2,1)S(1)} custom-call(bf16[768,2048]{1,0:T(8,128)(2,1)S(1)} %bitcast.7, bf16[1,2048,768]{2,1,0:T(8,128)(2,1)S(1)} %copy-done.2, bf16[1,2048,768]{2,1,0:T(8,128)(2,1)S(1)} %copy-done.3), custom_call_target="tpu_custom_call" | custom-call | flops 4831838208 | bytes 10616832 | tf_op jit(solution)/shard_map/hidden/pallas_call | solution.py:96
  66.2 0.0 collective-permute-done.5
  66.2 0.0 collective-permute-done.4
  66.2 0.0 collective-permute-done.3
  66.2 2.9 %collective-permute-start.8 = (f32[16,128]{1,0:T(8,128)S(1)}, f32[16,128]{1,0:T(8,128)S(1)}, u32[]{:S(2)}, u32[]{:S(2)}) collective-permute-start(f32[16,128]{1,0:T(8,128)S(1)} %add_add_fusion.2), channel_id=1, source_target_pairs={{0,48},{16,0},{32,16},{48,32},{64,112},{80,64},{96,80},{112,96},{1... | collective-permute-start | bytes 24584 | tf_op jit(solution)/shard_map/ppermute | solution.py:158
  69.1 0.7 collective-permute-start.7
  69.8 1.0 collective-permute-start.6
  70.8 0.0 copy-done.4
  70.8 3.0 %down.1 = bf16[768,2048]{1,0:T(8,128)(2,1)S(1)} custom-call(bf16[768,768]{1,0:T(8,128)(2,1)S(1)} %hidden.1.x_ref, bf16[1,768,2048]{2,1,0:T(8,128)(2,1)S(1)} %copy-done.4), custom_call_target="tpu_custom_call" | custom-call | flops 2415919104 | bytes 7471104 | tf_op jit(solution)/shard_map/down/pallas_call | solution.py:96
  73.8 0.0 copy-start
  73.8 1.6 %copy-done = bf16[768,2048]{1,0:T(8,128)(2,1)} copy-done((bf16[768,2048]{1,0:T(8,128)(2,1)}, bf16[768,2048]{1,0:T(8,128)(2,1)S(1)}, u32[]{:S(2)}) %copy-start) | copy-done | bytes 3145752
  75.4 0.0 collective-permute-done.8
  75.4 0.0 collective-permute-done.7
  75.4 0.0 collective-permute-done.6
  75.5 7.6 %all-to-all-start.1 = ((bf16[16,48,2048]{2,1,0:T(8,128)(2,1)}), bf16[16,48,2048]{2,1,0:T(8,128)(2,1)S(1)}, u32[]{:S(2)}, u32[]{:S(2)}) async-start(bf16[16,48,2048]{2,1,0:T(8,128)(2,1)} %bitcast.8), calls=%async_computation.1 | async-start | bytes 6291456 | tf_op jit(solution)/shard_map/all_to_all | solution.py:182
  83.1 0.3 collective-permute-start.11
  83.4 4.1 %collective-permute-start.10 = (f32[16,128]{1,0:T(8,128)S(1)}, f32[16,128]{1,0:T(8,128)S(1)}, u32[]{:S(2)}, u32[]{:S(2)}) collective-permute-start(f32[16,128]{1,0:T(8,128)S(1)} %add_add_fusion.1), channel_id=1, source_target_pairs={{0,128},{16,144},{32,160},{48,176},{64,192},{80,208},{96,224},{112... | collective-permute-start | bytes 24584 | tf_op jit(solution)/shard_map/ppermute | solution.py:158
  87.4 0.0 collective-permute-start.9
  87.4 0.0 collective-permute-done.11
  87.4 2.3 %collective-permute-done.10 = f32[16,128]{1,0:T(8,128)S(1)} collective-permute-done((f32[16,128]{1,0:T(8,128)S(1)}, f32[16,128]{1,0:T(8,128)S(1)}, u32[]{:S(2)}, u32[]{:S(2)}) %collective-permute-start.10) | collective-permute-done | bytes 8224 | tf_op jit(solution)/shard_map/ppermute | solution.py:158
  89.8 2.6 %collective-permute-done.9 = f32[16,128]{1,0:T(8,128)S(1)} collective-permute-done((f32[16,128]{1,0:T(8,128)S(1)}, f32[16,128]{1,0:T(8,128)S(1)}, u32[]{:S(2)}, u32[]{:S(2)}) %collective-permute-start.9) | collective-permute-done | bytes 8224 | tf_op jit(solution)/shard_map/ppermute | solution.py:158
  92.3 37.2 %all-to-all-done.1 = bf16[16,48,2048]{2,1,0:T(8,128)(2,1)S(1)} async-done(((bf16[16,48,2048]{2,1,0:T(8,128)(2,1)}), bf16[16,48,2048]{2,1,0:T(8,128)(2,1)S(1)}, u32[]{:S(2)}, u32[]{:S(2)}) %all-to-all-start.1) | async-done | bytes 3145760 | tf_op jit(solution)/shard_map/all_to_all | solution.py:182
  129.6 0.7 multiply_reduce_fusion
  130.9 2.8 %combine.1 = bf16[128,2048]{1,0:T(8,128)(2,1)} custom-call(f32[128,128]{1,0:T(8,128)S(1)} %get-tuple-element.13.meta_ref, bf16[768,2048]{1,0:T(8,128)(2,1)S(1)} %bitcast.6), custom_call_target="tpu_custom_call" | custom-call | flops 805306368 | bytes 3145728 | tf_op jit(solution)/shard_map/combine/pallas_call | solution.py:133
  (4 shorter events, 0.0 us)
Async XLA Ops:
  0.6 1.0 copy-start.5
  1.7 0.7 copy-start.6
  2.4 0.7 copy-start.7
  4.7 1.6 %copy-start.1 = (bf16[768,2048]{1,0:T(8,128)(2,1)}, bf16[768,2048]{1,0:T(8,128)(2,1)S(1)}, u32[]{:S(2)}) copy-start(bf16[768,2048]{1,0:T(8,128)(2,1)S(1)} %get-tuple-element.15) | copy-start | bytes 9437188
  6.4 49.1 %all-to-all-start = ((bf16[16,48,2048]{2,1,0:T(8,128)(2,1)}), bf16[16,48,2048]{2,1,0:T(8,128)(2,1)S(1)}, u32[]{:S(2)}, u32[]{:S(2)}) async-start(bf16[16,48,2048]{2,1,0:T(8,128)(2,1)} %bitcast.9), calls=%async_computation | async-start | bytes 6291456 | tf_op jit(solution)/shard_map/all_to_all | solution.py:173
  12.9 16.5 %collective-permute-start.2 = (f32[16,128]{1,0:T(8,128)S(1)}, f32[16,128]{1,0:T(8,128)S(1)}, u32[]{:S(2)}, u32[]{:S(2)}) collective-permute-start(f32[16,128]{1,0:T(8,128)S(1)} %get-tuple-element.14), channel_id=1, source_target_pairs={{0,3},{1,0},{2,1},{3,2},{4,7},{5,4},{6,5},{7,6},{8,11},{9,8},{10,9... | collective-permute-start | bytes 24584 | tf_op jit(solution)/shard_map/ppermute | solution.py:158
  13.5 25.4 %collective-permute-start.1 = (f32[16,128]{1,0:T(8,128)S(1)}, f32[16,128]{1,0:T(8,128)S(1)}, u32[]{:S(2)}, u32[]{:S(2)}) collective-permute-start(f32[16,128]{1,0:T(8,128)S(1)} %get-tuple-element.14), channel_id=1, source_target_pairs={{0,2},{1,3},{2,0},{3,1},{4,6},{5,7},{6,4},{7,5},{8,10},{9,11},{10,... | collective-permute-start | bytes 24584 | tf_op jit(solution)/shard_map/ppermute | solution.py:158
  14.4 24.5 %collective-permute-start = (f32[16,128]{1,0:T(8,128)S(1)}, f32[16,128]{1,0:T(8,128)S(1)}, u32[]{:S(2)}, u32[]{:S(2)}) collective-permute-start(f32[16,128]{1,0:T(8,128)S(1)} %get-tuple-element.14), channel_id=1, source_target_pairs={{0,1},{1,2},{2,3},{3,0},{4,5},{5,6},{6,7},{7,4},{8,9},{9,10},{10,1... | collective-permute-start | bytes 24584 | tf_op jit(solution)/shard_map/ppermute | solution.py:158
  55.5 10.7 %collective-permute-start.5 = (f32[16,128]{1,0:T(8,128)S(1)}, f32[16,128]{1,0:T(8,128)S(1)}, u32[]{:S(2)}, u32[]{:S(2)}) collective-permute-start(f32[16,128]{1,0:T(8,128)S(1)} %add_add_fusion.3), channel_id=1, source_target_pairs={{0,12},{1,13},{2,14},{3,15},{4,0},{5,1},{6,2},{7,3},{8,4},{9,5},{1... | collective-permute-start | bytes 24584 | tf_op jit(solution)/shard_map/ppermute | solution.py:158
  55.5 10.7 %collective-permute-start.4 = (f32[16,128]{1,0:T(8,128)S(1)}, f32[16,128]{1,0:T(8,128)S(1)}, u32[]{:S(2)}, u32[]{:S(2)}) collective-permute-start(f32[16,128]{1,0:T(8,128)S(1)} %add_add_fusion.3), channel_id=1, source_target_pairs={{0,8},{1,9},{2,10},{3,11},{4,12},{5,13},{6,14},{7,15},{8,0},{9,1},... | collective-permute-start | bytes 24584 | tf_op jit(solution)/shard_map/ppermute | solution.py:158
  55.5 10.7 %collective-permute-start.3 = (f32[16,128]{1,0:T(8,128)S(1)}, f32[16,128]{1,0:T(8,128)S(1)}, u32[]{:S(2)}, u32[]{:S(2)}) collective-permute-start(f32[16,128]{1,0:T(8,128)S(1)} %add_add_fusion.3), channel_id=1, source_target_pairs={{0,4},{1,5},{2,6},{3,7},{4,8},{5,9},{6,10},{7,11},{8,12},{9,13},{1... | collective-permute-start | bytes 24584 | tf_op jit(solution)/shard_map/ppermute | solution.py:158
  57.0 1.9 %copy-start.2 = (bf16[1,2048,768]{2,1,0:T(8,128)(2,1)S(1)}, bf16[1,2048,768]{2,1,0:T(8,128)(2,1)}, u32[]{:S(2)}) copy-start(bf16[1,2048,768]{2,1,0:T(8,128)(2,1)} %gate_ref.1) | copy-start | bytes 9437188
  58.9 1.9 %copy-start.3 = (bf16[1,2048,768]{2,1,0:T(8,128)(2,1)S(1)}, bf16[1,2048,768]{2,1,0:T(8,128)(2,1)}, u32[]{:S(2)}) copy-start(bf16[1,2048,768]{2,1,0:T(8,128)(2,1)} %up_ref.1) | copy-start | bytes 9437188
  60.8 10.0 %copy-start.4 = (bf16[1,768,2048]{2,1,0:T(8,128)(2,1)S(1)}, bf16[1,768,2048]{2,1,0:T(8,128)(2,1)}, u32[]{:S(2)}) copy-start(bf16[1,768,2048]{2,1,0:T(8,128)(2,1)} %down_ref.1) | copy-start | bytes 9437188
  66.2 9.2 %collective-permute-start.8 = (f32[16,128]{1,0:T(8,128)S(1)}, f32[16,128]{1,0:T(8,128)S(1)}, u32[]{:S(2)}, u32[]{:S(2)}) collective-permute-start(f32[16,128]{1,0:T(8,128)S(1)} %add_add_fusion.2), channel_id=1, source_target_pairs={{0,48},{16,0},{32,16},{48,32},{64,112},{80,64},{96,80},{112,96},{1... | collective-permute-start | bytes 24584 | tf_op jit(solution)/shard_map/ppermute | solution.py:158
  69.1 6.4 %collective-permute-start.7 = (f32[16,128]{1,0:T(8,128)S(1)}, f32[16,128]{1,0:T(8,128)S(1)}, u32[]{:S(2)}, u32[]{:S(2)}) collective-permute-start(f32[16,128]{1,0:T(8,128)S(1)} %add_add_fusion.2), channel_id=1, source_target_pairs={{0,32},{16,48},{32,0},{48,16},{64,96},{80,112},{96,64},{112,80},{1... | collective-permute-start | bytes 24584 | tf_op jit(solution)/shard_map/ppermute | solution.py:158
  69.8 5.7 %collective-permute-start.6 = (f32[16,128]{1,0:T(8,128)S(1)}, f32[16,128]{1,0:T(8,128)S(1)}, u32[]{:S(2)}, u32[]{:S(2)}) collective-permute-start(f32[16,128]{1,0:T(8,128)S(1)} %add_add_fusion.2), channel_id=1, source_target_pairs={{0,16},{16,32},{32,48},{48,0},{64,80},{80,96},{96,112},{112,64},{1... | collective-permute-start | bytes 24584 | tf_op jit(solution)/shard_map/ppermute | solution.py:158
  73.8 1.6 %copy-start = (bf16[768,2048]{1,0:T(8,128)(2,1)}, bf16[768,2048]{1,0:T(8,128)(2,1)S(1)}, u32[]{:S(2)}) copy-start(bf16[768,2048]{1,0:T(8,128)(2,1)S(1)} %down.1) | copy-start | bytes 9437188
  75.5 54.1 %all-to-all-start.1 = ((bf16[16,48,2048]{2,1,0:T(8,128)(2,1)}), bf16[16,48,2048]{2,1,0:T(8,128)(2,1)S(1)}, u32[]{:S(2)}, u32[]{:S(2)}) async-start(bf16[16,48,2048]{2,1,0:T(8,128)(2,1)} %bitcast.8), calls=%async_computation.1 | async-start | bytes 6291456 | tf_op jit(solution)/shard_map/all_to_all | solution.py:182
  83.1 4.4 %collective-permute-start.11 = (f32[16,128]{1,0:T(8,128)S(1)}, f32[16,128]{1,0:T(8,128)S(1)}, u32[]{:S(2)}, u32[]{:S(2)}) collective-permute-start(f32[16,128]{1,0:T(8,128)S(1)} %add_add_fusion.1), channel_id=1, source_target_pairs={{0,192},{16,208},{32,224},{48,240},{64,0},{80,16},{96,32},{112,48}... | collective-permute-start | bytes 24584 | tf_op jit(solution)/shard_map/ppermute | solution.py:158
  83.4 6.4 %collective-permute-start.10 = (f32[16,128]{1,0:T(8,128)S(1)}, f32[16,128]{1,0:T(8,128)S(1)}, u32[]{:S(2)}, u32[]{:S(2)}) collective-permute-start(f32[16,128]{1,0:T(8,128)S(1)} %add_add_fusion.1), channel_id=1, source_target_pairs={{0,128},{16,144},{32,160},{48,176},{64,192},{80,208},{96,224},{112... | collective-permute-start | bytes 24584 | tf_op jit(solution)/shard_map/ppermute | solution.py:158
  87.4 4.9 %collective-permute-start.9 = (f32[16,128]{1,0:T(8,128)S(1)}, f32[16,128]{1,0:T(8,128)S(1)}, u32[]{:S(2)}, u32[]{:S(2)}) collective-permute-start(f32[16,128]{1,0:T(8,128)S(1)} %add_add_fusion.1), channel_id=1, source_target_pairs={{0,64},{16,80},{32,96},{48,112},{64,128},{80,144},{96,160},{112,17... | collective-permute-start | bytes 24584 | tf_op jit(solution)/shard_map/ppermute | solution.py:158

commit v2 on v1

--- a/solution.py
+++ b/solution.py
@@ -10,23 +10,23 @@
 F32 = jnp.float32
 BF16 = jnp.bfloat16
 PARTS = 4
-
-
-def pack_kernel(cap, ids_ref, gates_ref, tok_ref, out_ref, meta_ref, stats_ref, dest_ref):
-    experts = stats_ref.shape[0]
+PACK_VMEM = 60 * 2**20
+
+
+def pack_kernel(cap, ids_ref, gates_ref, tok_ref, out_ref, meta_ref, dest_ref, note_ref):
     rows, toks = out_ref.shape[0], tok_ref.shape[0]
+    experts = rows * PARTS // cap
     step = pl.program_id(0)
 
     @pl.when(step == 0)
     def _():
         ids = ids_ref[...]
         gates = gates_ref[...]
-        labels = lax.broadcasted_iota(jnp.int32, (experts, toks), 0)
+        labels = lax.broadcasted_iota(jnp.int32, (toks, toks), 0)
         first = (labels == ids[0:1, :]).astype(F32)
         second = (labels == ids[1:2, :]).astype(F32)
-        before = lax.broadcasted_iota(jnp.int32, (toks, toks), 0)
-        after = lax.broadcasted_iota(jnp.int32, (toks, toks), 1)
-        earlier = (before < after).astype(F32).astype(BF16)
+        lanes = lax.broadcasted_iota(jnp.int32, (toks, toks), 1)
+        earlier = (labels < lanes).astype(F32).astype(BF16)
         first_rank = jnp.dot(first.astype(BF16), earlier, preferred_element_type=F32)
         second_rank = jnp.dot(second.astype(BF16), earlier, preferred_element_type=F32)
         first_count = jnp.sum(first, 1, keepdims=True)
@@ -35,20 +35,37 @@
         base = ids.astype(F32) * cap
         first_dest = base[0:1, :] + jnp.sum(first * first_rank, 0, keepdims=True)
         second_dest = base[1:2, :] + jnp.sum(second * (second_rank + first_count), 0, keepdims=True)
-        lanes = lax.broadcasted_iota(jnp.int32, stats_ref.shape, 1)
-        stats_ref[...] = jnp.where(lanes == 0, count, jnp.where(lanes == 1, mass, 0.0))
-        sub = lax.broadcasted_iota(jnp.int32, (toks, toks), 0)
-        rows_up = jnp.where(sub == 0, first_dest, jnp.where(sub == 1, second_dest, 0.0))
-        rows_up = jnp.where(sub == 2, gates[0:1, :], jnp.where(sub == 3, gates[1:2, :], rows_up))
-        meta_ref[...] = rows_up.T
         dest_ref[0:1, :] = first_dest.astype(jnp.int32)
         dest_ref[1:2, :] = second_dest.astype(jnp.int32)
+        high = mass.astype(BF16).astype(F32)
+        middle = (mass - high).astype(BF16).astype(F32)
+        low = mass - high - middle
+        columns = jnp.where(lanes == 0, count, jnp.where(lanes == 1, high, 0.0))
+        columns = jnp.where(lanes == 2, middle, jnp.where(lanes == 3, low, columns))
+        lines = columns.T
+        free = (count < cap) & (labels < experts)
+        for i in range(4):
+            line = jnp.where(free, lines[i : i + 1, :], 0.0)
+            note_ref[:, i * toks : (i + 1) * toks] = line.astype(BF16)
+        expert = lax.broadcasted_iota(jnp.int32, (toks, 1), 0).astype(F32)
+        slot = jnp.where((count < cap) & (expert < experts), expert * cap + (cap - 1), 1e6)
+        slot = jnp.min(slot, 0, keepdims=True)
+        lines = jnp.where(labels == 0, first_dest, jnp.where(labels == 1, second_dest, 0.0))
+        lines = jnp.where(labels == 2, gates[0:1, :], jnp.where(labels == 3, gates[1:2, :], lines))
+        lines = jnp.where(labels == 4, slot, lines)
+        meta_ref[...] = jnp.where(lanes == 5, free.astype(F32), lines.T)
 
     slots = lax.broadcasted_iota(jnp.int32, (rows, toks), 0) + step * rows
+    lanes = lax.broadcasted_iota(jnp.int32, (rows, toks), 1)
     dest = dest_ref[...]
     pick = (slots == dest[0:1, :]) | (slots == dest[1:2, :])
     pick = pick.astype(F32).astype(BF16)
-    out_ref[...] = jnp.dot(pick, tok_ref[...], preferred_element_type=F32).astype(BF16)
+    last = (slots == lanes * cap + (cap - 1)).astype(F32).astype(BF16)
+    edge = note_ref.shape[1]
+    head = jnp.dot(pick, tok_ref[:, :edge], preferred_element_type=F32)
+    head = head + jnp.dot(last, note_ref[...], preferred_element_type=F32)
+    out_ref[:, :edge] = head.astype(BF16)
+    out_ref[:, edge:] = jnp.dot(pick, tok_ref[:, edge:], preferred_element_type=F32).astype(BF16)
 
 
 def pack(ids, gates, tokens, experts, cap):
@@ -63,15 +80,13 @@
         out_specs=[
             pl.BlockSpec((rows, width), lambda i: (i, 0)),
             whole((toks, toks)),
-            whole((experts, 128)),
         ],
         out_shape=[
             jax.ShapeDtypeStruct((slots, width), BF16),
             jax.ShapeDtypeStruct((toks, toks), F32),
-            jax.ShapeDtypeStruct((experts, 128), F32),
-        ],
-        scratch_shapes=[pltpu.VMEM((8, toks), jnp.int32)],
-        compiler_params=pltpu.CompilerParams(vmem_limit_bytes=16 * 2**20),
+        ],
+        scratch_shapes=[pltpu.VMEM((8, toks), jnp.int32), pltpu.VMEM((toks, 4 * toks), BF16)],
+        compiler_params=pltpu.CompilerParams(vmem_limit_bytes=PACK_VMEM),
         cost_estimate=pl.CostEstimate(
             flops=2 * slots * toks * width, bytes_accessed=4 * slots * width, transcendentals=0
         ),
@@ -110,16 +125,19 @@
     )(x, *weights)
 
 
-def combine_kernel(meta_ref, rows_ref, out_ref, pick_ref):
+def combine_kernel(meta_ref, rows_ref, out_ref, note_ref, pick_ref):
     toks = out_ref.shape[0]
     slots = rows_ref.shape[0]
 
     @pl.when(pl.program_id(0) == 0)
     def _():
-        dest = meta_ref[:, 0:2].astype(jnp.int32)
+        dest = meta_ref[:, 0:5].astype(jnp.int32)
         lane = lax.broadcasted_iota(jnp.int32, (toks, slots), 1)
         pick_ref[:toks, :] = (lane == dest[:, 0:1]).astype(F32).astype(BF16)
         pick_ref[toks:, :] = (lane == dest[:, 1:2]).astype(F32).astype(BF16)
+        slot = (lane[:16, :] == dest[:16, 4:5]).astype(F32).astype(BF16)
+        note = jnp.dot(slot, rows_ref[:, :128], preferred_element_type=F32)
+        note_ref[...] = note[:8, :]
 
     both = jnp.dot(pick_ref[...], rows_ref[...], preferred_element_type=F32)
     weights = meta_ref[:, 2:4]
@@ -137,8 +155,14 @@
             pl.BlockSpec(meta.shape, lambda i: (0, 0)),
             pl.BlockSpec((slots, block), lambda i: (0, i)),
         ],
-        out_specs=pl.BlockSpec((toks, block), lambda i: (0, i)),
-        out_shape=jax.ShapeDtypeStruct((toks, width), BF16),
+        out_specs=[
+            pl.BlockSpec((toks, block), lambda i: (0, i)),
+            pl.BlockSpec((8, 128), lambda i: (0, 0)),
+        ],
+        out_shape=[
+            jax.ShapeDtypeStruct((toks, width), BF16),
+            jax.ShapeDtypeStruct((8, 128), F32),
+        ],
         scratch_shapes=[pltpu.VMEM((2 * toks, slots), BF16)],
         compiler_params=pltpu.CompilerParams(vmem_limit_bytes=16 * 2**20),
         cost_estimate=pl.CostEstimate(
@@ -168,23 +192,37 @@
     cap = min(toks * picks // 4, 3 * toks * picks // experts)
     all_tokens = toks * group * copies
 
-    outgoing, meta, stats = pack(expert_ids.T, gate_weights.T, tokens, experts, cap)
-    stats = radix_sum(stats, "expert", group, 1)
+    outgoing, meta = pack(expert_ids.T, gate_weights.T, tokens, experts, cap)
     received = lax.all_to_all(outgoing, "expert", split_axis=0, concat_axis=0, tiled=True)
+
+    notes = received.reshape(group, cap, width)[:, cap - 1, : 4 * toks].astype(F32)
+    notes = jnp.sum(notes, 0).reshape(4, toks)
+    stats = jnp.concatenate([notes[0:1], notes[1:2] + notes[2:3] + notes[3:4]])
     stats, received = lax.optimization_barrier((stats, received))
-    stats = radix_sum(stats, "expert", group, 4)
+    stats = radix_sum(stats, "dp", copies, 1)
     hidden = rows_kernel(hidden_kernel, received, (w_gate, w_up), w_gate.shape[2], 256, "hidden")
     stats, hidden = lax.optimization_barrier((stats, hidden))
-    stats = radix_sum(stats, "dp", copies, 1)
+    stats = radix_sum(stats, "dp", copies, 4)
     result = rows_kernel(down_kernel, hidden, (w_down,), width, 256, "down")
     stats, result = lax.optimization_barrier((stats, result))
-    stats = radix_sum(stats, "dp", copies, 4)
+
+    load, mass = stats[0, :experts], stats[1, :experts]
+    mine = lax.axis_index("expert")
+    aux_loss = experts * jnp.sum(load / (all_tokens * picks) * (mass / all_tokens))
+    high = aux_loss.astype(BF16)
+    middle = (aux_loss - high.astype(F32)).astype(BF16)
+    low = (aux_loss - high.astype(F32) - middle.astype(F32)).astype(BF16)
+    lanes = lax.broadcasted_iota(jnp.int32, (1, 1, toks), 2)
+    line = jnp.where(lanes == 0, high, jnp.where(lanes == 1, middle, jnp.where(lanes == 2, low, BF16(0))))
+    result = result.reshape(group, cap, width)
+    last = result[:, cap - 1 :, :toks]
+    is_free = meta[mine, 5] > 0
+    line = jnp.where(is_free, line, last)
+    result = lax.dynamic_update_slice(result, line, (0, cap - 1, 0)).reshape(experts * cap, width)
+
     returned = lax.all_to_all(result, "expert", split_axis=0, concat_axis=0, tiled=True)
-    stats, returned = lax.optimization_barrier((stats, returned))
-    mixed = combine(meta, returned)
-    load, mass = stats[:, 0], stats[:, 1]
-    aux_loss = experts * jnp.sum(load / (all_tokens * picks) * (mass / all_tokens))
-    return mixed, aux_loss
+    mixed, note = combine(meta, returned)
+    return mixed, note[0, 0] + note[0, 1] + note[0, 2]
 
 
 def solution(mesh):

time: 135 us -> 135 us (level)
  the two profiles are of different devices: /device:TPU:189 before, /device:TPU:1 now
where the time goes in v2:
time: 135 us; the launch traced here: 133 us
  blocking collectives  44.5 us (33%)
  waiting for transfers between devices  39.8 us (29%)
  starting transfers between devices  22 us (16%)
  Pallas kernels  15.7 us (12%)
  local copies, waits for them, and re-layouts  4.82 us (4%)
  between operations  4.45 us (3%)
  other arithmetic  1.96 us (1%)
    all_to_all x1, blocking collectives, on_device(): lax.all_to_all(result, 'expert', split_axis=0, concat_axis=0, tiled=True)  44.5 us
    all_to_all x1, waiting for transfers between devices, on_device(): lax.all_to_all(outgoing, 'expert', split_axis=0, concat_axis=0, tiled=True)  39.7 us
    ppermute x6, starting transfers between devices, radix_sum(): total = total + lax.ppermute(value, axis, pairs)  14.3 us
    pallas_call x2, Pallas kernels, rows_kernel(): pl.pallas_call(body, grid=(rows // block,), in_specs=[pl.BlockSpec((block...  8.35 us
    all_to_all x1, starting transfers between devices, on_device(): lax.all_to_all(outgoing, 'expert', split_axis=0, concat_axis=0, tiled=True)  7.71 us
    pallas_call x1, Pallas kernels, pack(): pl.pallas_call(functools.partial(pack_kernel, cap), grid=(PARTS,), in_spe...  4.53 us
    unnamed x8, local copies, waits for them, and re-layouts  3.79 us
    pallas_call x1, Pallas kernels, combine(): pl.pallas_call(combine_kernel, grid=(PARTS,), in_specs=[pl.BlockSpec(meta...  2.86 us
  transfers between devices with their start and end apart: 7, of which 2 were waited for; matrix products, arithmetic and copies ran while one was open for 0% of the time, Pallas kernels for 6%

profile of v2, /device:TPU:1, one launch (start us, length us, event | category | flops | bytes accessed | tf_op | source)
XLA Modules:
  0.0 133.2 jit_solution(11350613838773300763)
XLA Ops:
  0.6 4.5 %pack.1 = (bf16[768,2048]{1,0:T(8,128)(2,1)}, f32[128,128]{1,0:T(8,128)}) custom-call(s32[2,128]{1,0:T(2,128)} %bitcast.17, f32[2,128]{1,0:T(2,128)} %bitcast.18, bf16[128,2048]{1,0:T(8,128)(2,1)} %tok_ref.1), custom_call_target="tpu_custom_call" | custom-call | flops 402653184 | bytes 6291456 | tf_op jit(solution)/shard_map/pack/pallas_call | solution.py:76
  5.2 0.0 copy-start
  5.2 7.7 %all-to-all-start = ((bf16[16,48,2048]{2,1,0:T(8,128)(2,1)}), bf16[16,48,2048]{2,1,0:T(8,128)(2,1)S(1)}, u32[]{:S(2)}, u32[]{:S(2)}) async-start(bf16[16,48,2048]{2,1,0:T(8,128)(2,1)} %bitcast.16), calls=%async_computation | async-start | bytes 6291456 | tf_op jit(solution)/shard_map/all_to_all | solution.py:196
  12.9 0.0 copy-done
  12.9 0.6 fusion.2
  13.5 39.7 %all-to-all-done = bf16[16,48,2048]{2,1,0:T(8,128)(2,1)S(1)} async-done(((bf16[16,48,2048]{2,1,0:T(8,128)(2,1)}), bf16[16,48,2048]{2,1,0:T(8,128)(2,1)S(1)}, u32[]{:S(2)}, u32[]{:S(2)}) %all-to-all-start) | async-done | bytes 3145760 | tf_op jit(solution)/shard_map/all_to_all | solution.py:196
  53.2 0.1 fusion
  53.3 3.2 %collective-permute-start.2 = (f32[2,128]{1,0:T(2,128)S(1)}, f32[2,128]{1,0:T(2,128)S(1)}, u32[]{:S(2)}, u32[]{:S(2)}) collective-permute-start(f32[2,128]{1,0:T(2,128)S(1)} %pad_maximum_fusion), channel_id=1, source_target_pairs={{0,48},{16,0},{32,16},{48,32},{64,112},{80,64},{96,80},{112,96},{1... | collective-permute-start | bytes 3080 | tf_op jit(solution)/shard_map/ppermute | solution.py:182
  56.5 1.7 %collective-permute-start.1 = (f32[2,128]{1,0:T(2,128)S(1)}, f32[2,128]{1,0:T(2,128)S(1)}, u32[]{:S(2)}, u32[]{:S(2)}) collective-permute-start(f32[2,128]{1,0:T(2,128)S(1)} %pad_maximum_fusion), channel_id=1, source_target_pairs={{0,32},{16,48},{32,0},{48,16},{64,96},{80,112},{96,64},{112,80},{1... | collective-permute-start | bytes 3080 | tf_op jit(solution)/shard_map/ppermute | solution.py:182
  58.1 0.1 collective-permute-start
  58.2 0.0 copy-start.1
  58.2 1.9 %copy-done.1 = bf16[1,2048,768]{2,1,0:T(8,128)(2,1)S(1)} copy-done((bf16[1,2048,768]{2,1,0:T(8,128)(2,1)S(1)}, bf16[1,2048,768]{2,1,0:T(8,128)(2,1)}, u32[]{:S(2)}) %copy-start.1) | copy-done | bytes 3145752
  60.1 0.0 copy-start.2
  60.1 1.9 %copy-done.2 = bf16[1,2048,768]{2,1,0:T(8,128)(2,1)S(1)} copy-done((bf16[1,2048,768]{2,1,0:T(8,128)(2,1)S(1)}, bf16[1,2048,768]{2,1,0:T(8,128)(2,1)}, u32[]{:S(2)}) %copy-start.2) | copy-done | bytes 3145752
  62.0 0.0 copy-start.3
  62.0 5.4 %hidden.1.x_ref = bf16[768,768]{1,0:T(8,128)(2,1)S(1)} custom-call(bf16[768,2048]{1,0:T(8,128)(2,1)S(1)} %bitcast.13, bf16[1,2048,768]{2,1,0:T(8,128)(2,1)S(1)} %copy-done.1, bf16[1,2048,768]{2,1,0:T(8,128)(2,1)S(1)} %copy-done.2), custom_call_target="tpu_custom_call" | custom-call | flops 4831838208 | bytes 10616832 | tf_op jit(solution)/shard_map/hidden/pallas_call | solution.py:111
  67.4 0.0 collective-permute-done.2
  67.4 0.0 collective-permute-done.1
  67.4 0.0 collective-permute-done
  67.4 6.1 %collective-permute-start.5 = (f32[2,128]{1,0:T(2,128)S(1)}, f32[2,128]{1,0:T(2,128)S(1)}, u32[]{:S(2)}, u32[]{:S(2)}) collective-permute-start(f32[2,128]{1,0:T(2,128)S(1)} %add_add_fusion.1), channel_id=1, source_target_pairs={{0,192},{16,208},{32,224},{48,240},{64,0},{80,16},{96,32},{112,48}... | collective-permute-start | bytes 3080 | tf_op jit(solution)/shard_map/ppermute | solution.py:182
  73.5 1.0 collective-permute-start.4
  74.5 2.3 %collective-permute-start.3 = (f32[2,128]{1,0:T(2,128)S(1)}, f32[2,128]{1,0:T(2,128)S(1)}, u32[]{:S(2)}, u32[]{:S(2)}) collective-permute-start(f32[2,128]{1,0:T(2,128)S(1)} %add_add_fusion.1), channel_id=1, source_target_pairs={{0,64},{16,80},{32,96},{48,112},{64,128},{80,144},{96,160},{112,17... | collective-permute-start | bytes 3080 | tf_op jit(solution)/shard_map/ppermute | solution.py:182
  76.8 0.0 copy-done.3
  76.8 3.0 %down.1 = bf16[768,2048]{1,0:T(8,128)(2,1)S(1)} custom-call(bf16[768,768]{1,0:T(8,128)(2,1)S(1)} %hidden.1.x_ref, bf16[1,768,2048]{2,1,0:T(8,128)(2,1)S(1)} %copy-done.3), custom_call_target="tpu_custom_call" | custom-call | flops 2415919104 | bytes 7471104 | tf_op jit(solution)/shard_map/down/pallas_call | solution.py:111
  79.8 0.0 collective-permute-done.5
  79.8 0.1 collective-permute-done.4
  79.9 0.0 collective-permute-done.3
  79.9 0.6 multiply_reduce_fusion
  81.2 0.7 broadcast_select_fusion
  81.8 0.4 dynamic_update_slice.3
  82.2 44.5 %all_to_all.20 = bf16[16,48,2048]{2,1,0:T(8,128)(2,1)S(1)} all-to-all(bf16[16,48,2048]{2,1,0:T(8,128)(2,1)S(1)} %dynamic_update_slice.3), channel_id=1, replica_groups=mesh['dp'=16,'expert'=16] {'expert'}, dimensions={0} | all-to-all | bytes 6291456 | tf_op jit(solution)/shard_map/all_to_all | solution.py:223
  126.7 2.9 %combine.1 = (bf16[128,2048]{1,0:T(8,128)(2,1)}, f32[8,128]{1,0:T(8,128)S(1)}) custom-call(f32[128,128]{1,0:T(8,128)S(1)} %copy-done, bf16[768,2048]{1,0:T(8,128)(2,1)S(1)} %bitcast.12), custom_call_target="tpu_custom_call" | custom-call | flops 805306368 | bytes 3145728 | tf_op jit(solution)/shard_map/combine/pallas_call | solution.py:151
  129.5 0.6 fusion.1
  (5 shorter events, 0.0 us)
Async XLA Ops:
  5.2 7.7 %copy-start = (f32[128,128]{1,0:T(8,128)S(1)}, f32[128,128]{1,0:T(8,128)}, u32[]{:S(2)}) copy-start(f32[128,128]{1,0:T(8,128)} %get-tuple-element.12.meta_ref) | copy-start | bytes 196612
  5.2 48.0 %all-to-all-start = ((bf16[16,48,2048]{2,1,0:T(8,128)(2,1)}), bf16[16,48,2048]{2,1,0:T(8,128)(2,1)S(1)}, u32[]{:S(2)}, u32[]{:S(2)}) async-start(bf16[16,48,2048]{2,1,0:T(8,128)(2,1)} %bitcast.16), calls=%async_computation | async-start | bytes 6291456 | tf_op jit(solution)/shard_map/all_to_all | solution.py:196
  53.3 14.1 %collective-permute-start.2 = (f32[2,128]{1,0:T(2,128)S(1)}, f32[2,128]{1,0:T(2,128)S(1)}, u32[]{:S(2)}, u32[]{:S(2)}) collective-permute-start(f32[2,128]{1,0:T(2,128)S(1)} %pad_maximum_fusion), channel_id=1, source_target_pairs={{0,48},{16,0},{32,16},{48,32},{64,112},{80,64},{96,80},{112,96},{1... | collective-permute-start | bytes 3080 | tf_op jit(solution)/shard_map/ppermute | solution.py:182
  56.5 10.9 %collective-permute-start.1 = (f32[2,128]{1,0:T(2,128)S(1)}, f32[2,128]{1,0:T(2,128)S(1)}, u32[]{:S(2)}, u32[]{:S(2)}) collective-permute-start(f32[2,128]{1,0:T(2,128)S(1)} %pad_maximum_fusion), channel_id=1, source_target_pairs={{0,32},{16,48},{32,0},{48,16},{64,96},{80,112},{96,64},{112,80},{1... | collective-permute-start | bytes 3080 | tf_op jit(solution)/shard_map/ppermute | solution.py:182
  58.1 9.3 %collective-permute-start = (f32[2,128]{1,0:T(2,128)S(1)}, f32[2,128]{1,0:T(2,128)S(1)}, u32[]{:S(2)}, u32[]{:S(2)}) collective-permute-start(f32[2,128]{1,0:T(2,128)S(1)} %pad_maximum_fusion), channel_id=1, source_target_pairs={{0,16},{16,32},{32,48},{48,0},{64,80},{80,96},{96,112},{112,64},{1... | collective-permute-start | bytes 3080 | tf_op jit(solution)/shard_map/ppermute | solution.py:182
  58.2 1.9 %copy-start.1 = (bf16[1,2048,768]{2,1,0:T(8,128)(2,1)S(1)}, bf16[1,2048,768]{2,1,0:T(8,128)(2,1)}, u32[]{:S(2)}) copy-start(bf16[1,2048,768]{2,1,0:T(8,128)(2,1)} %gate_ref.1) | copy-start | bytes 9437188
  60.1 1.9 %copy-start.2 = (bf16[1,2048,768]{2,1,0:T(8,128)(2,1)S(1)}, bf16[1,2048,768]{2,1,0:T(8,128)(2,1)}, u32[]{:S(2)}) copy-start(bf16[1,2048,768]{2,1,0:T(8,128)(2,1)} %up_ref.1) | copy-start | bytes 9437188
  62.0 14.8 %copy-start.3 = (bf16[1,768,2048]{2,1,0:T(8,128)(2,1)S(1)}, bf16[1,768,2048]{2,1,0:T(8,128)(2,1)}, u32[]{:S(2)}) copy-start(bf16[1,768,2048]{2,1,0:T(8,128)(2,1)} %down_ref.1) | copy-start | bytes 9437188
  67.4 12.3 %collective-permute-start.5 = (f32[2,128]{1,0:T(2,128)S(1)}, f32[2,128]{1,0:T(2,128)S(1)}, u32[]{:S(2)}, u32[]{:S(2)}) collective-permute-start(f32[2,128]{1,0:T(2,128)S(1)} %add_add_fusion.1), channel_id=1, source_target_pairs={{0,192},{16,208},{32,224},{48,240},{64,0},{80,16},{96,32},{112,48}... | collective-permute-start | bytes 3080 | tf_op jit(solution)/shard_map/ppermute | solution.py:182
  73.5 6.3 %collective-permute-start.4 = (f32[2,128]{1,0:T(2,128)S(1)}, f32[2,128]{1,0:T(2,128)S(1)}, u32[]{:S(2)}, u32[]{:S(2)}) collective-permute-start(f32[2,128]{1,0:T(2,128)S(1)} %add_add_fusion.1), channel_id=1, source_target_pairs={{0,128},{16,144},{32,160},{48,176},{64,192},{80,208},{96,224},{112... | collective-permute-start | bytes 3080 | tf_op jit(solution)/shard_map/ppermute | solution.py:182
  74.5 5.3 %collective-permute-start.3 = (f32[2,128]{1,0:T(2,128)S(1)}, f32[2,128]{1,0:T(2,128)S(1)}, u32[]{:S(2)}, u32[]{:S(2)}) collective-permute-start(f32[2,128]{1,0:T(2,128)S(1)} %add_add_fusion.1), channel_id=1, source_target_pairs={{0,64},{16,80},{32,96},{48,112},{64,128},{80,144},{96,160},{112,17... | collective-permute-start | bytes 3080 | tf_op jit(solution)/shard_map/ppermute | solution.py:182

commit v3 on v1

v3 whole, which is shorter than its diff:
```python
import functools

import jax
import jax.numpy as jnp
from jax import lax
from jax.experimental import pallas as pl
from jax.experimental.pallas import tpu as pltpu
from jax.sharding import PartitionSpec as P

F32 = jnp.float32
BF16 = jnp.bfloat16
PARTS = 4
AXES = ("dp", "expert")


def pack_kernel(cap, ids_hbm, gates_hbm, tok_hbm, out_ref, meta_ref, stats_ref, ids_ref, gates_ref, tok_ref, sems):
    slots, toks = out_ref.shape[0], tok_ref.shape[0]
    rows = slots // PARTS
    ids_copy = pltpu.make_async_copy(ids_hbm, ids_ref, sems.at[0])
    gates_copy = pltpu.make_async_copy(gates_hbm, gates_ref, sems.at[1])
    tok_copy = pltpu.make_async_copy(tok_hbm, tok_ref, sems.at[2])
    ids_copy.start()
    gates_copy.start()
    tok_copy.start()
    ids_copy.wait()
    gates_copy.wait()

    ids = ids_ref[...]
    gates = gates_ref[...]
    labels = lax.broadcasted_iota(jnp.int32, (toks, toks), 0)
    lanes = lax.broadcasted_iota(jnp.int32, (toks, toks), 1)
    first = (labels == ids[0:1, :]).astype(F32)
    second = (labels == ids[1:2, :]).astype(F32)
    earlier = (labels < lanes).astype(F32).astype(BF16)
    first_rank = jnp.dot(first.astype(BF16), earlier, preferred_element_type=F32)
    second_rank = jnp.dot(second.astype(BF16), earlier, preferred_element_type=F32)
    first_count = jnp.sum(first, 1, keepdims=True)
    count = first_count + jnp.sum(second, 1, keepdims=True)
    mass = jnp.sum(first * gates[0:1, :] + second * gates[1:2, :], 1, keepdims=True)
    base = ids.astype(F32) * cap
    first_dest = base[0:1, :] + jnp.sum(first * first_rank, 0, keepdims=True)
    second_dest = base[1:2, :] + jnp.sum(second * (second_rank + first_count), 0, keepdims=True)
    stats_ref[...] = jnp.where(lanes == 0, count, jnp.where(lanes == 1, mass, 0.0)).T[:8, :]
    lines = jnp.where(labels == 0, first_dest, jnp.where(labels == 1, second_dest, 0.0))
    lines = jnp.where(labels == 2, gates[0:1, :], jnp.where(labels == 3, gates[1:2, :], lines))
    meta_ref[...] = lines.T

    tok_copy.wait()
    tokens = tok_ref[...]
    for part in range(PARTS):
        slot = lax.broadcasted_iota(jnp.int32, (rows, toks), 0) + part * rows
        pick = (slot == first_dest.astype(jnp.int32)) | (slot == second_dest.astype(jnp.int32))
        pick = pick.astype(F32).astype(BF16)
        out_ref[part * rows : (part + 1) * rows, :] = jnp.dot(
            pick, tokens, preferred_element_type=F32
        ).astype(BF16)


def pack(ids, gates, tokens, experts, cap):
    toks, width = tokens.shape
    slots = experts * cap
    return pl.pallas_call(
        functools.partial(pack_kernel, cap),
        in_specs=[pl.BlockSpec(memory_space=pltpu.HBM)] * 3,
        out_specs=[pl.BlockSpec(memory_space=pltpu.VMEM)] * 3,
        out_shape=[
            jax.ShapeDtypeStruct((slots, width), BF16),
            jax.ShapeDtypeStruct((toks, toks), F32),
            jax.ShapeDtypeStruct((8, toks), F32),
        ],
        scratch_shapes=[
            pltpu.VMEM(ids.shape, ids.dtype),
            pltpu.VMEM(gates.shape, gates.dtype),
            pltpu.VMEM(tokens.shape, tokens.dtype),
            pltpu.SemaphoreType.DMA((3,)),
        ],
        compiler_params=pltpu.CompilerParams(vmem_limit_bytes=16 * 2**20),
        cost_estimate=pl.CostEstimate(
            flops=2 * slots * toks * width, bytes_accessed=4 * slots * width, transcendentals=0
        ),
        name="pack",
    )(*(pltpu.with_memory_space_constraint(a, pltpu.HBM) for a in (ids, gates, tokens)))


def ffn_kernel(x_ref, gate_ref, up_ref, down_ref, out_ref):
    x = x_ref[...]
    gate = jnp.dot(x, gate_ref[0], preferred_element_type=F32)
    up = jnp.dot(x, up_ref[0], preferred_element_type=F32)
    hidden = (gate / (1.0 + jnp.exp(-gate)) * up).astype(BF16)
    out_ref[...] = jnp.dot(hidden, down_ref[0], preferred_element_type=F32).astype(BF16)


def ffn(x, w_gate, w_up, w_down):
    rows, width = x.shape
    middle = w_gate.shape[2]
    block = rows // 3
    held = pl.BlockSpec(memory_space=pltpu.VMEM)
    return pl.pallas_call(
        ffn_kernel,
        grid=(3,),
        in_specs=[pl.BlockSpec((block, width), lambda i: (i, 0)), held, held, held],
        out_specs=pl.BlockSpec((block, width), lambda i: (i, 0)),
        out_shape=pltpu.HBM((rows, width), BF16),
        compiler_params=pltpu.CompilerParams(vmem_limit_bytes=32 * 2**20),
        cost_estimate=pl.CostEstimate(
            flops=6 * rows * width * middle,
            bytes_accessed=4 * rows * width + 6 * width * middle,
            transcendentals=rows * middle,
        ),
        name="ffn",
    )(x, w_gate, w_up, w_down)


def combine_kernel(meta_ref, rows_ref, out_ref, pick_ref):
    toks = out_ref.shape[0]
    slots = rows_ref.shape[0]

    @pl.when(pl.program_id(0) == 0)
    def _():
        dest = meta_ref[:, 0:2].astype(jnp.int32)
        lane = lax.broadcasted_iota(jnp.int32, (toks, slots), 1)
        pick_ref[:toks, :] = (lane == dest[:, 0:1]).astype(F32).astype(BF16)
        pick_ref[toks:, :] = (lane == dest[:, 1:2]).astype(F32).astype(BF16)

    both = jnp.dot(pick_ref[...], rows_ref[...], preferred_element_type=F32)
    weights = meta_ref[:, 2:4]
    out_ref[...] = (weights[:, 0:1] * both[:toks] + weights[:, 1:2] * both[toks:]).astype(BF16)


def combine(meta, rows):
    toks = meta.shape[0]
    slots, width = rows.shape
    block = width // PARTS
    return pl.pallas_call(
        combine_kernel,
        grid=(PARTS,),
        in_specs=[
            pl.BlockSpec(meta.shape, lambda i: (0, 0)),
            pl.BlockSpec((slots, block), lambda i: (0, i)),
        ],
        out_specs=pl.BlockSpec((toks, block), lambda i: (0, i)),
        out_shape=jax.ShapeDtypeStruct((toks, width), BF16),
        scratch_shapes=[pltpu.VMEM((2 * toks, slots), BF16)],
        compiler_params=pltpu.CompilerParams(vmem_limit_bytes=16 * 2**20),
        cost_estimate=pl.CostEstimate(
            flops=4 * toks * slots * width, bytes_accessed=2 * slots * width, transcendentals=0
        ),
        name="combine",
    )(meta, rows)


def add_round(value, size, stride, step):
    return value + lax.ppermute(value, AXES, [(i, i ^ stride) for i in range(size) if (i // step) % 2 == 1])


def hand_over(value, size, step, sender):
    turn = step if sender == 0 else -step
    return lax.ppermute(value, AXES, [(i, i + turn) for i in range(size) if (i // step) % 2 == sender])


def on_device(tokens, expert_ids, gate_weights, w_gate, w_up, w_down):
    toks, width = tokens.shape
    picks = expert_ids.shape[1]
    group = lax.axis_size("expert")
    copies = lax.axis_size("dp")
    experts = w_gate.shape[0] * group
    cap = min(toks * picks // 4, 3 * toks * picks // experts)
    all_tokens = toks * group * copies

    size = copies * group
    stride = 2 * group
    outgoing, meta, stats = pack(expert_ids.T, gate_weights.T, tokens, experts, cap)
    stats = stats + hand_over(stats, size, group, 0)
    for bit in (1, 2, 4, 8):
        stats = add_round(stats, size, bit, group)
    stats, outgoing = lax.optimization_barrier((stats, outgoing))
    received = lax.all_to_all(outgoing, "expert", split_axis=0, concat_axis=0, tiled=True)
    result = ffn(received, w_gate, w_up, w_down)
    stats, result = lax.optimization_barrier((stats, result))
    returned = lax.all_to_all(result, "expert", split_axis=0, concat_axis=0, tiled=True)
    for bit in (stride, 2 * stride, 4 * stride):
        stats = add_round(stats, size, bit, group)
    stats = jnp.where(lax.axis_index("dp") % 2 == 1, stats, hand_over(stats, size, group, 1))
    load, mass = stats[0, :experts], stats[1, :experts]
    aux_loss = experts * jnp.sum(load / (all_tokens * picks) * (mass / all_tokens))
    return combine(meta, returned), aux_loss


def solution(mesh):
    rows = P(("dp", "expert"), None)
    held = P("expert", None, None)
    return jax.shard_map(
        on_device,
        mesh=mesh,
        in_specs=(rows, rows, rows, held, held, held),
        out_specs=(rows, P()),
        check_vma=False,
    )
```

time: 135 us -> 102 us (0.76)
  the two profiles are of different devices: /device:TPU:189 before, /device:TPU:1 now
where the time goes in v3:
time: 102 us; the launch traced here: 100 us
  starting transfers between devices  33.4 us (33%)
  blocking collectives  28.5 us (28%)
  waiting for transfers between devices  19.7 us (19%)
  Pallas kernels  13.7 us (13%)
  between operations  2.53 us (2%)
  local copies, waits for them, and re-layouts  1.9 us (2%)
    all_to_all x1, blocking collectives, on_device(): lax.all_to_all(outgoing, 'expert', split_axis=0, concat_axis=0, tiled=True)  28.5 us
    ppermute x7, starting transfers between devices, add_round(): lax.ppermute(value, AXES, [(i, i ^ stride) for i in range(size) if i // s...  27.1 us
    ppermute x7, waiting for transfers between devices, add_round(): lax.ppermute(value, AXES, [(i, i ^ stride) for i in range(size) if i // s...  13.7 us
    pallas_call x1, Pallas kernels, ffn(): pl.pallas_call(ffn_kernel, grid=(3,), in_specs=[pl.BlockSpec((block, widt...  8.82 us
    ppermute x2, waiting for transfers between devices, hand_over(): lax.ppermute(value, AXES, [(i, i + turn) for i in range(size) if i // ste...  4.66 us
    all_to_all x1, starting transfers between devices, on_device(): lax.all_to_all(result, 'expert', split_axis=0, concat_axis=0, tiled=True)  3.74 us
    pallas_call x1, Pallas kernels, combine(): pl.pallas_call(combine_kernel, grid=(PARTS,), in_specs=[pl.BlockSpec(meta...  2.78 us
    ppermute x2, starting transfers between devices, hand_over(): lax.ppermute(value, AXES, [(i, i + turn) for i in range(size) if i // ste...  2.57 us
  transfers between devices with their start and end apart: 10, of which 10 were waited for; matrix products, arithmetic and copies ran while one was open for 1% of the time, Pallas kernels for 0%

profile of v3, /device:TPU:1, one launch (start us, length us, event | category | flops | bytes accessed | tf_op | source)
XLA Modules:
  0.0 100.4 jit_solution(6035134600165629730)
XLA Ops:
  0.6 2.1 %pack.1 = (bf16[768,2048]{1,0:T(8,128)(2,1)S(1)}, f32[128,128]{1,0:T(8,128)S(1)}, f32[8,128]{1,0:T(8,128)S(1)}) custom-call(s32[2,128]{1,0:T(2,128)} %bitcast.10, f32[2,128]{1,0:T(2,128)} %bitcast.11, bf16[128,2048]{1,0:T(8,128)(2,1)} %tok_hbm.1), custom_call_target="tpu_custom_call" | custom-call | flops 402653184 | bytes 6291456 | tf_op jit(solution)/shard_map/pack/pallas_call | solution.py:62
  2.7 1.3 %collective-permute-start = (f32[8,128]{1,0:T(8,128)S(1)}, f32[8,128]{1,0:T(8,128)S(1)}, u32[]{:S(2)}, u32[]{:S(2)}) collective-permute-start(f32[8,128]{1,0:T(8,128)S(1)} %get-tuple-element.10), channel_id=1, source_target_pairs={{0,16},{1,17},{2,18},{3,19},{4,20},{5,21},{6,22},{7,23},{8,24},{9,... | collective-permute-start | bytes 12296 | tf_op jit(solution)/shard_map/ppermute | solution.py:158
  4.0 3.9 %collective-permute-done = f32[8,128]{1,0:T(8,128)S(1)} collective-permute-done((f32[8,128]{1,0:T(8,128)S(1)}, f32[8,128]{1,0:T(8,128)S(1)}, u32[]{:S(2)}, u32[]{:S(2)}) %collective-permute-start) | collective-permute-done | bytes 4128 | tf_op jit(solution)/shard_map/ppermute | solution.py:158
  7.9 1.9 %collective-permute-start.1 = (f32[8,128]{1,0:T(8,128)S(1)}, f32[8,128]{1,0:T(8,128)S(1)}, u32[]{:S(2)}, u32[]{:S(2)}) collective-permute-start(f32[8,128]{1,0:T(8,128)S(1)} %add.28), channel_id=1, source_target_pairs={{16,17},{17,16},{18,19},{19,18},{20,21},{21,20},{22,23},{23,22},{2... | collective-permute-start | bytes 12296 | tf_op jit(solution)/shard_map/ppermute | solution.py:153
  9.8 2.4 %collective-permute-done.1 = f32[8,128]{1,0:T(8,128)S(1)} collective-permute-done((f32[8,128]{1,0:T(8,128)S(1)}, f32[8,128]{1,0:T(8,128)S(1)}, u32[]{:S(2)}, u32[]{:S(2)}) %collective-permute-start.1) | collective-permute-done | bytes 4128 | tf_op jit(solution)/shard_map/ppermute | solution.py:153
  12.2 3.5 %collective-permute-start.2 = (f32[8,128]{1,0:T(8,128)S(1)}, f32[8,128]{1,0:T(8,128)S(1)}, u32[]{:S(2)}, u32[]{:S(2)}) collective-permute-start(f32[8,128]{1,0:T(8,128)S(1)} %add.29), channel_id=1, source_target_pairs={{16,18},{17,19},{18,16},{19,17},{20,22},{21,23},{22,20},{23,21},{2... | collective-permute-start | bytes 12296 | tf_op jit(solution)/shard_map/ppermute | solution.py:153
  15.8 2.3 %collective-permute-done.2 = f32[8,128]{1,0:T(8,128)S(1)} collective-permute-done((f32[8,128]{1,0:T(8,128)S(1)}, f32[8,128]{1,0:T(8,128)S(1)}, u32[]{:S(2)}, u32[]{:S(2)}) %collective-permute-start.2) | collective-permute-done | bytes 4128 | tf_op jit(solution)/shard_map/ppermute | solution.py:153
  18.1 1.9 %collective-permute-start.3 = (f32[8,128]{1,0:T(8,128)S(1)}, f32[8,128]{1,0:T(8,128)S(1)}, u32[]{:S(2)}, u32[]{:S(2)}) collective-permute-start(f32[8,128]{1,0:T(8,128)S(1)} %add.30), channel_id=1, source_target_pairs={{16,20},{17,21},{18,22},{19,23},{20,16},{21,17},{22,18},{23,19},{2... | collective-permute-start | bytes 12296 | tf_op jit(solution)/shard_map/ppermute | solution.py:153
  20.0 2.8 %collective-permute-done.3 = f32[8,128]{1,0:T(8,128)S(1)} collective-permute-done((f32[8,128]{1,0:T(8,128)S(1)}, f32[8,128]{1,0:T(8,128)S(1)}, u32[]{:S(2)}, u32[]{:S(2)}) %collective-permute-start.3) | collective-permute-done | bytes 4128 | tf_op jit(solution)/shard_map/ppermute | solution.py:153
  22.8 3.4 %collective-permute-start.4 = (f32[8,128]{1,0:T(8,128)S(1)}, f32[8,128]{1,0:T(8,128)S(1)}, u32[]{:S(2)}, u32[]{:S(2)}) collective-permute-start(f32[8,128]{1,0:T(8,128)S(1)} %add.31), channel_id=1, source_target_pairs={{16,24},{17,25},{18,26},{19,27},{20,28},{21,29},{22,30},{23,31},{2... | collective-permute-start | bytes 12296 | tf_op jit(solution)/shard_map/ppermute | solution.py:153
  26.2 2.9 %collective-permute-done.4 = f32[8,128]{1,0:T(8,128)S(1)} collective-permute-done((f32[8,128]{1,0:T(8,128)S(1)}, f32[8,128]{1,0:T(8,128)S(1)}, u32[]{:S(2)}, u32[]{:S(2)}) %collective-permute-start.4) | collective-permute-done | bytes 4128 | tf_op jit(solution)/shard_map/ppermute | solution.py:153
  29.1 0.0 copy-start
  29.1 0.0 copy-start.1
  29.1 28.5 %all_to_all.22 = bf16[16,48,2048]{2,1,0:T(8,128)(2,1)S(1)} all-to-all(bf16[16,48,2048]{2,1,0:T(8,128)(2,1)S(1)} %bitcast.7), channel_id=1, replica_groups=mesh['dp'=16,'expert'=16] {'expert'}, dimensions={0} | all-to-all | bytes 6291456 | tf_op jit(solution)/shard_map/all_to_all | solution.py:177
  57.6 0.0 copy-done
  57.6 0.0 copy-done.1
  57.6 0.0 copy-start.2
  57.6 1.9 %copy-done.2 = bf16[1,768,2048]{2,1,0:T(8,128)(2,1)S(1)} copy-done((bf16[1,768,2048]{2,1,0:T(8,128)(2,1)S(1)}, bf16[1,768,2048]{2,1,0:T(8,128)(2,1)}, u32[]{:S(2)}) %copy-start.2) | copy-done | bytes 3145752
  59.5 8.8 %ffn.1 = bf16[768,2048]{1,0:T(8,128)(2,1)} custom-call(bf16[768,2048]{1,0:T(8,128)(2,1)S(1)} %bitcast.8, bf16[1,2048,768]{2,1,0:T(8,128)(2,1)S(1)} %copy-done, bf16[1,2048,768]{2,1,0:T(8,128)(2,1)S(1)} %copy-done.1, bf16[1,768,2048]{2,1,0:T(8,128)(2,1)S(1)} %copy-done.2), custom_call_target="tpu_custom_call" | custom-call | flops 7247757312 | bytes 15728640 | tf_op jit(solution)/shard_map/ffn/pallas_call | solution.py:98
  68.3 3.7 %all-to-all-start.1 = ((bf16[16,48,2048]{2,1,0:T(8,128)(2,1)}), bf16[16,48,2048]{2,1,0:T(8,128)(2,1)S(1)}, u32[]{:S(2)}, u32[]{:S(2)}) async-start(bf16[16,48,2048]{2,1,0:T(8,128)(2,1)} %bitcast.9), calls=%async_computation.1 | async-start | bytes 6291456 | tf_op jit(solution)/shard_map/all_to_all | solution.py:180
  72.1 3.6 %collective-permute-start.5 = (f32[8,128]{1,0:T(8,128)S(1)}, f32[8,128]{1,0:T(8,128)S(1)}, u32[]{:S(2)}, u32[]{:S(2)}) collective-permute-start(f32[8,128]{1,0:T(8,128)S(1)} %add.32), channel_id=1, source_target_pairs={{16,48},{17,49},{18,50},{19,51},{20,52},{21,53},{22,54},{23,55},{2... | collective-permute-start | bytes 12296 | tf_op jit(solution)/shard_map/ppermute | solution.py:153
  75.6 1.3 %collective-permute-done.5 = f32[8,128]{1,0:T(8,128)S(1)} collective-permute-done((f32[8,128]{1,0:T(8,128)S(1)}, f32[8,128]{1,0:T(8,128)S(1)}, u32[]{:S(2)}, u32[]{:S(2)}) %collective-permute-start.5) | collective-permute-done | bytes 4128 | tf_op jit(solution)/shard_map/ppermute | solution.py:153
  76.9 4.9 %collective-permute-start.6 = (f32[8,128]{1,0:T(8,128)S(1)}, f32[8,128]{1,0:T(8,128)S(1)}, u32[]{:S(2)}, u32[]{:S(2)}) collective-permute-start(f32[8,128]{1,0:T(8,128)S(1)} %add.34), channel_id=1, source_target_pairs={{16,80},{17,81},{18,82},{19,83},{20,84},{21,85},{22,86},{23,87},{2... | collective-permute-start | bytes 12296 | tf_op jit(solution)/shard_map/ppermute | solution.py:153
  81.8 1.0 collective-permute-done.6
  82.8 8.0 %collective-permute-start.7 = (f32[8,128]{1,0:T(8,128)S(1)}, f32[8,128]{1,0:T(8,128)S(1)}, u32[]{:S(2)}, u32[]{:S(2)}) collective-permute-start(f32[8,128]{1,0:T(8,128)S(1)} %add.35), channel_id=1, source_target_pairs={{16,144},{17,145},{18,146},{19,147},{20,148},{21,149},{22,150},{23... | collective-permute-start | bytes 12296 | tf_op jit(solution)/shard_map/ppermute | solution.py:153
  90.8 1.0 collective-permute-done.7
  91.8 1.3 %collective-permute-start.8 = (f32[8,128]{1,0:T(8,128)S(1)}, f32[8,128]{1,0:T(8,128)S(1)}, u32[]{:S(2)}, u32[]{:S(2)}) collective-permute-start(f32[8,128]{1,0:T(8,128)S(1)} %add.36), channel_id=1, source_target_pairs={{16,0},{17,1},{18,2},{19,3},{20,4},{21,5},{22,6},{23,7},{24,8},{25... | collective-permute-start | bytes 12296 | tf_op jit(solution)/shard_map/ppermute | solution.py:158
  93.1 0.8 collective-permute-done.8
  93.9 0.6 multiply_reduce_fusion
  95.1 1.4 %all-to-all-done.1 = bf16[16,48,2048]{2,1,0:T(8,128)(2,1)S(1)} async-done(((bf16[16,48,2048]{2,1,0:T(8,128)(2,1)}), bf16[16,48,2048]{2,1,0:T(8,128)(2,1)S(1)}, u32[]{:S(2)}, u32[]{:S(2)}) %all-to-all-start.1) | async-done | bytes 3145760 | tf_op jit(solution)/shard_map/all_to_all | solution.py:180
  96.5 2.8 %combine.1 = bf16[128,2048]{1,0:T(8,128)(2,1)} custom-call(f32[128,128]{1,0:T(8,128)S(1)} %get-tuple-element.9.meta_ref, bf16[768,2048]{1,0:T(8,128)(2,1)S(1)} %bitcast.6), custom_call_target="tpu_custom_call" | custom-call | flops 805306368 | bytes 3145728 | tf_op jit(solution)/shard_map/combine/pallas_call | solution.py:134
  (9 shorter events, 0.0 us)
Async XLA Ops:
  2.7 5.2 %collective-permute-start = (f32[8,128]{1,0:T(8,128)S(1)}, f32[8,128]{1,0:T(8,128)S(1)}, u32[]{:S(2)}, u32[]{:S(2)}) collective-permute-start(f32[8,128]{1,0:T(8,128)S(1)} %get-tuple-element.10), channel_id=1, source_target_pairs={{0,16},{1,17},{2,18},{3,19},{4,20},{5,21},{6,22},{7,23},{8,24},{9,... | collective-permute-start | bytes 12296 | tf_op jit(solution)/shard_map/ppermute | solution.py:158
  7.9 4.3 %collective-permute-start.1 = (f32[8,128]{1,0:T(8,128)S(1)}, f32[8,128]{1,0:T(8,128)S(1)}, u32[]{:S(2)}, u32[]{:S(2)}) collective-permute-start(f32[8,128]{1,0:T(8,128)S(1)} %add.28), channel_id=1, source_target_pairs={{16,17},{17,16},{18,19},{19,18},{20,21},{21,20},{22,23},{23,22},{2... | collective-permute-start | bytes 12296 | tf_op jit(solution)/shard_map/ppermute | solution.py:153
  12.2 5.8 %collective-permute-start.2 = (f32[8,128]{1,0:T(8,128)S(1)}, f32[8,128]{1,0:T(8,128)S(1)}, u32[]{:S(2)}, u32[]{:S(2)}) collective-permute-start(f32[8,128]{1,0:T(8,128)S(1)} %add.29), channel_id=1, source_target_pairs={{16,18},{17,19},{18,16},{19,17},{20,22},{21,23},{22,20},{23,21},{2... | collective-permute-start | bytes 12296 | tf_op jit(solution)/shard_map/ppermute | solution.py:153
  18.1 4.7 %collective-permute-start.3 = (f32[8,128]{1,0:T(8,128)S(1)}, f32[8,128]{1,0:T(8,128)S(1)}, u32[]{:S(2)}, u32[]{:S(2)}) collective-permute-start(f32[8,128]{1,0:T(8,128)S(1)} %add.30), channel_id=1, source_target_pairs={{16,20},{17,21},{18,22},{19,23},{20,16},{21,17},{22,18},{23,19},{2... | collective-permute-start | bytes 12296 | tf_op jit(solution)/shard_map/ppermute | solution.py:153
  22.8 6.2 %collective-permute-start.4 = (f32[8,128]{1,0:T(8,128)S(1)}, f32[8,128]{1,0:T(8,128)S(1)}, u32[]{:S(2)}, u32[]{:S(2)}) collective-permute-start(f32[8,128]{1,0:T(8,128)S(1)} %add.31), channel_id=1, source_target_pairs={{16,24},{17,25},{18,26},{19,27},{20,28},{21,29},{22,30},{23,31},{2... | collective-permute-start | bytes 12296 | tf_op jit(solution)/shard_map/ppermute | solution.py:153
  29.1 28.5 %copy-start = (bf16[1,2048,768]{2,1,0:T(8,128)(2,1)S(1)}, bf16[1,2048,768]{2,1,0:T(8,128)(2,1)}, u32[]{:S(2)}) copy-start(bf16[1,2048,768]{2,1,0:T(8,128)(2,1)} %gate_ref.1) | copy-start | bytes 9437188
  29.1 28.5 %copy-start.1 = (bf16[1,2048,768]{2,1,0:T(8,128)(2,1)S(1)}, bf16[1,2048,768]{2,1,0:T(8,128)(2,1)}, u32[]{:S(2)}) copy-start(bf16[1,2048,768]{2,1,0:T(8,128)(2,1)} %up_ref.1) | copy-start | bytes 9437188
  57.6 1.9 %copy-start.2 = (bf16[1,768,2048]{2,1,0:T(8,128)(2,1)S(1)}, bf16[1,768,2048]{2,1,0:T(8,128)(2,1)}, u32[]{:S(2)}) copy-start(bf16[1,768,2048]{2,1,0:T(8,128)(2,1)} %down_ref.1) | copy-start | bytes 9437188
  68.3 28.2 %all-to-all-start.1 = ((bf16[16,48,2048]{2,1,0:T(8,128)(2,1)}), bf16[16,48,2048]{2,1,0:T(8,128)(2,1)S(1)}, u32[]{:S(2)}, u32[]{:S(2)}) async-start(bf16[16,48,2048]{2,1,0:T(8,128)(2,1)} %bitcast.9), calls=%async_computation.1 | async-start | bytes 6291456 | tf_op jit(solution)/shard_map/all_to_all | solution.py:180
  72.1 4.8 %collective-permute-start.5 = (f32[8,128]{1,0:T(8,128)S(1)}, f32[8,128]{1,0:T(8,128)S(1)}, u32[]{:S(2)}, u32[]{:S(2)}) collective-permute-start(f32[8,128]{1,0:T(8,128)S(1)} %add.32), channel_id=1, source_target_pairs={{16,48},{17,49},{18,50},{19,51},{20,52},{21,53},{22,54},{23,55},{2... | collective-permute-start | bytes 12296 | tf_op jit(solution)/shard_map/ppermute | solution.py:153
  76.9 5.9 %collective-permute-start.6 = (f32[8,128]{1,0:T(8,128)S(1)}, f32[8,128]{1,0:T(8,128)S(1)}, u32[]{:S(2)}, u32[]{:S(2)}) collective-permute-start(f32[8,128]{1,0:T(8,128)S(1)} %add.34), channel_id=1, source_target_pairs={{16,80},{17,81},{18,82},{19,83},{20,84},{21,85},{22,86},{23,87},{2... | collective-permute-start | bytes 12296 | tf_op jit(solution)/shard_map/ppermute | solution.py:153
  82.8 9.0 %collective-permute-start.7 = (f32[8,128]{1,0:T(8,128)S(1)}, f32[8,128]{1,0:T(8,128)S(1)}, u32[]{:S(2)}, u32[]{:S(2)}) collective-permute-start(f32[8,128]{1,0:T(8,128)S(1)} %add.35), channel_id=1, source_target_pairs={{16,144},{17,145},{18,146},{19,147},{20,148},{21,149},{22,150},{23... | collective-permute-start | bytes 12296 | tf_op jit(solution)/shard_map/ppermute | solution.py:153
  91.8 2.1 %collective-permute-start.8 = (f32[8,128]{1,0:T(8,128)S(1)}, f32[8,128]{1,0:T(8,128)S(1)}, u32[]{:S(2)}, u32[]{:S(2)}) collective-permute-start(f32[8,128]{1,0:T(8,128)S(1)} %add.36), channel_id=1, source_target_pairs={{16,0},{17,1},{18,2},{19,3},{20,4},{21,5},{22,6},{23,7},{24,8},{25... | collective-permute-start | bytes 12296 | tf_op jit(solution)/shard_map/ppermute | solution.py:158

commit v4 on v3

v4 whole, which is shorter than its diff:
```python
import functools

import jax
import jax.numpy as jnp
from jax import lax
from jax.experimental import pallas as pl
from jax.experimental.pallas import tpu as pltpu
from jax.sharding import PartitionSpec as P

F32 = jnp.float32
BF16 = jnp.bfloat16
PARTS = 4
AXES = ("dp", "expert")


def slots_of(ids, cap):
    toks = ids.shape[1]
    labels = lax.broadcasted_iota(jnp.int32, (toks, toks), 0)
    lanes = lax.broadcasted_iota(jnp.int32, (toks, toks), 1)
    first = (labels == ids[0:1, :]).astype(F32)
    second = (labels == ids[1:2, :]).astype(F32)
    earlier = (labels < lanes).astype(F32).astype(BF16)
    first_rank = jnp.dot(first.astype(BF16), earlier, preferred_element_type=F32)
    second_rank = jnp.dot(second.astype(BF16), earlier, preferred_element_type=F32)
    first_count = jnp.sum(first, 1, keepdims=True)
    base = ids.astype(F32) * cap
    first_slot = base[0:1, :] + jnp.sum(first * first_rank, 0, keepdims=True)
    second_slot = base[1:2, :] + jnp.sum(second * (second_rank + first_count), 0, keepdims=True)
    return first_slot, second_slot, first, second


def pack_kernel(cap, ids_hbm, gates_hbm, tok_hbm, out_ref, stats_ref, ids_ref, gates_ref, tok_ref, sems):
    slots, toks = out_ref.shape[0], tok_ref.shape[0]
    rows = slots // PARTS
    ids_copy = pltpu.make_async_copy(ids_hbm, ids_ref, sems.at[0])
    gates_copy = pltpu.make_async_copy(gates_hbm, gates_ref, sems.at[1])
    tok_copy = pltpu.make_async_copy(tok_hbm, tok_ref, sems.at[2])
    ids_copy.start()
    gates_copy.start()
    tok_copy.start()
    ids_copy.wait()
    gates_copy.wait()

    gates = gates_ref[...]
    first_slot, second_slot, first, second = slots_of(ids_ref[...], cap)
    count = jnp.sum(first + second, 1, keepdims=True)
    mass = jnp.sum(first * gates[0:1, :] + second * gates[1:2, :], 1, keepdims=True)
    lanes = lax.broadcasted_iota(jnp.int32, (toks, toks), 1)
    stats_ref[...] = jnp.where(lanes == 0, count, jnp.where(lanes == 1, mass, 0.0)).T[:8, :]

    tok_copy.wait()
    tokens = tok_ref[...]
    first_slot, second_slot = first_slot.astype(jnp.int32), second_slot.astype(jnp.int32)
    for part in range(PARTS):
        slot = lax.broadcasted_iota(jnp.int32, (rows, toks), 0) + part * rows
        pick = ((slot == first_slot) | (slot == second_slot)).astype(F32).astype(BF16)
        out_ref[part * rows : (part + 1) * rows, :] = jnp.dot(
            pick, tokens, preferred_element_type=F32
        ).astype(BF16)


def pack(ids, gates, tokens, experts, cap):
    toks, width = tokens.shape
    slots = experts * cap
    return pl.pallas_call(
        functools.partial(pack_kernel, cap),
        in_specs=[pl.BlockSpec(memory_space=pltpu.HBM)] * 3,
        out_specs=[pl.BlockSpec(memory_space=pltpu.VMEM)] * 2,
        out_shape=[
            jax.ShapeDtypeStruct((slots, width), BF16),
            jax.ShapeDtypeStruct((8, toks), F32),
        ],
        scratch_shapes=[
            pltpu.VMEM(ids.shape, ids.dtype),
            pltpu.VMEM(gates.shape, gates.dtype),
            pltpu.VMEM(tokens.shape, tokens.dtype),
            pltpu.SemaphoreType.DMA((3,)),
        ],
        compiler_params=pltpu.CompilerParams(vmem_limit_bytes=16 * 2**20),
        cost_estimate=pl.CostEstimate(
            flops=2 * slots * toks * width, bytes_accessed=4 * slots * width, transcendentals=0
        ),
        name="pack",
    )(*(pltpu.with_memory_space_constraint(a, pltpu.HBM) for a in (ids, gates, tokens)))


def hidden_kernel(x_ref, gate_ref, up_ref, out_ref):
    x = x_ref[...]
    for start in range(0, out_ref.shape[1], 256):
        tile = slice(start, start + 256)
        gate = jnp.dot(x, gate_ref[0, :, tile], preferred_element_type=F32)
        up = jnp.dot(x, up_ref[0, :, tile], preferred_element_type=F32)
        out_ref[:, tile] = (gate / (1.0 + jnp.exp(-gate)) * up).astype(BF16)


def hidden_of(x, w_gate, w_up):
    rows, width = x.shape
    middle = w_gate.shape[2]
    held = pl.BlockSpec(memory_space=pltpu.VMEM)
    return pl.pallas_call(
        hidden_kernel,
        in_specs=[held] * 3,
        out_specs=held,
        out_shape=jax.ShapeDtypeStruct((rows, middle), BF16),
        compiler_params=pltpu.CompilerParams(vmem_limit_bytes=16 * 2**20),
        cost_estimate=pl.CostEstimate(
            flops=4 * rows * width * middle,
            bytes_accessed=2 * rows * width + 4 * width * middle,
            transcendentals=rows * middle,
        ),
        name="hidden",
    )(x, w_gate, w_up)


def down_kernel(x_ref, down_ref, out_hbm, out_ref, sems):
    copies = []
    for part in range(sems.shape[0]):
        tile = pl.ds(part * 256, 256)
        out_ref[tile, :] = jnp.dot(
            x_ref[tile, :], down_ref[0], preferred_element_type=F32
        ).astype(BF16)
        copies.append(pltpu.make_async_copy(out_ref.at[tile], out_hbm.at[tile], sems.at[part]))
        copies[-1].start()
    for copy in copies:
        copy.wait()


def down_of(x, w_down):
    rows, middle = x.shape
    width = w_down.shape[2]
    held = pl.BlockSpec(memory_space=pltpu.VMEM)
    return pl.pallas_call(
        down_kernel,
        in_specs=[held] * 2,
        out_specs=pl.BlockSpec(memory_space=pltpu.HBM),
        out_shape=pltpu.HBM((rows, width), BF16),
        scratch_shapes=[pltpu.VMEM((rows, width), BF16), pltpu.SemaphoreType.DMA((rows // 256,))],
        compiler_params=pltpu.CompilerParams(vmem_limit_bytes=16 * 2**20),
        cost_estimate=pl.CostEstimate(
            flops=2 * rows * width * middle,
            bytes_accessed=2 * rows * width + 2 * width * middle,
            transcendentals=0,
        ),
        name="down",
    )(x, w_down)


def select_kernel(cap, ids_ref, pick_ref):
    toks, slots = ids_ref.shape[1], pick_ref.shape[1]
    first_slot, second_slot, _, _ = slots_of(ids_ref[...], cap)
    labels = lax.broadcasted_iota(jnp.int32, (toks, toks), 0)
    lines = jnp.where(labels == 0, first_slot, jnp.where(labels == 1, second_slot, 0.0)).T
    dest = lines[:, 0:2].astype(jnp.int32)
    lane = lax.broadcasted_iota(jnp.int32, (toks, slots), 1)
    pick_ref[:toks, :] = (lane == dest[:, 0:1]).astype(F32).astype(BF16)
    pick_ref[toks:, :] = (lane == dest[:, 1:2]).astype(F32).astype(BF16)


def select(ids, slots, cap):
    toks = ids.shape[1]
    held = pl.BlockSpec(memory_space=pltpu.VMEM)
    return pl.pallas_call(
        functools.partial(select_kernel, cap),
        in_specs=[held],
        out_specs=held,
        out_shape=jax.ShapeDtypeStruct((2 * toks, slots), BF16),
        compiler_params=pltpu.CompilerParams(vmem_limit_bytes=4 * 2**20),
        cost_estimate=pl.CostEstimate(flops=0, bytes_accessed=4 * toks * slots, transcendentals=0),
        name="select",
    )(ids)


def combine_kernel(pick_ref, gates_ref, rows_ref, out_hbm, out_ref, sems):
    toks, width = out_ref.shape
    gates = gates_ref[...]
    labels = lax.broadcasted_iota(jnp.int32, (toks, toks), 0)
    lines = jnp.where(labels == 0, gates[0:1, :], jnp.where(labels == 1, gates[1:2, :], 0.0)).T
    first, second = lines[:, 0:1], lines[:, 1:2]
    block = width // PARTS
    copies = []
    for part in range(PARTS):
        tile = pl.ds(part * block, block)
        both = jnp.dot(pick_ref[...], rows_ref[:, tile], preferred_element_type=F32)
        out_ref[:, tile] = (first * both[:toks] + second * both[toks:]).astype(BF16)
        copies.append(
            pltpu.make_async_copy(out_ref.at[:, tile], out_hbm.at[:, tile], sems.at[part])
        )
        copies[-1].start()
    for copy in copies:
        copy.wait()


def combine(pick, gates, rows):
    toks = gates.shape[1]
    slots, width = rows.shape
    held = pl.BlockSpec(memory_space=pltpu.VMEM)
    return pl.pallas_call(
        combine_kernel,
        in_specs=[held] * 3,
        out_specs=pl.BlockSpec(memory_space=pltpu.HBM),
        out_shape=pltpu.HBM((toks, width), BF16),
        scratch_shapes=[pltpu.VMEM((toks, width), BF16), pltpu.SemaphoreType.DMA((PARTS,))],
        compiler_params=pltpu.CompilerParams(vmem_limit_bytes=16 * 2**20),
        cost_estimate=pl.CostEstimate(
            flops=4 * toks * slots * width, bytes_accessed=2 * slots * width, transcendentals=0
        ),
        name="combine",
    )(pick, gates, rows)


def add_round(value, size, flip, step):
    return value + lax.ppermute(value, AXES, [(i, i ^ flip) for i in range(size) if (i // step) % 2 == 1])


def hand_over(value, size, step, sender):
    turn = step if sender == 0 else -step
    return lax.ppermute(value, AXES, [(i, i + turn) for i in range(size) if (i // step) % 2 == sender])


def on_device(tokens, expert_ids, gate_weights, w_gate, w_up, w_down):
    toks, width = tokens.shape
    picks = expert_ids.shape[1]
    group = lax.axis_size("expert")
    copies = lax.axis_size("dp")
    experts = w_gate.shape[0] * group
    cap = min(toks * picks // 4, 3 * toks * picks // experts)
    all_tokens = toks * group * copies

    size = copies * group
    stride = 2 * group
    ids, gates = expert_ids.T, gate_weights.T
    outgoing, stats = pack(ids, gates, tokens, experts, cap)
    stats = stats + hand_over(stats, size, group, 0)
    late = lax.axis_index("dp") % 2 == 1

    def plane_sum(value):
        for flip in (1, 3, 4, 12):
            value = add_round(value, size, flip, group)
        return value

    stats = lax.cond(late, plane_sum, lambda value: value, stats)
    stats, outgoing = lax.optimization_barrier((stats, outgoing))
    received = lax.all_to_all(outgoing, "expert", split_axis=0, concat_axis=0, tiled=True)
    result = down_of(hidden_of(received, w_gate, w_up), w_down)
    stats, result, ids, gates = lax.optimization_barrier((stats, result, ids, gates))
    returned = lax.all_to_all(result, "expert", split_axis=0, concat_axis=0, tiled=True)
    pick = select(ids, experts * cap, cap)
    for flip in (1, 2, 7):
        stats = add_round(stats, size, flip * stride, group)
    stats = jnp.where(late, stats, hand_over(stats, size, group, 1))
    load, mass = stats[0, :experts], stats[1, :experts]
    aux_loss = experts * jnp.sum(load / (all_tokens * picks) * (mass / all_tokens))
    return combine(pick, gates, returned), aux_loss


def solution(mesh):
    rows = P(("dp", "expert"), None)
    held = P("expert", None, None)
    return jax.shard_map(
        on_device,
        mesh=mesh,
        in_specs=(rows, rows, rows, held, held, held),
        out_specs=(rows, P()),
        check_vma=False,
    )
```

time: 102 us -> 97.4 us (0.955)
  local copies, waits for them, and re-layouts: 1.9 us -> 0.02 us
  starting transfers between devices: 33.4 us -> 31.8 us
    unnamed x6 -> x10, local copies, waits for them, and re-layouts: 1.9 us -> 0.02 us
    ppermute x7, starting transfers between devices: 27.1 us -> 25.4 us  [add_round(): lax.ppermute(value, AXES, [(i, i ^ flip) for i in range(size) if i // ste...]
    all_to_all x1, waiting for transfers between devices: 1.38 us -> 2.79 us  [on_device(): lax.all_to_all(result, 'expert', split_axis=0, concat_axis=0, tiled=True)]
    pallas_call x2 -> x4, Pallas kernels: 11.6 us -> 10.7 us  [the longest x1 5.05 us: hidden_of(): pl.pallas_call(hidden_kernel, in_specs=[held] * 3, out_specs=held, out_sh...]
where the time goes in v4:
time: 97.4 us; the launch traced here: 96.8 us
  starting transfers between devices  31.8 us (33%)
  blocking collectives  28.3 us (29%)
  waiting for transfers between devices  20.7 us (21%)
  Pallas kernels  12.8 us (13%)
  between operations  2.55 us (3%)
    all_to_all x1, blocking collectives, on_device(): lax.all_to_all(outgoing, 'expert', split_axis=0, concat_axis=0, tiled=True)  28.3 us
    ppermute x7, starting transfers between devices, add_round(): lax.ppermute(value, AXES, [(i, i ^ flip) for i in range(size) if i // ste...  25.4 us
    ppermute x7, waiting for transfers between devices, add_round(): lax.ppermute(value, AXES, [(i, i ^ flip) for i in range(size) if i // ste...  13.6 us
    pallas_call x1, Pallas kernels, hidden_of(): pl.pallas_call(hidden_kernel, in_specs=[held] * 3, out_specs=held, out_sh...  5.05 us
    ppermute x2, waiting for transfers between devices, hand_over(): lax.ppermute(value, AXES, [(i, i + turn) for i in range(size) if i // ste...  4.26 us
    all_to_all x1, starting transfers between devices, on_device(): lax.all_to_all(result, 'expert', split_axis=0, concat_axis=0, tiled=True)  3.75 us
    pallas_call x1, Pallas kernels, down_of(): pl.pallas_call(down_kernel, in_specs=[held] * 2, out_specs=pl.BlockSpec(m...  3.61 us
    all_to_all x1, waiting for transfers between devices, on_device(): lax.all_to_all(result, 'expert', split_axis=0, concat_axis=0, tiled=True)  2.79 us
  transfers between devices with their start and end apart: 10, of which 10 were waited for; matrix products, arithmetic and copies ran while one was open for 1% of the time, Pallas kernels for 0%

profile of v4, /device:TPU:1, one launch (start us, length us, event | category | flops | bytes accessed | tf_op | source)
XLA Modules:
  0.0 96.8 jit_solution(12060171447650129035)
XLA Ops:
  0.6 2.1 %pack.1 = (bf16[768,2048]{1,0:T(8,128)(2,1)S(1)}, f32[8,128]{1,0:T(8,128)S(1)}) custom-call(s32[2,128]{1,0:T(2,128)} %bitcast.9, f32[2,128]{1,0:T(2,128)} %bitcast.11, bf16[128,2048]{1,0:T(8,128)(2,1)} %tok_hbm.1), custom_call_target="tpu_custom_call" | custom-call | flops 402653184 | bytes 6291456 | tf_op jit(solution)/shard_map/pack/pallas_call | solution.py:65
  2.7 1.3 %collective-permute-start.4 = (f32[8,128]{1,0:T(8,128)S(1)}, f32[8,128]{1,0:T(8,128)S(1)}, u32[]{:S(2)}, u32[]{:S(2)}) collective-permute-start(f32[8,128]{1,0:T(8,128)S(1)} %get-tuple-element.15), channel_id=1, source_target_pairs={{0,16},{1,17},{2,18},{3,19},{4,20},{5,21},{6,22},{7,23},{8,24},{9,... | collective-permute-start | bytes 12296 | tf_op jit(solution)/shard_map/ppermute | solution.py:217
  4.0 3.9 %collective-permute-done.4 = f32[8,128]{1,0:T(8,128)S(1)} collective-permute-done((f32[8,128]{1,0:T(8,128)S(1)}, f32[8,128]{1,0:T(8,128)S(1)}, u32[]{:S(2)}, u32[]{:S(2)}) %collective-permute-start.4) | collective-permute-done | bytes 4128 | tf_op jit(solution)/shard_map/ppermute | solution.py:217
  7.9 20.8 %conditional.1 = (f32[8,128]{1,0:T(8,128)S(1)}) conditional(s32[]{:T(128)} %convert_element_type.3, f32[8,128]{1,0:T(8,128)S(1)} %add.35, f32[8,128]{1,0:T(8,128)S(1)} %add.35), branch_computations={%region_0.1_spmd, %region_1.2_spmd} | conditional | flops 4096 | bytes 114856 | solution.py:241
  7.9 1.9 %collective-permute-start = (f32[8,128]{1,0:T(8,128)S(1)}, f32[8,128]{1,0:T(8,128)S(1)}, u32[]{:S(2)}, u32[]{:S(2)}) collective-permute-start(f32[8,128]{1,0:T(8,128)S(1)} %param.1), channel_id=1, source_target_pairs={{16,17},{17,16},{18,19},{19,18},{20,21},{21,20},{22,23},{23,22},{2... | collective-permute-start | bytes 12296 | tf_op jit(solution)/shard_map/cond/branch_1_fun/ppermute | solution.py:212
  9.8 2.4 %collective-permute-done = f32[8,128]{1,0:T(8,128)S(1)} collective-permute-done((f32[8,128]{1,0:T(8,128)S(1)}, f32[8,128]{1,0:T(8,128)S(1)}, u32[]{:S(2)}, u32[]{:S(2)}) %collective-permute-start) | collective-permute-done | bytes 4128 | tf_op jit(solution)/shard_map/cond/branch_1_fun/ppermute | solution.py:212
  12.2 3.3 %collective-permute-start.1 = (f32[8,128]{1,0:T(8,128)S(1)}, f32[8,128]{1,0:T(8,128)S(1)}, u32[]{:S(2)}, u32[]{:S(2)}) collective-permute-start(f32[8,128]{1,0:T(8,128)S(1)} %add.25), channel_id=1, source_target_pairs={{16,19},{17,18},{18,17},{19,16},{20,23},{21,22},{22,21},{23,20},{2... | collective-permute-start | bytes 12296 | tf_op jit(solution)/shard_map/cond/branch_1_fun/ppermute | solution.py:212
  15.6 2.2 %collective-permute-done.1 = f32[8,128]{1,0:T(8,128)S(1)} collective-permute-done((f32[8,128]{1,0:T(8,128)S(1)}, f32[8,128]{1,0:T(8,128)S(1)}, u32[]{:S(2)}, u32[]{:S(2)}) %collective-permute-start.1) | collective-permute-done | bytes 4128 | tf_op jit(solution)/shard_map/cond/branch_1_fun/ppermute | solution.py:212
  17.8 1.9 %collective-permute-start.2 = (f32[8,128]{1,0:T(8,128)S(1)}, f32[8,128]{1,0:T(8,128)S(1)}, u32[]{:S(2)}, u32[]{:S(2)}) collective-permute-start(f32[8,128]{1,0:T(8,128)S(1)} %add.26), channel_id=1, source_target_pairs={{16,20},{17,21},{18,22},{19,23},{20,16},{21,17},{22,18},{23,19},{2... | collective-permute-start | bytes 12296 | tf_op jit(solution)/shard_map/cond/branch_1_fun/ppermute | solution.py:212
  19.7 2.8 %collective-permute-done.2 = f32[8,128]{1,0:T(8,128)S(1)} collective-permute-done((f32[8,128]{1,0:T(8,128)S(1)}, f32[8,128]{1,0:T(8,128)S(1)}, u32[]{:S(2)}, u32[]{:S(2)}) %collective-permute-start.2) | collective-permute-done | bytes 4128 | tf_op jit(solution)/shard_map/cond/branch_1_fun/ppermute | solution.py:212
  22.5 3.2 %collective-permute-start.3 = (f32[8,128]{1,0:T(8,128)S(1)}, f32[8,128]{1,0:T(8,128)S(1)}, u32[]{:S(2)}, u32[]{:S(2)}) collective-permute-start(f32[8,128]{1,0:T(8,128)S(1)} %add.27), channel_id=1, source_target_pairs={{16,28},{17,29},{18,30},{19,31},{20,24},{21,25},{22,26},{23,27},{2... | collective-permute-start | bytes 12296 | tf_op jit(solution)/shard_map/cond/branch_1_fun/ppermute | solution.py:212
  25.7 3.0 %collective-permute-done.3 = f32[8,128]{1,0:T(8,128)S(1)} collective-permute-done((f32[8,128]{1,0:T(8,128)S(1)}, f32[8,128]{1,0:T(8,128)S(1)}, u32[]{:S(2)}, u32[]{:S(2)}) %collective-permute-start.3) | collective-permute-done | bytes 4128 | tf_op jit(solution)/shard_map/cond/branch_1_fun/ppermute | solution.py:212
  28.7 0.0 copy-start.2
  28.7 0.0 copy-start.3
  28.7 28.3 %all_to_all.22 = bf16[16,48,2048]{2,1,0:T(8,128)(2,1)S(1)} all-to-all(bf16[16,48,2048]{2,1,0:T(8,128)(2,1)S(1)} %bitcast.7), channel_id=1, replica_groups=mesh['dp'=16,'expert'=16] {'expert'}, dimensions={0} | all-to-all | bytes 6291456 | tf_op jit(solution)/shard_map/all_to_all | solution.py:243
  56.9 0.0 copy-done.2
  56.9 0.0 copy-done.3
  56.9 0.0 copy-start.4
  56.9 5.1 %hidden.1.x_ref = bf16[768,768]{1,0:T(8,128)(2,1)S(1)} custom-call(bf16[768,2048]{1,0:T(8,128)(2,1)S(1)} %bitcast.8, bf16[1,2048,768]{2,1,0:T(8,128)(2,1)S(1)} %copy-done.2, bf16[1,2048,768]{2,1,0:T(8,128)(2,1)S(1)} %copy-done.3), custom_call_target="tpu_custom_call" | custom-call | flops 4831838208 | bytes 9437184 | tf_op jit(solution)/shard_map/hidden/pallas_call | solution.py:100
  62.0 0.0 copy-done.4
  62.0 3.6 %down.1 = bf16[768,2048]{1,0:T(8,128)(2,1)} custom-call(bf16[768,768]{1,0:T(8,128)(2,1)S(1)} %hidden.1.x_ref, bf16[1,768,2048]{2,1,0:T(8,128)(2,1)S(1)} %copy-done.4), custom_call_target="tpu_custom_call" | custom-call | flops 2415919104 | bytes 6291456 | tf_op jit(solution)/shard_map/down/pallas_call | solution.py:132
  65.6 0.0 copy-start
  65.6 0.0 copy-start.1
  65.7 3.8 %all-to-all-start.1 = ((bf16[16,48,2048]{2,1,0:T(8,128)(2,1)}), bf16[16,48,2048]{2,1,0:T(8,128)(2,1)S(1)}, u32[]{:S(2)}, u32[]{:S(2)}) async-start(bf16[16,48,2048]{2,1,0:T(8,128)(2,1)} %bitcast.13), calls=%async_computation.1 | async-start | bytes 6291456 | tf_op jit(solution)/shard_map/all_to_all | solution.py:246
  69.4 3.5 %collective-permute-start.5 = (f32[8,128]{1,0:T(8,128)S(1)}, f32[8,128]{1,0:T(8,128)S(1)}, u32[]{:S(2)}, u32[]{:S(2)}) collective-permute-start(f32[8,128]{1,0:T(8,128)S(1)} %get-tuple-element.23), channel_id=1, source_target_pairs={{16,48},{17,49},{18,50},{19,51},{20,52},{21,53},{22,54},{23,55},{2... | collective-permute-start | bytes 12296 | tf_op jit(solution)/shard_map/ppermute | solution.py:212
  73.0 1.3 %collective-permute-done.5 = f32[8,128]{1,0:T(8,128)S(1)} collective-permute-done((f32[8,128]{1,0:T(8,128)S(1)}, f32[8,128]{1,0:T(8,128)S(1)}, u32[]{:S(2)}, u32[]{:S(2)}) %collective-permute-start.5) | collective-permute-done | bytes 4128 | tf_op jit(solution)/shard_map/ppermute | solution.py:212
  74.2 4.9 %collective-permute-start.6 = (f32[8,128]{1,0:T(8,128)S(1)}, f32[8,128]{1,0:T(8,128)S(1)}, u32[]{:S(2)}, u32[]{:S(2)}) collective-permute-start(f32[8,128]{1,0:T(8,128)S(1)} %add.36), channel_id=1, source_target_pairs={{16,80},{17,81},{18,82},{19,83},{20,84},{21,85},{22,86},{23,87},{2... | collective-permute-start | bytes 12296 | tf_op jit(solution)/shard_map/ppermute | solution.py:212
  79.1 1.0 %collective-permute-done.6 = f32[8,128]{1,0:T(8,128)S(1)} collective-permute-done((f32[8,128]{1,0:T(8,128)S(1)}, f32[8,128]{1,0:T(8,128)S(1)}, u32[]{:S(2)}, u32[]{:S(2)}) %collective-permute-start.6) | collective-permute-done | bytes 4128 | tf_op jit(solution)/shard_map/ppermute | solution.py:212
  80.1 6.7 %collective-permute-start.7 = (f32[8,128]{1,0:T(8,128)S(1)}, f32[8,128]{1,0:T(8,128)S(1)}, u32[]{:S(2)}, u32[]{:S(2)}) collective-permute-start(f32[8,128]{1,0:T(8,128)S(1)} %add.37), channel_id=1, source_target_pairs={{16,240},{17,241},{18,242},{19,243},{20,244},{21,245},{22,246},{23... | collective-permute-start | bytes 12296 | tf_op jit(solution)/shard_map/ppermute | solution.py:212
  86.8 1.0 %collective-permute-done.7 = f32[8,128]{1,0:T(8,128)S(1)} collective-permute-done((f32[8,128]{1,0:T(8,128)S(1)}, f32[8,128]{1,0:T(8,128)S(1)}, u32[]{:S(2)}, u32[]{:S(2)}) %collective-permute-start.7) | collective-permute-done | bytes 4128 | tf_op jit(solution)/shard_map/ppermute | solution.py:212
  87.8 1.3 %collective-permute-start.8 = (f32[8,128]{1,0:T(8,128)S(1)}, f32[8,128]{1,0:T(8,128)S(1)}, u32[]{:S(2)}, u32[]{:S(2)}) collective-permute-start(f32[8,128]{1,0:T(8,128)S(1)} %add.38), channel_id=1, source_target_pairs={{16,0},{17,1},{18,2},{19,3},{20,4},{21,5},{22,6},{23,7},{24,8},{25... | collective-permute-start | bytes 12296 | tf_op jit(solution)/shard_map/ppermute | solution.py:217
  89.1 0.0 copy-done
  89.1 0.4 select.3.pick_ref
  89.5 0.4 collective-permute-done.8
  89.9 0.6 multiply_reduce_fusion
  91.1 2.8 %all-to-all-done.1 = bf16[16,48,2048]{2,1,0:T(8,128)(2,1)S(1)} async-done(((bf16[16,48,2048]{2,1,0:T(8,128)(2,1)}), bf16[16,48,2048]{2,1,0:T(8,128)(2,1)S(1)}, u32[]{:S(2)}, u32[]{:S(2)}) %all-to-all-start.1) | async-done | bytes 3145760 | tf_op jit(solution)/shard_map/all_to_all | solution.py:246
  93.9 0.0 copy-done.1
  93.9 1.7 %combine.1 = bf16[128,2048]{1,0:T(8,128)(2,1)} custom-call(bf16[256,768]{1,0:T(8,128)(2,1)S(1)} %select.3.pick_ref, f32[2,128]{1,0:T(2,128)S(1)} %bitcast.12, bf16[768,2048]{1,0:T(8,128)(2,1)S(1)} %bitcast.6), custom_call_target="tpu_custom_call" | custom-call | flops 805306368 | bytes 3145728 | tf_op jit(solution)/shard_map/combine/pallas_call | solution.py:197
  (9 shorter events, 0.0 us)
Async XLA Ops:
  2.7 5.2 %collective-permute-start.4 = (f32[8,128]{1,0:T(8,128)S(1)}, f32[8,128]{1,0:T(8,128)S(1)}, u32[]{:S(2)}, u32[]{:S(2)}) collective-permute-start(f32[8,128]{1,0:T(8,128)S(1)} %get-tuple-element.15), channel_id=1, source_target_pairs={{0,16},{1,17},{2,18},{3,19},{4,20},{5,21},{6,22},{7,23},{8,24},{9,... | collective-permute-start | bytes 12296 | tf_op jit(solution)/shard_map/ppermute | solution.py:217
  7.9 4.3 %collective-permute-start = (f32[8,128]{1,0:T(8,128)S(1)}, f32[8,128]{1,0:T(8,128)S(1)}, u32[]{:S(2)}, u32[]{:S(2)}) collective-permute-start(f32[8,128]{1,0:T(8,128)S(1)} %param.1), channel_id=1, source_target_pairs={{16,17},{17,16},{18,19},{19,18},{20,21},{21,20},{22,23},{23,22},{2... | collective-permute-start | bytes 12296 | tf_op jit(solution)/shard_map/cond/branch_1_fun/ppermute | solution.py:212
  12.2 5.6 %collective-permute-start.1 = (f32[8,128]{1,0:T(8,128)S(1)}, f32[8,128]{1,0:T(8,128)S(1)}, u32[]{:S(2)}, u32[]{:S(2)}) collective-permute-start(f32[8,128]{1,0:T(8,128)S(1)} %add.25), channel_id=1, source_target_pairs={{16,19},{17,18},{18,17},{19,16},{20,23},{21,22},{22,21},{23,20},{2... | collective-permute-start | bytes 12296 | tf_op jit(solution)/shard_map/cond/branch_1_fun/ppermute | solution.py:212
  17.8 4.7 %collective-permute-start.2 = (f32[8,128]{1,0:T(8,128)S(1)}, f32[8,128]{1,0:T(8,128)S(1)}, u32[]{:S(2)}, u32[]{:S(2)}) collective-permute-start(f32[8,128]{1,0:T(8,128)S(1)} %add.26), channel_id=1, source_target_pairs={{16,20},{17,21},{18,22},{19,23},{20,16},{21,17},{22,18},{23,19},{2... | collective-permute-start | bytes 12296 | tf_op jit(solution)/shard_map/cond/branch_1_fun/ppermute | solution.py:212
  22.5 6.1 %collective-permute-start.3 = (f32[8,128]{1,0:T(8,128)S(1)}, f32[8,128]{1,0:T(8,128)S(1)}, u32[]{:S(2)}, u32[]{:S(2)}) collective-permute-start(f32[8,128]{1,0:T(8,128)S(1)} %add.27), channel_id=1, source_target_pairs={{16,28},{17,29},{18,30},{19,31},{20,24},{21,25},{22,26},{23,27},{2... | collective-permute-start | bytes 12296 | tf_op jit(solution)/shard_map/cond/branch_1_fun/ppermute | solution.py:212
  28.7 28.3 %copy-start.2 = (bf16[1,2048,768]{2,1,0:T(8,128)(2,1)S(1)}, bf16[1,2048,768]{2,1,0:T(8,128)(2,1)}, u32[]{:S(2)}) copy-start(bf16[1,2048,768]{2,1,0:T(8,128)(2,1)} %gate_ref.1) | copy-start | bytes 9437188
  28.7 28.3 %copy-start.3 = (bf16[1,2048,768]{2,1,0:T(8,128)(2,1)S(1)}, bf16[1,2048,768]{2,1,0:T(8,128)(2,1)}, u32[]{:S(2)}) copy-start(bf16[1,2048,768]{2,1,0:T(8,128)(2,1)} %up_ref.1) | copy-start | bytes 9437188
  56.9 5.1 %copy-start.4 = (bf16[1,768,2048]{2,1,0:T(8,128)(2,1)S(1)}, bf16[1,768,2048]{2,1,0:T(8,128)(2,1)}, u32[]{:S(2)}) copy-start(bf16[1,768,2048]{2,1,0:T(8,128)(2,1)} %down_ref.1) | copy-start | bytes 9437188
  65.6 23.4 %copy-start = (s32[128,2]{0,1:T(2,128)S(1)}, s32[128,2]{0,1:T(2,128)}, u32[]{:S(2)}) copy-start(s32[128,2]{0,1:T(2,128)} %param.9) | copy-start | bytes 3076
  65.6 28.3 %copy-start.1 = (f32[128,2]{0,1:T(2,128)S(1)}, f32[128,2]{0,1:T(2,128)}, u32[]{:S(2)}) copy-start(f32[128,2]{0,1:T(2,128)} %param.10) | copy-start | bytes 3076
  65.7 28.3 %all-to-all-start.1 = ((bf16[16,48,2048]{2,1,0:T(8,128)(2,1)}), bf16[16,48,2048]{2,1,0:T(8,128)(2,1)S(1)}, u32[]{:S(2)}, u32[]{:S(2)}) async-start(bf16[16,48,2048]{2,1,0:T(8,128)(2,1)} %bitcast.13), calls=%async_computation.1 | async-start | bytes 6291456 | tf_op jit(solution)/shard_map/all_to_all | solution.py:246
  69.4 4.8 %collective-permute-start.5 = (f32[8,128]{1,0:T(8,128)S(1)}, f32[8,128]{1,0:T(8,128)S(1)}, u32[]{:S(2)}, u32[]{:S(2)}) collective-permute-start(f32[8,128]{1,0:T(8,128)S(1)} %get-tuple-element.23), channel_id=1, source_target_pairs={{16,48},{17,49},{18,50},{19,51},{20,52},{21,53},{22,54},{23,55},{2... | collective-permute-start | bytes 12296 | tf_op jit(solution)/shard_map/ppermute | solution.py:212
  74.2 5.9 %collective-permute-start.6 = (f32[8,128]{1,0:T(8,128)S(1)}, f32[8,128]{1,0:T(8,128)S(1)}, u32[]{:S(2)}, u32[]{:S(2)}) collective-permute-start(f32[8,128]{1,0:T(8,128)S(1)} %add.36), channel_id=1, source_target_pairs={{16,80},{17,81},{18,82},{19,83},{20,84},{21,85},{22,86},{23,87},{2... | collective-permute-start | bytes 12296 | tf_op jit(solution)/shard_map/ppermute | solution.py:212
  80.1 7.7 %collective-permute-start.7 = (f32[8,128]{1,0:T(8,128)S(1)}, f32[8,128]{1,0:T(8,128)S(1)}, u32[]{:S(2)}, u32[]{:S(2)}) collective-permute-start(f32[8,128]{1,0:T(8,128)S(1)} %add.37), channel_id=1, source_target_pairs={{16,240},{17,241},{18,242},{19,243},{20,244},{21,245},{22,246},{23... | collective-permute-start | bytes 12296 | tf_op jit(solution)/shard_map/ppermute | solution.py:212
  87.8 2.1 %collective-permute-start.8 = (f32[8,128]{1,0:T(8,128)S(1)}, f32[8,128]{1,0:T(8,128)S(1)}, u32[]{:S(2)}, u32[]{:S(2)}) collective-permute-start(f32[8,128]{1,0:T(8,128)S(1)} %add.38), channel_id=1, source_target_pairs={{16,0},{17,1},{18,2},{19,3},{20,4},{21,5},{22,6},{23,7},{24,8},{25... | collective-permute-start | bytes 12296 | tf_op jit(solution)/shard_map/ppermute | solution.py:217

commit v5 on v4

--- a/solution.py
+++ b/solution.py
@@ -29,9 +29,10 @@
     return first_slot, second_slot, first, second
 
 
-def pack_kernel(cap, ids_hbm, gates_hbm, tok_hbm, out_ref, stats_ref, ids_ref, gates_ref, tok_ref, sems):
-    slots, toks = out_ref.shape[0], tok_ref.shape[0]
-    rows = slots // PARTS
+def count_kernel(
+    cap, ids_hbm, gates_hbm, tok_hbm, slot_ref, stats_ref, tok_ref, ids_ref, gates_ref, sems
+):
+    toks = ids_ref.shape[1]
     ids_copy = pltpu.make_async_copy(ids_hbm, ids_ref, sems.at[0])
     gates_copy = pltpu.make_async_copy(gates_hbm, gates_ref, sems.at[1])
     tok_copy = pltpu.make_async_copy(tok_hbm, tok_ref, sems.at[2])
@@ -39,18 +40,45 @@
     gates_copy.start()
     tok_copy.start()
     ids_copy.wait()
+    first_slot, second_slot, first, second = slots_of(ids_ref[...], cap)
+    slot_ref[0:1, :] = first_slot.astype(jnp.int32)
+    slot_ref[1:2, :] = second_slot.astype(jnp.int32)
+    count = jnp.sum(first + second, 1, keepdims=True)
     gates_copy.wait()
-
     gates = gates_ref[...]
-    first_slot, second_slot, first, second = slots_of(ids_ref[...], cap)
-    count = jnp.sum(first + second, 1, keepdims=True)
     mass = jnp.sum(first * gates[0:1, :] + second * gates[1:2, :], 1, keepdims=True)
     lanes = lax.broadcasted_iota(jnp.int32, (toks, toks), 1)
     stats_ref[...] = jnp.where(lanes == 0, count, jnp.where(lanes == 1, mass, 0.0)).T[:8, :]
-
     tok_copy.wait()
+
+
+def count(ids, gates, tokens, cap):
+    toks = ids.shape[1]
+    return pl.pallas_call(
+        functools.partial(count_kernel, cap),
+        in_specs=[pl.BlockSpec(memory_space=pltpu.HBM)] * 3,
+        out_specs=[pl.BlockSpec(memory_space=pltpu.VMEM)] * 3,
+        out_shape=[
+            jax.ShapeDtypeStruct((8, toks), jnp.int32),
+            jax.ShapeDtypeStruct((8, toks), F32),
+            jax.ShapeDtypeStruct(tokens.shape, tokens.dtype),
+        ],
+        scratch_shapes=[
+            pltpu.VMEM(ids.shape, ids.dtype),
+            pltpu.VMEM(gates.shape, gates.dtype),
+            pltpu.SemaphoreType.DMA((3,)),
+        ],
+        compiler_params=pltpu.CompilerParams(vmem_limit_bytes=4 * 2**20),
+        cost_estimate=pl.CostEstimate(flops=4 * toks**3, bytes_accessed=8 * toks, transcendentals=0),
+        name="count",
+    )(*(pltpu.with_memory_space_constraint(a, pltpu.HBM) for a in (ids, gates, tokens)))
+
+
+def pack_kernel(slot_ref, tok_ref, out_ref):
+    toks = tok_ref.shape[0]
+    rows = out_ref.shape[0] // PARTS
     tokens = tok_ref[...]
-    first_slot, second_slot = first_slot.astype(jnp.int32), second_slot.astype(jnp.int32)
+    first_slot, second_slot = slot_ref[0:1, :], slot_ref[1:2, :]
     for part in range(PARTS):
         slot = lax.broadcasted_iota(jnp.int32, (rows, toks), 0) + part * rows
         pick = ((slot == first_slot) | (slot == second_slot)).astype(F32).astype(BF16)
@@ -59,29 +87,20 @@
         ).astype(BF16)
 
 
-def pack(ids, gates, tokens, experts, cap):
+def pack(slots, tokens, count):
     toks, width = tokens.shape
-    slots = experts * cap
-    return pl.pallas_call(
-        functools.partial(pack_kernel, cap),
-        in_specs=[pl.BlockSpec(memory_space=pltpu.HBM)] * 3,
-        out_specs=[pl.BlockSpec(memory_space=pltpu.VMEM)] * 2,
-        out_shape=[
-            jax.ShapeDtypeStruct((slots, width), BF16),
-            jax.ShapeDtypeStruct((8, toks), F32),
-        ],
-        scratch_shapes=[
-            pltpu.VMEM(ids.shape, ids.dtype),
-            pltpu.VMEM(gates.shape, gates.dtype),
-            pltpu.VMEM(tokens.shape, tokens.dtype),
-            pltpu.SemaphoreType.DMA((3,)),
-        ],
-        compiler_params=pltpu.CompilerParams(vmem_limit_bytes=16 * 2**20),
-        cost_estimate=pl.CostEstimate(
-            flops=2 * slots * toks * width, bytes_accessed=4 * slots * width, transcendentals=0
+    held = pl.BlockSpec(memory_space=pltpu.VMEM)
+    return pl.pallas_call(
+        pack_kernel,
+        in_specs=[held] * 2,
+        out_specs=held,
+        out_shape=jax.ShapeDtypeStruct((count, width), BF16),
+        compiler_params=pltpu.CompilerParams(vmem_limit_bytes=8 * 2**20),
+        cost_estimate=pl.CostEstimate(
+            flops=2 * count * toks * width, bytes_accessed=4 * count * width, transcendentals=0
         ),
         name="pack",
-    )(*(pltpu.with_memory_space_constraint(a, pltpu.HBM) for a in (ids, gates, tokens)))
+    )(slots, tokens)
 
 
 def hidden_kernel(x_ref, gate_ref, up_ref, out_ref):
@@ -113,14 +132,17 @@
 
 
 def down_kernel(x_ref, down_ref, out_hbm, out_ref, sems):
+    rows = x_ref.shape[0]
     copies = []
-    for part in range(sems.shape[0]):
-        tile = pl.ds(part * 256, 256)
+    start = 0
+    for part, size in enumerate((rows // 2, rows // 3, rows // 6)):
+        tile = pl.ds(start, size)
         out_ref[tile, :] = jnp.dot(
             x_ref[tile, :], down_ref[0], preferred_element_type=F32
         ).astype(BF16)
         copies.append(pltpu.make_async_copy(out_ref.at[tile], out_hbm.at[tile], sems.at[part]))
         copies[-1].start()
+        start += size
     for copy in copies:
         copy.wait()
 
@@ -134,7 +156,7 @@
         in_specs=[held] * 2,
         out_specs=pl.BlockSpec(memory_space=pltpu.HBM),
         out_shape=pltpu.HBM((rows, width), BF16),
-        scratch_shapes=[pltpu.VMEM((rows, width), BF16), pltpu.SemaphoreType.DMA((rows // 256,))],
+        scratch_shapes=[pltpu.VMEM((rows, width), BF16), pltpu.SemaphoreType.DMA((3,))],
         compiler_params=pltpu.CompilerParams(vmem_limit_bytes=16 * 2**20),
         cost_estimate=pl.CostEstimate(
             flops=2 * rows * width * middle,
@@ -229,8 +251,10 @@
     size = copies * group
     stride = 2 * group
     ids, gates = expert_ids.T, gate_weights.T
-    outgoing, stats = pack(ids, gates, tokens, experts, cap)
-    stats = stats + hand_over(stats, size, group, 0)
+    slots, stats, tokens = count(ids, gates, tokens, cap)
+    swap = [(i, i + group if (i // group) % 2 == 0 else i - group) for i in range(size)]
+    stats = stats + lax.ppermute(stats, AXES, swap)
+    outgoing = pack(slots, tokens, experts * cap)
     late = lax.axis_index("dp") % 2 == 1
 
     def plane_sum(value):

time: 97.4 us -> 95 us (0.975)
  waiting for transfers between devices: 20.7 us -> 18.9 us
  blocking collectives: 28.3 us -> 26.9 us
    ppermute x2 -> x1, waiting for transfers between devices: 4.26 us -> 0.41 us  [hand_over(): lax.ppermute(value, AXES, [(i, i + turn) for i in range(size) if i // ste...]
    ppermute x0 -> x1, starting transfers between devices: none -> 3.33 us  [on_device(): stats = stats + lax.ppermute(stats, AXES, swap)]
    ppermute x7, waiting for transfers between devices: 13.6 us -> 15.7 us  [add_round(): lax.ppermute(value, AXES, [(i, i ^ flip) for i in range(size) if i // ste...]
    all_to_all x1, blocking collectives: 28.3 us -> 26.9 us  [on_device(): lax.all_to_all(outgoing, 'expert', split_axis=0, concat_axis=0, tiled=True)]
    ppermute x2 -> x1, starting transfers between devices: 2.57 us -> 1.28 us  [hand_over(): lax.ppermute(value, AXES, [(i, i + turn) for i in range(size) if i // ste...]
    ppermute x7, starting transfers between devices: 25.4 us -> 24.2 us  [add_round(): lax.ppermute(value, AXES, [(i, i ^ flip) for i in range(size) if i // ste...]
    pallas_call x1 -> x2, Pallas kernels: 2.08 us -> 2.06 us  [the longest x1 1.1 us: count(): pl.pallas_call(functools.partial(count_kernel, cap), in_specs=[pl.BlockSp...]
  transfers between devices with their start and end apart: 10 -> 10, of which waited for: 10 -> 9; matrix products, arithmetic and copies ran while one was open for 1% -> 1% of each run, Pallas kernels for 0% -> 1%
where the time goes in v5:
time: 95 us; the launch traced here: 94.4 us
  starting transfers between devices  32.6 us (34%)
  blocking collectives  26.9 us (28%)
  waiting for transfers between devices  18.9 us (20%)
  Pallas kernels  12.7 us (13%)
  between operations  2.56 us (3%)
    all_to_all x1, blocking collectives, on_device(): lax.all_to_all(outgoing, 'expert', split_axis=0, concat_axis=0, tiled=True)  26.9 us
    ppermute x7, starting transfers between devices, add_round(): lax.ppermute(value, AXES, [(i, i ^ flip) for i in range(size) if i // ste...  24.2 us
    ppermute x7, waiting for transfers between devices, add_round(): lax.ppermute(value, AXES, [(i, i ^ flip) for i in range(size) if i // ste...  15.7 us
    pallas_call x1, Pallas kernels, hidden_of(): pl.pallas_call(hidden_kernel, in_specs=[held] * 3, out_specs=held, out_sh...  5.05 us
    all_to_all x1, starting transfers between devices, on_device(): lax.all_to_all(result, 'expert', split_axis=0, concat_axis=0, tiled=True)  3.75 us
    pallas_call x1, Pallas kernels, down_of(): pl.pallas_call(down_kernel, in_specs=[held] * 2, out_specs=pl.BlockSpec(m...  3.45 us
    ppermute x1, starting transfers between devices, on_device(): stats = stats + lax.ppermute(stats, AXES, swap)  3.33 us
    all_to_all x1, waiting for transfers between devices, on_device(): lax.all_to_all(result, 'expert', split_axis=0, concat_axis=0, tiled=True)  2.8 us
  transfers between devices with their start and end apart: 10, of which 9 were waited for; matrix products, arithmetic and copies ran while one was open for 1% of the time, Pallas kernels for 1%

profile of v5, /device:TPU:1, one launch (start us, length us, event | category | flops | bytes accessed | tf_op | source)
XLA Modules:
  0.0 94.4 jit_solution(17426012005121300563)
XLA Ops:
  0.6 1.1 %count.1 = (s32[8,128]{1,0:T(8,128)S(1)}, f32[8,128]{1,0:T(8,128)S(1)}, bf16[128,2048]{1,0:T(8,128)(2,1)S(1)}) custom-call(s32[2,128]{1,0:T(2,128)} %bitcast.9, f32[2,128]{1,0:T(2,128)} %bitcast.11, bf16[128,2048]{1,0:T(8,128)(2,1)} %tok_hbm.1), custom_call_target="tpu_custom_call" | custom-call | flops 8388608 | bytes 1024 | tf_op jit(solution)/shard_map/count/pallas_call | solution.py:57
  1.7 3.3 %collective-permute-start.4 = (f32[8,128]{1,0:T(8,128)S(1)}, f32[8,128]{1,0:T(8,128)S(1)}, u32[]{:S(2)}, u32[]{:S(2)}) collective-permute-start(f32[8,128]{1,0:T(8,128)S(1)} %get-tuple-element.16), channel_id=1, source_target_pairs={{0,16},{1,17},{2,18},{3,19},{4,20},{5,21},{6,22},{7,23},{8,24},{9,... | collective-permute-start | bytes 12296 | tf_op jit(solution)/shard_map/ppermute | solution.py:256
  5.1 1.0 %pack.1 = bf16[768,2048]{1,0:T(8,128)(2,1)S(1)} custom-call(s32[8,128]{1,0:T(8,128)S(1)} %get-tuple-element.17.slot_ref, bf16[128,2048]{1,0:T(8,128)(2,1)S(1)} %get-tuple-element.18.tok_ref), custom_call_target="tpu_custom_call" | custom-call | flops 402653184 | bytes 6291456 | tf_op jit(solution)/shard_map/pack/pallas_call | solution.py:93
  6.0 0.0 collective-permute-done.4
  6.1 21.7 %conditional.1 = (f32[8,128]{1,0:T(8,128)S(1)}) conditional(s32[]{:T(128)} %convert_element_type.3, f32[8,128]{1,0:T(8,128)S(1)} %add.35, f32[8,128]{1,0:T(8,128)S(1)} %add.35), branch_computations={%region_0.1_spmd, %region_1.2_spmd} | conditional | flops 4096 | bytes 114856 | solution.py:265
  6.1 1.9 %collective-permute-start = (f32[8,128]{1,0:T(8,128)S(1)}, f32[8,128]{1,0:T(8,128)S(1)}, u32[]{:S(2)}, u32[]{:S(2)}) collective-permute-start(f32[8,128]{1,0:T(8,128)S(1)} %param.1), channel_id=1, source_target_pairs={{16,17},{17,16},{18,19},{19,18},{20,21},{21,20},{22,23},{23,22},{2... | collective-permute-start | bytes 12296 | tf_op jit(solution)/shard_map/cond/branch_1_fun/ppermute | solution.py:234
  8.0 2.4 %collective-permute-done = f32[8,128]{1,0:T(8,128)S(1)} collective-permute-done((f32[8,128]{1,0:T(8,128)S(1)}, f32[8,128]{1,0:T(8,128)S(1)}, u32[]{:S(2)}, u32[]{:S(2)}) %collective-permute-start) | collective-permute-done | bytes 4128 | tf_op jit(solution)/shard_map/cond/branch_1_fun/ppermute | solution.py:234
  10.4 2.9 %collective-permute-start.1 = (f32[8,128]{1,0:T(8,128)S(1)}, f32[8,128]{1,0:T(8,128)S(1)}, u32[]{:S(2)}, u32[]{:S(2)}) collective-permute-start(f32[8,128]{1,0:T(8,128)S(1)} %add.25), channel_id=1, source_target_pairs={{16,19},{17,18},{18,17},{19,16},{20,23},{21,22},{22,21},{23,20},{2... | collective-permute-start | bytes 12296 | tf_op jit(solution)/shard_map/cond/branch_1_fun/ppermute | solution.py:234
  13.4 3.0 %collective-permute-done.1 = f32[8,128]{1,0:T(8,128)S(1)} collective-permute-done((f32[8,128]{1,0:T(8,128)S(1)}, f32[8,128]{1,0:T(8,128)S(1)}, u32[]{:S(2)}, u32[]{:S(2)}) %collective-permute-start.1) | collective-permute-done | bytes 4128 | tf_op jit(solution)/shard_map/cond/branch_1_fun/ppermute | solution.py:234
  16.3 1.9 %collective-permute-start.2 = (f32[8,128]{1,0:T(8,128)S(1)}, f32[8,128]{1,0:T(8,128)S(1)}, u32[]{:S(2)}, u32[]{:S(2)}) collective-permute-start(f32[8,128]{1,0:T(8,128)S(1)} %add.26), channel_id=1, source_target_pairs={{16,20},{17,21},{18,22},{19,23},{20,16},{21,17},{22,18},{23,19},{2... | collective-permute-start | bytes 12296 | tf_op jit(solution)/shard_map/cond/branch_1_fun/ppermute | solution.py:234
  18.3 2.8 %collective-permute-done.2 = f32[8,128]{1,0:T(8,128)S(1)} collective-permute-done((f32[8,128]{1,0:T(8,128)S(1)}, f32[8,128]{1,0:T(8,128)S(1)}, u32[]{:S(2)}, u32[]{:S(2)}) %collective-permute-start.2) | collective-permute-done | bytes 4128 | tf_op jit(solution)/shard_map/cond/branch_1_fun/ppermute | solution.py:234
  21.1 2.4 %collective-permute-start.3 = (f32[8,128]{1,0:T(8,128)S(1)}, f32[8,128]{1,0:T(8,128)S(1)}, u32[]{:S(2)}, u32[]{:S(2)}) collective-permute-start(f32[8,128]{1,0:T(8,128)S(1)} %add.27), channel_id=1, source_target_pairs={{16,28},{17,29},{18,30},{19,31},{20,24},{21,25},{22,26},{23,27},{2... | collective-permute-start | bytes 12296 | tf_op jit(solution)/shard_map/cond/branch_1_fun/ppermute | solution.py:234
  23.5 4.3 %collective-permute-done.3 = f32[8,128]{1,0:T(8,128)S(1)} collective-permute-done((f32[8,128]{1,0:T(8,128)S(1)}, f32[8,128]{1,0:T(8,128)S(1)}, u32[]{:S(2)}, u32[]{:S(2)}) %collective-permute-start.3) | collective-permute-done | bytes 4128 | tf_op jit(solution)/shard_map/cond/branch_1_fun/ppermute | solution.py:234
  27.7 0.0 copy-start.2
  27.7 0.0 copy-start.3
  27.8 26.9 %all_to_all.22 = bf16[16,48,2048]{2,1,0:T(8,128)(2,1)S(1)} all-to-all(bf16[16,48,2048]{2,1,0:T(8,128)(2,1)S(1)} %bitcast.6), channel_id=1, replica_groups=mesh['dp'=16,'expert'=16] {'expert'}, dimensions={0} | all-to-all | bytes 6291456 | tf_op jit(solution)/shard_map/all_to_all | solution.py:267
  54.7 0.0 copy-done.2
  54.7 0.0 copy-done.3
  54.7 0.0 copy-start.4
  54.7 5.1 %hidden.1.x_ref = bf16[768,768]{1,0:T(8,128)(2,1)S(1)} custom-call(bf16[768,2048]{1,0:T(8,128)(2,1)S(1)} %bitcast.8, bf16[1,2048,768]{2,1,0:T(8,128)(2,1)S(1)} %copy-done.2, bf16[1,2048,768]{2,1,0:T(8,128)(2,1)S(1)} %copy-done.3), custom_call_target="tpu_custom_call" | custom-call | flops 4831838208 | bytes 9437184 | tf_op jit(solution)/shard_map/hidden/pallas_call | solution.py:119
  59.8 0.0 copy-done.4
  59.8 3.5 %down.1 = bf16[768,2048]{1,0:T(8,128)(2,1)} custom-call(bf16[768,768]{1,0:T(8,128)(2,1)S(1)} %hidden.1.x_ref, bf16[1,768,2048]{2,1,0:T(8,128)(2,1)S(1)} %copy-done.4), custom_call_target="tpu_custom_call" | custom-call | flops 2415919104 | bytes 6291456 | tf_op jit(solution)/shard_map/down/pallas_call | solution.py:154
  63.2 0.0 copy-start
  63.2 0.0 copy-start.1
  63.2 3.8 %all-to-all-start.1 = ((bf16[16,48,2048]{2,1,0:T(8,128)(2,1)}), bf16[16,48,2048]{2,1,0:T(8,128)(2,1)S(1)}, u32[]{:S(2)}, u32[]{:S(2)}) async-start(bf16[16,48,2048]{2,1,0:T(8,128)(2,1)} %bitcast.13), calls=%async_computation.1 | async-start | bytes 6291456 | tf_op jit(solution)/shard_map/all_to_all | solution.py:270
  67.0 3.5 %collective-permute-start.5 = (f32[8,128]{1,0:T(8,128)S(1)}, f32[8,128]{1,0:T(8,128)S(1)}, u32[]{:S(2)}, u32[]{:S(2)}) collective-permute-start(f32[8,128]{1,0:T(8,128)S(1)} %get-tuple-element.25), channel_id=1, source_target_pairs={{16,48},{17,49},{18,50},{19,51},{20,52},{21,53},{22,54},{23,55},{2... | collective-permute-start | bytes 12296 | tf_op jit(solution)/shard_map/ppermute | solution.py:234
  70.6 1.3 %collective-permute-done.5 = f32[8,128]{1,0:T(8,128)S(1)} collective-permute-done((f32[8,128]{1,0:T(8,128)S(1)}, f32[8,128]{1,0:T(8,128)S(1)}, u32[]{:S(2)}, u32[]{:S(2)}) %collective-permute-start.5) | collective-permute-done | bytes 4128 | tf_op jit(solution)/shard_map/ppermute | solution.py:234
  71.8 4.9 %collective-permute-start.6 = (f32[8,128]{1,0:T(8,128)S(1)}, f32[8,128]{1,0:T(8,128)S(1)}, u32[]{:S(2)}, u32[]{:S(2)}) collective-permute-start(f32[8,128]{1,0:T(8,128)S(1)} %add.36), channel_id=1, source_target_pairs={{16,80},{17,81},{18,82},{19,83},{20,84},{21,85},{22,86},{23,87},{2... | collective-permute-start | bytes 12296 | tf_op jit(solution)/shard_map/ppermute | solution.py:234
  76.7 1.0 %collective-permute-done.6 = f32[8,128]{1,0:T(8,128)S(1)} collective-permute-done((f32[8,128]{1,0:T(8,128)S(1)}, f32[8,128]{1,0:T(8,128)S(1)}, u32[]{:S(2)}, u32[]{:S(2)}) %collective-permute-start.6) | collective-permute-done | bytes 4128 | tf_op jit(solution)/shard_map/ppermute | solution.py:234
  77.7 6.7 %collective-permute-start.7 = (f32[8,128]{1,0:T(8,128)S(1)}, f32[8,128]{1,0:T(8,128)S(1)}, u32[]{:S(2)}, u32[]{:S(2)}) collective-permute-start(f32[8,128]{1,0:T(8,128)S(1)} %add.37), channel_id=1, source_target_pairs={{16,240},{17,241},{18,242},{19,243},{20,244},{21,245},{22,246},{23... | collective-permute-start | bytes 12296 | tf_op jit(solution)/shard_map/ppermute | solution.py:234
  84.4 1.0 %collective-permute-done.7 = f32[8,128]{1,0:T(8,128)S(1)} collective-permute-done((f32[8,128]{1,0:T(8,128)S(1)}, f32[8,128]{1,0:T(8,128)S(1)}, u32[]{:S(2)}, u32[]{:S(2)}) %collective-permute-start.7) | collective-permute-done | bytes 4128 | tf_op jit(solution)/shard_map/ppermute | solution.py:234
  85.4 1.3 %collective-permute-start.8 = (f32[8,128]{1,0:T(8,128)S(1)}, f32[8,128]{1,0:T(8,128)S(1)}, u32[]{:S(2)}, u32[]{:S(2)}) collective-permute-start(f32[8,128]{1,0:T(8,128)S(1)} %add.38), channel_id=1, source_target_pairs={{16,0},{17,1},{18,2},{19,3},{20,4},{21,5},{22,6},{23,7},{24,8},{25... | collective-permute-start | bytes 12296 | tf_op jit(solution)/shard_map/ppermute | solution.py:239
  86.7 0.0 copy-done
  86.7 0.4 select.3.pick_ref
  87.1 0.4 collective-permute-done.8
  87.5 0.6 multiply_reduce_fusion
  88.7 2.8 %all-to-all-done.1 = bf16[16,48,2048]{2,1,0:T(8,128)(2,1)S(1)} async-done(((bf16[16,48,2048]{2,1,0:T(8,128)(2,1)}), bf16[16,48,2048]{2,1,0:T(8,128)(2,1)S(1)}, u32[]{:S(2)}, u32[]{:S(2)}) %all-to-all-start.1) | async-done | bytes 3145760 | tf_op jit(solution)/shard_map/all_to_all | solution.py:270
  91.5 0.0 copy-done.1
  91.5 1.7 %combine.1 = bf16[128,2048]{1,0:T(8,128)(2,1)} custom-call(bf16[256,768]{1,0:T(8,128)(2,1)S(1)} %select.3.pick_ref, f32[2,128]{1,0:T(2,128)S(1)} %bitcast.12, bf16[768,2048]{1,0:T(8,128)(2,1)S(1)} %bitcast.7), custom_call_target="tpu_custom_call" | custom-call | flops 805306368 | bytes 3145728 | tf_op jit(solution)/shard_map/combine/pallas_call | solution.py:219
  (9 shorter events, 0.0 us)
Async XLA Ops:
  1.7 4.3 %collective-permute-start.4 = (f32[8,128]{1,0:T(8,128)S(1)}, f32[8,128]{1,0:T(8,128)S(1)}, u32[]{:S(2)}, u32[]{:S(2)}) collective-permute-start(f32[8,128]{1,0:T(8,128)S(1)} %get-tuple-element.16), channel_id=1, source_target_pairs={{0,16},{1,17},{2,18},{3,19},{4,20},{5,21},{6,22},{7,23},{8,24},{9,... | collective-permute-start | bytes 12296 | tf_op jit(solution)/shard_map/ppermute | solution.py:256
  6.1 4.4 %collective-permute-start = (f32[8,128]{1,0:T(8,128)S(1)}, f32[8,128]{1,0:T(8,128)S(1)}, u32[]{:S(2)}, u32[]{:S(2)}) collective-permute-start(f32[8,128]{1,0:T(8,128)S(1)} %param.1), channel_id=1, source_target_pairs={{16,17},{17,16},{18,19},{19,18},{20,21},{21,20},{22,23},{23,22},{2... | collective-permute-start | bytes 12296 | tf_op jit(solution)/shard_map/cond/branch_1_fun/ppermute | solution.py:234
  10.4 5.9 %collective-permute-start.1 = (f32[8,128]{1,0:T(8,128)S(1)}, f32[8,128]{1,0:T(8,128)S(1)}, u32[]{:S(2)}, u32[]{:S(2)}) collective-permute-start(f32[8,128]{1,0:T(8,128)S(1)} %add.25), channel_id=1, source_target_pairs={{16,19},{17,18},{18,17},{19,16},{20,23},{21,22},{22,21},{23,20},{2... | collective-permute-start | bytes 12296 | tf_op jit(solution)/shard_map/cond/branch_1_fun/ppermute | solution.py:234
  16.3 4.7 %collective-permute-start.2 = (f32[8,128]{1,0:T(8,128)S(1)}, f32[8,128]{1,0:T(8,128)S(1)}, u32[]{:S(2)}, u32[]{:S(2)}) collective-permute-start(f32[8,128]{1,0:T(8,128)S(1)} %add.26), channel_id=1, source_target_pairs={{16,20},{17,21},{18,22},{19,23},{20,16},{21,17},{22,18},{23,19},{2... | collective-permute-start | bytes 12296 | tf_op jit(solution)/shard_map/cond/branch_1_fun/ppermute | solution.py:234
  21.1 6.7 %collective-permute-start.3 = (f32[8,128]{1,0:T(8,128)S(1)}, f32[8,128]{1,0:T(8,128)S(1)}, u32[]{:S(2)}, u32[]{:S(2)}) collective-permute-start(f32[8,128]{1,0:T(8,128)S(1)} %add.27), channel_id=1, source_target_pairs={{16,28},{17,29},{18,30},{19,31},{20,24},{21,25},{22,26},{23,27},{2... | collective-permute-start | bytes 12296 | tf_op jit(solution)/shard_map/cond/branch_1_fun/ppermute | solution.py:234
  27.7 26.9 %copy-start.2 = (bf16[1,2048,768]{2,1,0:T(8,128)(2,1)S(1)}, bf16[1,2048,768]{2,1,0:T(8,128)(2,1)}, u32[]{:S(2)}) copy-start(bf16[1,2048,768]{2,1,0:T(8,128)(2,1)} %gate_ref.1) | copy-start | bytes 9437188
  27.7 26.9 %copy-start.3 = (bf16[1,2048,768]{2,1,0:T(8,128)(2,1)S(1)}, bf16[1,2048,768]{2,1,0:T(8,128)(2,1)}, u32[]{:S(2)}) copy-start(bf16[1,2048,768]{2,1,0:T(8,128)(2,1)} %up_ref.1) | copy-start | bytes 9437188
  54.7 5.1 %copy-start.4 = (bf16[1,768,2048]{2,1,0:T(8,128)(2,1)S(1)}, bf16[1,768,2048]{2,1,0:T(8,128)(2,1)}, u32[]{:S(2)}) copy-start(bf16[1,768,2048]{2,1,0:T(8,128)(2,1)} %down_ref.1) | copy-start | bytes 9437188
  63.2 23.4 %copy-start = (s32[128,2]{0,1:T(2,128)S(1)}, s32[128,2]{0,1:T(2,128)}, u32[]{:S(2)}) copy-start(s32[128,2]{0,1:T(2,128)} %param.9) | copy-start | bytes 3076
  63.2 28.3 %copy-start.1 = (f32[128,2]{0,1:T(2,128)S(1)}, f32[128,2]{0,1:T(2,128)}, u32[]{:S(2)}) copy-start(f32[128,2]{0,1:T(2,128)} %param.10) | copy-start | bytes 3076
  63.2 28.3 %all-to-all-start.1 = ((bf16[16,48,2048]{2,1,0:T(8,128)(2,1)}), bf16[16,48,2048]{2,1,0:T(8,128)(2,1)S(1)}, u32[]{:S(2)}, u32[]{:S(2)}) async-start(bf16[16,48,2048]{2,1,0:T(8,128)(2,1)} %bitcast.13), calls=%async_computation.1 | async-start | bytes 6291456 | tf_op jit(solution)/shard_map/all_to_all | solution.py:270
  67.0 4.8 %collective-permute-start.5 = (f32[8,128]{1,0:T(8,128)S(1)}, f32[8,128]{1,0:T(8,128)S(1)}, u32[]{:S(2)}, u32[]{:S(2)}) collective-permute-start(f32[8,128]{1,0:T(8,128)S(1)} %get-tuple-element.25), channel_id=1, source_target_pairs={{16,48},{17,49},{18,50},{19,51},{20,52},{21,53},{22,54},{23,55},{2... | collective-permute-start | bytes 12296 | tf_op jit(solution)/shard_map/ppermute | solution.py:234
  71.8 5.9 %collective-permute-start.6 = (f32[8,128]{1,0:T(8,128)S(1)}, f32[8,128]{1,0:T(8,128)S(1)}, u32[]{:S(2)}, u32[]{:S(2)}) collective-permute-start(f32[8,128]{1,0:T(8,128)S(1)} %add.36), channel_id=1, source_target_pairs={{16,80},{17,81},{18,82},{19,83},{20,84},{21,85},{22,86},{23,87},{2... | collective-permute-start | bytes 12296 | tf_op jit(solution)/shard_map/ppermute | solution.py:234
  77.7 7.7 %collective-permute-start.7 = (f32[8,128]{1,0:T(8,128)S(1)}, f32[8,128]{1,0:T(8,128)S(1)}, u32[]{:S(2)}, u32[]{:S(2)}) collective-permute-start(f32[8,128]{1,0:T(8,128)S(1)} %add.37), channel_id=1, source_target_pairs={{16,240},{17,241},{18,242},{19,243},{20,244},{21,245},{22,246},{23... | collective-permute-start | bytes 12296 | tf_op jit(solution)/shard_map/ppermute | solution.py:234
  85.4 2.1 %collective-permute-start.8 = (f32[8,128]{1,0:T(8,128)S(1)}, f32[8,128]{1,0:T(8,128)S(1)}, u32[]{:S(2)}, u32[]{:S(2)}) collective-permute-start(f32[8,128]{1,0:T(8,128)S(1)} %add.38), channel_id=1, source_target_pairs={{16,0},{17,1},{18,2},{19,3},{20,4},{21,5},{22,6},{23,7},{24,8},{25... | collective-permute-start | bytes 12296 | tf_op jit(solution)/shard_map/ppermute | solution.py:239

commit v6 on v5

--- a/solution.py
+++ b/solution.py
@@ -30,7 +30,7 @@
 
 
 def count_kernel(
-    cap, ids_hbm, gates_hbm, tok_hbm, slot_ref, stats_ref, tok_ref, ids_ref, gates_ref, sems
+    experts, cap, ids_hbm, gates_hbm, tok_hbm, slot_ref, stats_ref, tok_ref, gates_ref, ids_ref, sems
 ):
     toks = ids_ref.shape[1]
     ids_copy = pltpu.make_async_copy(ids_hbm, ids_ref, sems.at[0])
@@ -41,37 +41,48 @@
     tok_copy.start()
     ids_copy.wait()
     first_slot, second_slot, first, second = slots_of(ids_ref[...], cap)
-    slot_ref[0:1, :] = first_slot.astype(jnp.int32)
-    slot_ref[1:2, :] = second_slot.astype(jnp.int32)
     count = jnp.sum(first + second, 1, keepdims=True)
     gates_copy.wait()
     gates = gates_ref[...]
     mass = jnp.sum(first * gates[0:1, :] + second * gates[1:2, :], 1, keepdims=True)
     lanes = lax.broadcasted_iota(jnp.int32, (toks, toks), 1)
-    stats_ref[...] = jnp.where(lanes == 0, count, jnp.where(lanes == 1, mass, 0.0)).T[:8, :]
+    stats = jnp.where(lanes == 0, count, jnp.where(lanes == 1, mass, 0.0)).T[:8, :]
+    stats_ref[...] = stats
+    lane, line = lanes[:8, :], lax.broadcasted_iota(jnp.int32, (8, toks), 0)
+    free = ((stats[0:1, :] < cap) & (lane < experts)).astype(jnp.int32)
+    slots = jnp.where(line == 0, first_slot.astype(jnp.int32), second_slot.astype(jnp.int32))
+    slot_ref[...] = jnp.where(line < 2, slots, free)
     tok_copy.wait()
 
 
-def count(ids, gates, tokens, cap):
+def count(ids, gates, tokens, experts, cap):
     toks = ids.shape[1]
     return pl.pallas_call(
-        functools.partial(count_kernel, cap),
+        functools.partial(count_kernel, experts, cap),
         in_specs=[pl.BlockSpec(memory_space=pltpu.HBM)] * 3,
-        out_specs=[pl.BlockSpec(memory_space=pltpu.VMEM)] * 3,
+        out_specs=[pl.BlockSpec(memory_space=pltpu.VMEM)] * 4,
         out_shape=[
             jax.ShapeDtypeStruct((8, toks), jnp.int32),
             jax.ShapeDtypeStruct((8, toks), F32),
             jax.ShapeDtypeStruct(tokens.shape, tokens.dtype),
+            jax.ShapeDtypeStruct(gates.shape, gates.dtype),
         ],
         scratch_shapes=[
             pltpu.VMEM(ids.shape, ids.dtype),
-            pltpu.VMEM(gates.shape, gates.dtype),
             pltpu.SemaphoreType.DMA((3,)),
         ],
         compiler_params=pltpu.CompilerParams(vmem_limit_bytes=4 * 2**20),
         cost_estimate=pl.CostEstimate(flops=4 * toks**3, bytes_accessed=8 * toks, transcendentals=0),
         name="count",
     )(*(pltpu.with_memory_space_constraint(a, pltpu.HBM) for a in (ids, gates, tokens)))
+
+
+def pieces(value, count):
+    parts = []
+    for _ in range(count):
+        parts.append(value.astype(BF16).astype(F32))
+        value = value - parts[-1]
+    return parts
 
 
 def pack_kernel(slot_ref, tok_ref, out_ref):
@@ -103,7 +114,49 @@
     )(slots, tokens)
 
 
-def hidden_kernel(x_ref, gate_ref, up_ref, out_ref):
+def is_free(slot_ref, expert):
+    lane = lax.broadcasted_iota(jnp.int32, (1, slot_ref.shape[1]), 1)
+    return jnp.sum(jnp.where(lane == expert, slot_ref[2:3, :], 0), 1, keepdims=True) > 0
+
+
+def note_kernel(experts, cap, slot_ref, sums_ref, in_ref, out_ref):
+    lines = pieces(sums_ref[0:1, :], 2) + pieces(sums_ref[1:2, :], 3)
+    line = jnp.concatenate(lines, 1)
+    edge = line.shape[1]
+    line = jnp.broadcast_to(line, (16, edge))
+    last = lax.broadcasted_iota(jnp.int32, (16, edge), 0) == 15
+    for e in range(experts):
+        tile = slice((e + 1) * cap - 16, (e + 1) * cap)
+        old = in_ref[tile, :edge].astype(F32)
+        out_ref[tile, :edge] = jnp.where(last & is_free(slot_ref, e), line, old).astype(BF16)
+
+
+def note(slots, sums, rows, experts, cap):
+    held = pl.BlockSpec(memory_space=pltpu.VMEM)
+    return pl.pallas_call(
+        functools.partial(note_kernel, experts, cap),
+        in_specs=[held] * 3,
+        out_specs=held,
+        out_shape=jax.ShapeDtypeStruct(rows.shape, rows.dtype),
+        input_output_aliases={2: 0},
+        compiler_params=pltpu.CompilerParams(vmem_limit_bytes=4 * 2**20),
+        cost_estimate=pl.CostEstimate(flops=0, bytes_accessed=2**16, transcendentals=0),
+        name="note",
+    )(slots, sums, rows)
+
+
+def hidden_kernel(experts, cap, tokens, x_ref, gate_ref, up_ref, out_ref, loss_ref):
+    lanes = loss_ref.shape[1]
+    total = jnp.zeros((16, 5 * lanes), F32)
+    for end in range(cap, x_ref.shape[0] + 1, cap):
+        total = total + x_ref[end - 16 : end, : 5 * lanes].astype(F32)
+    part = [total[15:16, i * lanes : (i + 1) * lanes] for i in range(5)]
+    load, mass = part[0] + part[1], part[2] + part[3] + part[4]
+    loss = experts * jnp.sum(load / (2 * tokens) * (mass / tokens), 1, keepdims=True)
+    lane = lax.broadcasted_iota(jnp.int32, loss_ref.shape, 1)
+    high, middle, low = pieces(loss, 3)
+    line = jnp.where(lane == 0, high, jnp.where(lane == 1, middle, jnp.where(lane == 2, low, 0.0)))
+    loss_ref[...] = line
     x = x_ref[...]
     for start in range(0, out_ref.shape[1], 256):
         tile = slice(start, start + 256)
@@ -112,15 +165,15 @@
         out_ref[:, tile] = (gate / (1.0 + jnp.exp(-gate)) * up).astype(BF16)
 
 
-def hidden_of(x, w_gate, w_up):
+def hidden_of(x, w_gate, w_up, experts, cap, tokens):
     rows, width = x.shape
     middle = w_gate.shape[2]
     held = pl.BlockSpec(memory_space=pltpu.VMEM)
     return pl.pallas_call(
-        hidden_kernel,
+        functools.partial(hidden_kernel, experts, cap, tokens),
         in_specs=[held] * 3,
-        out_specs=held,
-        out_shape=jax.ShapeDtypeStruct((rows, middle), BF16),
+        out_specs=[held] * 2,
+        out_shape=[jax.ShapeDtypeStruct((rows, middle), BF16), jax.ShapeDtypeStruct((8, 128), F32)],
         compiler_params=pltpu.CompilerParams(vmem_limit_bytes=16 * 2**20),
         cost_estimate=pl.CostEstimate(
             flops=4 * rows * width * middle,
@@ -131,32 +184,30 @@
     )(x, w_gate, w_up)
 
 
-def down_kernel(x_ref, down_ref, out_hbm, out_ref, sems):
-    rows = x_ref.shape[0]
-    copies = []
-    start = 0
-    for part, size in enumerate((rows // 2, rows // 3, rows // 6)):
-        tile = pl.ds(start, size)
+def down_kernel(cap, mine_ref, slot_ref, loss_ref, x_ref, down_ref, out_ref):
+    for start in range(0, x_ref.shape[0], 256):
+        tile = slice(start, start + 256)
         out_ref[tile, :] = jnp.dot(
             x_ref[tile, :], down_ref[0], preferred_element_type=F32
         ).astype(BF16)
-        copies.append(pltpu.make_async_copy(out_ref.at[tile], out_hbm.at[tile], sems.at[part]))
-        copies[-1].start()
-        start += size
-    for copy in copies:
-        copy.wait()
-
-
-def down_of(x, w_down):
+    row = lax.broadcasted_iota(jnp.int32, (16, 128), 0)
+    here = (row == 15) & is_free(slot_ref, mine_ref[0])
+    line = jnp.broadcast_to(loss_ref[0:1, :], (16, 128))
+    for end in range(cap, x_ref.shape[0] + 1, cap):
+        tile = slice(end - 16, end)
+        old = out_ref[tile, 0:128].astype(F32)
+        out_ref[tile, 0:128] = jnp.where(here, line, old).astype(BF16)
+
+
+def down_of(mine, slots, loss, x, w_down, cap):
     rows, middle = x.shape
     width = w_down.shape[2]
     held = pl.BlockSpec(memory_space=pltpu.VMEM)
     return pl.pallas_call(
-        down_kernel,
-        in_specs=[held] * 2,
-        out_specs=pl.BlockSpec(memory_space=pltpu.HBM),
-        out_shape=pltpu.HBM((rows, width), BF16),
-        scratch_shapes=[pltpu.VMEM((rows, width), BF16), pltpu.SemaphoreType.DMA((3,))],
+        functools.partial(down_kernel, cap),
+        in_specs=[pl.BlockSpec(memory_space=pltpu.SMEM)] + [held] * 4,
+        out_specs=held,
+        out_shape=jax.ShapeDtypeStruct((rows, width), BF16),
         compiler_params=pltpu.CompilerParams(vmem_limit_bytes=16 * 2**20),
         cost_estimate=pl.CostEstimate(
             flops=2 * rows * width * middle,
@@ -164,13 +215,13 @@
             transcendentals=0,
         ),
         name="down",
-    )(x, w_down)
-
-
-def select_kernel(cap, ids_ref, pick_ref):
-    toks, slots = ids_ref.shape[1], pick_ref.shape[1]
-    first_slot, second_slot, _, _ = slots_of(ids_ref[...], cap)
+    )(mine, slots, loss, x, w_down)
+
+
+def select_kernel(slot_ref, pick_ref):
+    toks, slots = slot_ref.shape[1], pick_ref.shape[1]
     labels = lax.broadcasted_iota(jnp.int32, (toks, toks), 0)
+    first_slot, second_slot = slot_ref[0:1, :].astype(F32), slot_ref[1:2, :].astype(F32)
     lines = jnp.where(labels == 0, first_slot, jnp.where(labels == 1, second_slot, 0.0)).T
     dest = lines[:, 0:2].astype(jnp.int32)
     lane = lax.broadcasted_iota(jnp.int32, (toks, slots), 1)
@@ -178,18 +229,58 @@
     pick_ref[toks:, :] = (lane == dest[:, 1:2]).astype(F32).astype(BF16)
 
 
-def select(ids, slots, cap):
-    toks = ids.shape[1]
-    held = pl.BlockSpec(memory_space=pltpu.VMEM)
-    return pl.pallas_call(
-        functools.partial(select_kernel, cap),
+def select(slots, count):
+    toks = slots.shape[1]
+    held = pl.BlockSpec(memory_space=pltpu.VMEM)
+    return pl.pallas_call(
+        select_kernel,
         in_specs=[held],
         out_specs=held,
-        out_shape=jax.ShapeDtypeStruct((2 * toks, slots), BF16),
+        out_shape=jax.ShapeDtypeStruct((2 * toks, count), BF16),
         compiler_params=pltpu.CompilerParams(vmem_limit_bytes=4 * 2**20),
-        cost_estimate=pl.CostEstimate(flops=0, bytes_accessed=4 * toks * slots, transcendentals=0),
+        cost_estimate=pl.CostEstimate(flops=0, bytes_accessed=4 * toks * count, transcendentals=0),
         name="select",
-    )(ids)
+    )(slots)
+
+
+def read_kernel(cap, slot_ref, rows_ref, out_ref):
+    line = rows_ref[3 * cap - 16 : 3 * cap, 0:128].astype(F32)[15:16, :]
+    for e in (1, 0):
+        other = rows_ref[(e + 1) * cap - 16 : (e + 1) * cap, 0:128].astype(F32)[15:16, :]
+        line = jnp.where(is_free(slot_ref, e), other, line)
+    out_ref[...] = jnp.broadcast_to(line, out_ref.shape)
+
+
+def read(slots, rows, cap):
+    held = pl.BlockSpec(memory_space=pltpu.VMEM)
+    return pl.pallas_call(
+        functools.partial(read_kernel, cap),
+        in_specs=[held] * 2,
+        out_specs=held,
+        out_shape=jax.ShapeDtypeStruct((8, 128), F32),
+        compiler_params=pltpu.CompilerParams(vmem_limit_bytes=4 * 2**20),
+        cost_estimate=pl.CostEstimate(flops=0, bytes_accessed=2**14, transcendentals=0),
+        name="read",
+    )(slots, rows)
+
+
+def loss_kernel(late_ref, mine_ref, other_ref, out_ref):
+    lane = lax.broadcasted_iota(jnp.int32, (1, 128), 1)
+    line = jnp.where(late_ref[0] > 0, mine_ref[0:1, :], other_ref[0:1, :])
+    out_ref[0, 0] = jnp.sum(jnp.where(lane < 3, line, 0.0))
+
+
+def loss_of(late, mine, other):
+    held = pl.BlockSpec(memory_space=pltpu.VMEM)
+    far = pl.BlockSpec(memory_space=pltpu.SMEM)
+    return pl.pallas_call(
+        loss_kernel,
+        in_specs=[far, held, held],
+        out_specs=far,
+        out_shape=jax.ShapeDtypeStruct((1, 1), F32),
+        compiler_params=pltpu.CompilerParams(vmem_limit_bytes=2**20),
+        name="loss",
+    )(late, mine, other)
 
 
 def combine_kernel(pick_ref, gates_ref, rows_ref, out_hbm, out_ref, sems):
@@ -234,11 +325,6 @@
     return value + lax.ppermute(value, AXES, [(i, i ^ flip) for i in range(size) if (i // step) % 2 == 1])
 
 
-def hand_over(value, size, step, sender):
-    turn = step if sender == 0 else -step
-    return lax.ppermute(value, AXES, [(i, i + turn) for i in range(size) if (i // step) % 2 == sender])
-
-
 def on_device(tokens, expert_ids, gate_weights, w_gate, w_up, w_down):
     toks, width = tokens.shape
     picks = expert_ids.shape[1]
@@ -251,30 +337,32 @@
     size = copies * group
     stride = 2 * group
     ids, gates = expert_ids.T, gate_weights.T
-    slots, stats, tokens = count(ids, gates, tokens, cap)
+    slots, stats, tokens, gates = count(ids, gates, tokens, experts, cap)
     swap = [(i, i + group if (i // group) % 2 == 0 else i - group) for i in range(size)]
-    stats = stats + lax.ppermute(stats, AXES, swap)
+    late = lax.axis_index("dp") % 2
+    mine = lax.axis_index("expert").reshape(1)
+    other = lax.ppermute(stats, AXES, swap)
     outgoing = pack(slots, tokens, experts * cap)
-    late = lax.axis_index("dp") % 2 == 1
-
-    def plane_sum(value):
-        for flip in (1, 3, 4, 12):
-            value = add_round(value, size, flip, group)
+    pick = select(slots, experts * cap)
+
+    def column_sum(value, other):
+        value = value + other
+        for flip in (1, 2, 7):
+            value = add_round(value, size, flip * stride, group)
         return value
 
-    stats = lax.cond(late, plane_sum, lambda value: value, stats)
-    stats, outgoing = lax.optimization_barrier((stats, outgoing))
+    stats = lax.cond(late == 1, column_sum, lambda value, other: value, stats, other)
+    outgoing = note(slots, stats, outgoing, experts, cap)
+    late, mine, pick, outgoing = lax.optimization_barrier((late.reshape(1), mine, pick, outgoing))
     received = lax.all_to_all(outgoing, "expert", split_axis=0, concat_axis=0, tiled=True)
-    result = down_of(hidden_of(received, w_gate, w_up), w_down)
-    stats, result, ids, gates = lax.optimization_barrier((stats, result, ids, gates))
+    hidden, loss = hidden_of(received, w_gate, w_up, experts, cap, all_tokens)
+    result = down_of(mine, slots, loss, hidden, w_down, cap)
     returned = lax.all_to_all(result, "expert", split_axis=0, concat_axis=0, tiled=True)
-    pick = select(ids, experts * cap, cap)
-    for flip in (1, 2, 7):
-        stats = add_round(stats, size, flip * stride, group)
-    stats = jnp.where(late, stats, hand_over(stats, size, group, 1))
-    load, mass = stats[0, :experts], stats[1, :experts]
-    aux_loss = experts * jnp.sum(load / (all_tokens * picks) * (mass / all_tokens))
-    return combine(pick, gates, returned), aux_loss
+    loss = read(slots, returned, cap)
+    other = lax.ppermute(loss, AXES, swap)
+    mixed = combine(pick, gates, returned)
+    other, mixed = lax.optimization_barrier((other, mixed))
+    return mixed, loss_of(late, loss, other).reshape(())
 
 
 def solution(mesh):

time: 95 us -> 91.2 us (0.960)
  blocking collectives: 26.9 us -> 56.4 us
  starting transfers between devices: 32.6 us -> 14.3 us
  waiting for transfers between devices: 18.9 us -> 5.6 us
  between operations: 2.56 us -> 0.76 us
    all_to_all x0 -> x1, blocking collectives: none -> 26.2 us  [on_device(): lax.all_to_all(result, 'expert', split_axis=0, concat_axis=0, tiled=True)]
    ppermute x7 -> x3, starting transfers between devices: 24.2 us -> 11 us  [add_round(): lax.ppermute(value, AXES, [(i, i ^ flip) for i in range(size) if i // ste...]
    ppermute x7 -> x3, waiting for transfers between devices: 15.7 us -> 5.59 us  [add_round(): lax.ppermute(value, AXES, [(i, i ^ flip) for i in range(size) if i // ste...]
    all_to_all x1 -> x0, starting transfers between devices: 3.75 us -> none  [on_device(): lax.all_to_all(result, 'expert', split_axis=0, concat_axis=0, tiled=True)]
    all_to_all x1, blocking collectives: 26.9 us -> 30.3 us  [on_device(): lax.all_to_all(outgoing, 'expert', split_axis=0, concat_axis=0, tiled=True)]
    all_to_all x1 -> x0, waiting for transfers between devices: 2.8 us -> none  [on_device(): lax.all_to_all(result, 'expert', split_axis=0, concat_axis=0, tiled=True)]
    ppermute x2, starting transfers between devices: 4.61 us -> 3.35 us  [the longest x1 3.33 us: on_device(): other = lax.ppermute(stats, AXES, swap)]
    pallas_call x4 -> x7, Pallas kernels: 9.99 us -> 9.9 us  [the longest x1 5.08 us: hidden_of(): pl.pallas_call(functools.partial(hidden_kernel, experts, cap, tokens), in...]
  transfers between devices with their start and end apart: 10 -> 5, of which waited for: 9 -> 3; matrix products, arithmetic and copies ran while one was open for 1% -> 0% of each run, Pallas kernels for 1% -> 3%
where the time goes in v6:
time: 91.2 us; the launch traced here: 89.8 us
  blocking collectives  56.4 us (62%)
  starting transfers between devices  14.3 us (16%)
  Pallas kernels  12.6 us (14%)
  waiting for transfers between devices  5.6 us (6%)
    all_to_all x1, blocking collectives, on_device(): lax.all_to_all(outgoing, 'expert', split_axis=0, concat_axis=0, tiled=True)  30.3 us
    all_to_all x1, blocking collectives, on_device(): lax.all_to_all(result, 'expert', split_axis=0, concat_axis=0, tiled=True)  26.2 us
    ppermute x3, starting transfers between devices, add_round(): lax.ppermute(value, AXES, [(i, i ^ flip) for i in range(size) if i // ste...  11 us
    ppermute x3, waiting for transfers between devices, add_round(): lax.ppermute(value, AXES, [(i, i ^ flip) for i in range(size) if i // ste...  5.59 us
    pallas_call x1, Pallas kernels, hidden_of(): pl.pallas_call(functools.partial(hidden_kernel, experts, cap, tokens), in...  5.08 us
    ppermute x1, starting transfers between devices, on_device(): other = lax.ppermute(stats, AXES, swap)  3.33 us
    pallas_call x1, Pallas kernels, down_of(): pl.pallas_call(functools.partial(down_kernel, cap), in_specs=[pl.BlockSpe...  2.63 us
  transfers between devices with their start and end apart: 5, of which 3 were waited for; matrix products, arithmetic and copies ran while one was open for 0% of the time, Pallas kernels for 3%

profile of v6, /device:TPU:1, one launch (start us, length us, event | category | flops | bytes accessed | tf_op | source)
XLA Modules:
  0.0 89.8 jit_solution(8985986232998738884)
XLA Ops:
  0.6 1.1 %count.1 = (s32[8,128]{1,0:T(8,128)S(1)}, f32[8,128]{1,0:T(8,128)S(1)}, bf16[128,2048]{1,0:T(8,128)(2,1)S(1)}, f32[2,128]{1,0:T(2,128)S(1)}) custom-call(s32[2,128]{1,0:T(2,128)} %bitcast.14, f32[2,128]{1,0:T(2,128)} %bitcast.15, bf16[128,2048]{1,0:T(8,128)(2,1)} %tok_hbm.1), custom_call_target="tpu_custom_call" | custom-call | flops 8388608 | bytes 1024 | tf_op jit(solution)/shard_map/count/pallas_call | solution.py:60
  1.7 3.3 %collective-permute-start.3 = (f32[8,128]{1,0:T(8,128)S(1)}, f32[8,128]{1,0:T(8,128)S(1)}, u32[]{:S(2)}, u32[]{:S(2)}) collective-permute-start(f32[8,128]{1,0:T(8,128)S(1)} %get-tuple-element.25), channel_id=1, source_target_pairs={{0,16},{1,17},{2,18},{3,19},{4,20},{5,21},{6,22},{7,23},{8,24},{9,... | collective-permute-start | bytes 12296 | tf_op jit(solution)/shard_map/ppermute | solution.py:344
  5.1 1.0 %pack.1.in_ref = bf16[768,2048]{1,0:T(8,128)(2,1)S(1)} custom-call(s32[8,128]{1,0:T(8,128)S(1)} %get-tuple-element.24.slot_ref, bf16[128,2048]{1,0:T(8,128)(2,1)S(1)} %get-tuple-element.26.tok_ref), custom_call_target="tpu_custom_call" | custom-call | flops 402653184 | bytes 6291456 | tf_op jit(solution)/shard_map/pack/pallas_call | solution.py:104
  6.0 0.2 select.3.pick_ref
  6.3 0.0 collective-permute-done.3
  6.3 16.6 %conditional.1 = (f32[8,128]{1,0:T(8,128)S(1)}) conditional(s32[]{:T(128)} %convert_element_type.3, f32[8,128]{1,0:T(8,128)S(1)} %get-tuple-element.25, (f32[8,128]{1,0:T(8,128)S(1)}, f32[8,128]{1,0:T(8,128)S(1)}) %tuple.16), branch_computations={%region_0.1_spmd, %region_1.2_spmd} | conditional | flops 4096 | bytes 98432 | solution.py:354
  6.3 1.9 %collective-permute-start = (f32[8,128]{1,0:T(8,128)S(1)}, f32[8,128]{1,0:T(8,128)S(1)}, u32[]{:S(2)}, u32[]{:S(2)}) collective-permute-start(f32[8,128]{1,0:T(8,128)S(1)} %add.11), channel_id=1, source_target_pairs={{16,48},{17,49},{18,50},{19,51},{20,52},{21,53},{22,54},{23,55},{2... | collective-permute-start | bytes 12296 | tf_op jit(solution)/shard_map/cond/branch_1_fun/ppermute | solution.py:325
  8.2 2.4 %collective-permute-done = f32[8,128]{1,0:T(8,128)S(1)} collective-permute-done((f32[8,128]{1,0:T(8,128)S(1)}, f32[8,128]{1,0:T(8,128)S(1)}, u32[]{:S(2)}, u32[]{:S(2)}) %collective-permute-start) | collective-permute-done | bytes 4128 | tf_op jit(solution)/shard_map/cond/branch_1_fun/ppermute | solution.py:325
  10.7 3.3 %collective-permute-start.1 = (f32[8,128]{1,0:T(8,128)S(1)}, f32[8,128]{1,0:T(8,128)S(1)}, u32[]{:S(2)}, u32[]{:S(2)}) collective-permute-start(f32[8,128]{1,0:T(8,128)S(1)} %add.12), channel_id=1, source_target_pairs={{16,80},{17,81},{18,82},{19,83},{20,84},{21,85},{22,86},{23,87},{2... | collective-permute-start | bytes 12296 | tf_op jit(solution)/shard_map/cond/branch_1_fun/ppermute | solution.py:325
  14.0 1.9 %collective-permute-done.1 = f32[8,128]{1,0:T(8,128)S(1)} collective-permute-done((f32[8,128]{1,0:T(8,128)S(1)}, f32[8,128]{1,0:T(8,128)S(1)}, u32[]{:S(2)}, u32[]{:S(2)}) %collective-permute-start.1) | collective-permute-done | bytes 4128 | tf_op jit(solution)/shard_map/cond/branch_1_fun/ppermute | solution.py:325
  15.9 5.7 %collective-permute-start.2 = (f32[8,128]{1,0:T(8,128)S(1)}, f32[8,128]{1,0:T(8,128)S(1)}, u32[]{:S(2)}, u32[]{:S(2)}) collective-permute-start(f32[8,128]{1,0:T(8,128)S(1)} %add.13), channel_id=1, source_target_pairs={{16,240},{17,241},{18,242},{19,243},{20,244},{21,245},{22,246},{23... | collective-permute-start | bytes 12296 | tf_op jit(solution)/shard_map/cond/branch_1_fun/ppermute | solution.py:325
  21.7 1.3 %collective-permute-done.2 = f32[8,128]{1,0:T(8,128)S(1)} collective-permute-done((f32[8,128]{1,0:T(8,128)S(1)}, f32[8,128]{1,0:T(8,128)S(1)}, u32[]{:S(2)}, u32[]{:S(2)}) %collective-permute-start.2) | collective-permute-done | bytes 4128 | tf_op jit(solution)/shard_map/cond/branch_1_fun/ppermute | solution.py:325
  22.9 0.1 note.1
  23.1 0.0 copy-start
  23.1 0.0 copy-start.1
  23.1 30.3 %all_to_all.22 = bf16[16,48,2048]{2,1,0:T(8,128)(2,1)S(1)} all-to-all(bf16[16,48,2048]{2,1,0:T(8,128)(2,1)S(1)} %bitcast.9), channel_id=1, replica_groups=mesh['dp'=16,'expert'=16] {'expert'}, dimensions={0} | all-to-all | bytes 6291456 | tf_op jit(solution)/shard_map/all_to_all | solution.py:357
  53.4 0.0 copy-done
  53.4 0.0 copy-done.1
  53.4 0.0 copy-start.2
  53.4 5.1 %hidden.1 = (bf16[768,768]{1,0:T(8,128)(2,1)S(1)}, f32[8,128]{1,0:T(8,128)S(1)}) custom-call(bf16[768,2048]{1,0:T(8,128)(2,1)S(1)} %bitcast.12, bf16[1,2048,768]{2,1,0:T(8,128)(2,1)S(1)} %copy-done, bf16[1,2048,768]{2,1,0:T(8,128)(2,1)S(1)} %copy-done.1), custom_call_target="tpu_custom_call" | custom-call | flops 4831838208 | bytes 9437184 | tf_op jit(solution)/shard_map/hidden/pallas_call | solution.py:172
  58.5 0.0 copy-done.2
  58.5 2.6 %down.1 = bf16[768,2048]{1,0:T(8,128)(2,1)S(1)} custom-call(s32[1]{0:T(128)} %bitcast.3.mine_ref, s32[8,128]{1,0:T(8,128)S(1)} %get-tuple-element.24.slot_ref, f32[8,128]{1,0:T(8,128)S(1)} %get-tuple-element.29.loss_ref, bf16[768,768]{1,0:T(8,128)(2,1)S(1)} %get-tuple-element.30.x_ref, bf16[1,768,2048]{2,1,0:T(8,128)(2,1)S(1)} %copy-done.2), custom_call_target="tpu_custom_call" | custom-call | flops 2415919104 | bytes 6291456 | tf_op jit(solution)/shard_map/down/pallas_call | solution.py:206
  61.1 26.2 %all_to_all.23 = bf16[16,48,2048]{2,1,0:T(8,128)(2,1)S(1)} all-to-all(bf16[16,48,2048]{2,1,0:T(8,128)(2,1)S(1)} %bitcast.13), channel_id=1, replica_groups=mesh['dp'=16,'expert'=16] {'expert'}, dimensions={0} | all-to-all | bytes 6291456 | tf_op jit(solution)/shard_map/all_to_all | solution.py:360
  87.3 0.1 read.1.mine_ref
  87.4 0.0 collective-permute-start.4
  87.4 1.7 %combine.1 = bf16[128,2048]{1,0:T(8,128)(2,1)} custom-call(bf16[256,768]{1,0:T(8,128)(2,1)S(1)} %select.3.pick_ref, f32[2,128]{1,0:T(2,128)S(1)} %get-tuple-element.32.gates_ref, bf16[768,2048]{1,0:T(8,128)(2,1)S(1)} %bitcast.11), custom_call_target="tpu_custom_call" | custom-call | flops 805306368 | bytes 3145728 | tf_op jit(solution)/shard_map/combine/pallas_call | solution.py:310
  89.1 0.0 collective-permute-done.4.other_ref
  89.2 0.6 loss.1
  (4 shorter events, 0.0 us)
Async XLA Ops:
  1.7 4.5 %collective-permute-start.3 = (f32[8,128]{1,0:T(8,128)S(1)}, f32[8,128]{1,0:T(8,128)S(1)}, u32[]{:S(2)}, u32[]{:S(2)}) collective-permute-start(f32[8,128]{1,0:T(8,128)S(1)} %get-tuple-element.25), channel_id=1, source_target_pairs={{0,16},{1,17},{2,18},{3,19},{4,20},{5,21},{6,22},{7,23},{8,24},{9,... | collective-permute-start | bytes 12296 | tf_op jit(solution)/shard_map/ppermute | solution.py:344
  6.3 4.4 %collective-permute-start = (f32[8,128]{1,0:T(8,128)S(1)}, f32[8,128]{1,0:T(8,128)S(1)}, u32[]{:S(2)}, u32[]{:S(2)}) collective-permute-start(f32[8,128]{1,0:T(8,128)S(1)} %add.11), channel_id=1, source_target_pairs={{16,48},{17,49},{18,50},{19,51},{20,52},{21,53},{22,54},{23,55},{2... | collective-permute-start | bytes 12296 | tf_op jit(solution)/shard_map/cond/branch_1_fun/ppermute | solution.py:325
  10.7 5.2 %collective-permute-start.1 = (f32[8,128]{1,0:T(8,128)S(1)}, f32[8,128]{1,0:T(8,128)S(1)}, u32[]{:S(2)}, u32[]{:S(2)}) collective-permute-start(f32[8,128]{1,0:T(8,128)S(1)} %add.12), channel_id=1, source_target_pairs={{16,80},{17,81},{18,82},{19,83},{20,84},{21,85},{22,86},{23,87},{2... | collective-permute-start | bytes 12296 | tf_op jit(solution)/shard_map/cond/branch_1_fun/ppermute | solution.py:325
  15.9 7.0 %collective-permute-start.2 = (f32[8,128]{1,0:T(8,128)S(1)}, f32[8,128]{1,0:T(8,128)S(1)}, u32[]{:S(2)}, u32[]{:S(2)}) collective-permute-start(f32[8,128]{1,0:T(8,128)S(1)} %add.13), channel_id=1, source_target_pairs={{16,240},{17,241},{18,242},{19,243},{20,244},{21,245},{22,246},{23... | collective-permute-start | bytes 12296 | tf_op jit(solution)/shard_map/cond/branch_1_fun/ppermute | solution.py:325
  23.1 30.3 %copy-start = (bf16[1,2048,768]{2,1,0:T(8,128)(2,1)S(1)}, bf16[1,2048,768]{2,1,0:T(8,128)(2,1)}, u32[]{:S(2)}) copy-start(bf16[1,2048,768]{2,1,0:T(8,128)(2,1)} %gate_ref.1) | copy-start | bytes 9437188
  23.1 30.3 %copy-start.1 = (bf16[1,2048,768]{2,1,0:T(8,128)(2,1)S(1)}, bf16[1,2048,768]{2,1,0:T(8,128)(2,1)}, u32[]{:S(2)}) copy-start(bf16[1,2048,768]{2,1,0:T(8,128)(2,1)} %up_ref.1) | copy-start | bytes 9437188
  53.4 5.1 %copy-start.2 = (bf16[1,768,2048]{2,1,0:T(8,128)(2,1)S(1)}, bf16[1,768,2048]{2,1,0:T(8,128)(2,1)}, u32[]{:S(2)}) copy-start(bf16[1,768,2048]{2,1,0:T(8,128)(2,1)} %down_ref.1) | copy-start | bytes 9437188
  87.4 1.8 %collective-permute-start.4 = (f32[8,128]{1,0:T(8,128)S(1)}, f32[8,128]{1,0:T(8,128)S(1)}, u32[]{:S(2)}, u32[]{:S(2)}) collective-permute-start(f32[8,128]{1,0:T(8,128)S(1)} %read.1.mine_ref), channel_id=1, source_target_pairs={{0,16},{1,17},{2,18},{3,19},{4,20},{5,21},{6,22},{7,23},{8,24},{9,... | collective-permute-start | bytes 12296 | tf_op jit(solution)/shard_map/ppermute | solution.py:362

commit v7 on v6

--- a/solution.py
+++ b/solution.py
@@ -10,18 +10,24 @@
 F32 = jnp.float32
 BF16 = jnp.bfloat16
 PARTS = 4
+ROUNDS = (
+    (1, 0, 3, 2, 5, 4, 7, 6),
+    (2, 3, 0, 1, 6, 7, 4, 5),
+    (6, 7, 4, 5, 2, 3, 0, 1),
+)
 AXES = ("dp", "expert")
 
 
-def slots_of(ids, cap):
+def slots_of(ids, experts, cap):
     toks = ids.shape[1]
-    labels = lax.broadcasted_iota(jnp.int32, (toks, toks), 0)
-    lanes = lax.broadcasted_iota(jnp.int32, (toks, toks), 1)
+    labels = lax.broadcasted_iota(jnp.int32, (experts, toks), 0)
     first = (labels == ids[0:1, :]).astype(F32)
     second = (labels == ids[1:2, :]).astype(F32)
-    earlier = (labels < lanes).astype(F32).astype(BF16)
-    first_rank = jnp.dot(first.astype(BF16), earlier, preferred_element_type=F32)
-    second_rank = jnp.dot(second.astype(BF16), earlier, preferred_element_type=F32)
+    before = lax.broadcasted_iota(jnp.int32, (toks, toks), 0)
+    earlier = (before < lax.broadcasted_iota(jnp.int32, (toks, toks), 1)).astype(F32).astype(BF16)
+    both = jnp.concatenate([first, second], 0).astype(BF16)
+    rank = jnp.dot(both, earlier, preferred_element_type=F32)
+    first_rank, second_rank = rank[:experts], rank[experts:]
     first_count = jnp.sum(first, 1, keepdims=True)
     base = ids.astype(F32) * cap
     first_slot = base[0:1, :] + jnp.sum(first * first_rank, 0, keepdims=True)
@@ -40,15 +46,17 @@
     gates_copy.start()
     tok_copy.start()
     ids_copy.wait()
-    first_slot, second_slot, first, second = slots_of(ids_ref[...], cap)
+    first_slot, second_slot, first, second = slots_of(ids_ref[...], experts, cap)
     count = jnp.sum(first + second, 1, keepdims=True)
     gates_copy.wait()
     gates = gates_ref[...]
     mass = jnp.sum(first * gates[0:1, :] + second * gates[1:2, :], 1, keepdims=True)
-    lanes = lax.broadcasted_iota(jnp.int32, (toks, toks), 1)
-    stats = jnp.where(lanes == 0, count, jnp.where(lanes == 1, mass, 0.0)).T[:8, :]
+    lanes = lax.broadcasted_iota(jnp.int32, (experts, toks), 1)
+    stats = jnp.where(lanes == 0, count, jnp.where(lanes == 1, mass, 0.0))
+    stats = jnp.concatenate([stats, jnp.zeros((toks - experts, toks), F32)], 0).T[:8, :]
     stats_ref[...] = stats
-    lane, line = lanes[:8, :], lax.broadcasted_iota(jnp.int32, (8, toks), 0)
+    lane = lax.broadcasted_iota(jnp.int32, (8, toks), 1)
+    line = lax.broadcasted_iota(jnp.int32, (8, toks), 0)
     free = ((stats[0:1, :] < cap) & (lane < experts)).astype(jnp.int32)
     slots = jnp.where(line == 0, first_slot.astype(jnp.int32), second_slot.astype(jnp.int32))
     slot_ref[...] = jnp.where(line < 2, slots, free)
@@ -184,14 +192,14 @@
     )(x, w_gate, w_up)
 
 
-def down_kernel(cap, mine_ref, slot_ref, loss_ref, x_ref, down_ref, out_ref):
+def down_kernel(cap, slot_ref, loss_ref, x_ref, down_ref, out_ref):
     for start in range(0, x_ref.shape[0], 256):
         tile = slice(start, start + 256)
         out_ref[tile, :] = jnp.dot(
             x_ref[tile, :], down_ref[0], preferred_element_type=F32
         ).astype(BF16)
     row = lax.broadcasted_iota(jnp.int32, (16, 128), 0)
-    here = (row == 15) & is_free(slot_ref, mine_ref[0])
+    here = (row == 15) & is_free(slot_ref, lax.axis_index("expert"))
     line = jnp.broadcast_to(loss_ref[0:1, :], (16, 128))
     for end in range(cap, x_ref.shape[0] + 1, cap):
         tile = slice(end - 16, end)
@@ -199,13 +207,13 @@
         out_ref[tile, 0:128] = jnp.where(here, line, old).astype(BF16)
 
 
-def down_of(mine, slots, loss, x, w_down, cap):
+def down_of(slots, loss, x, w_down, cap):
     rows, middle = x.shape
     width = w_down.shape[2]
     held = pl.BlockSpec(memory_space=pltpu.VMEM)
     return pl.pallas_call(
         functools.partial(down_kernel, cap),
-        in_specs=[pl.BlockSpec(memory_space=pltpu.SMEM)] + [held] * 4,
+        in_specs=[held] * 4,
         out_specs=held,
         out_shape=jax.ShapeDtypeStruct((rows, width), BF16),
         compiler_params=pltpu.CompilerParams(vmem_limit_bytes=16 * 2**20),
@@ -215,7 +223,7 @@
             transcendentals=0,
         ),
         name="down",
-    )(mine, slots, loss, x, w_down)
+    )(slots, loss, x, w_down)
 
 
 def select_kernel(slot_ref, pick_ref):
@@ -264,23 +272,24 @@
     )(slots, rows)
 
 
-def loss_kernel(late_ref, mine_ref, other_ref, out_ref):
+def loss_kernel(mine_ref, other_ref, out_ref):
     lane = lax.broadcasted_iota(jnp.int32, (1, 128), 1)
-    line = jnp.where(late_ref[0] > 0, mine_ref[0:1, :], other_ref[0:1, :])
+    late = lax.axis_index("dp") % 2 == 1
+    line = jnp.where(late, mine_ref[0:1, :], other_ref[0:1, :])
     out_ref[0, 0] = jnp.sum(jnp.where(lane < 3, line, 0.0))
 
 
-def loss_of(late, mine, other):
+def loss_of(mine, other):
     held = pl.BlockSpec(memory_space=pltpu.VMEM)
     far = pl.BlockSpec(memory_space=pltpu.SMEM)
     return pl.pallas_call(
         loss_kernel,
-        in_specs=[far, held, held],
+        in_specs=[held] * 2,
         out_specs=far,
         out_shape=jax.ShapeDtypeStruct((1, 1), F32),
         compiler_params=pltpu.CompilerParams(vmem_limit_bytes=2**20),
         name="loss",
-    )(late, mine, other)
+    )(mine, other)
 
 
 def combine_kernel(pick_ref, gates_ref, rows_ref, out_hbm, out_ref, sems):
@@ -321,8 +330,12 @@
     )(pick, gates, rows)
 
 
-def add_round(value, size, flip, step):
-    return value + lax.ppermute(value, AXES, [(i, i ^ flip) for i in range(size) if (i // step) % 2 == 1])
+def add_round(value, size, step, partner):
+    stride = 2 * step
+    pairs = [
+        (i, partner[i // stride] * stride + i % stride) for i in range(size) if (i // step) % 2 == 1
+    ]
+    return value + lax.ppermute(value, AXES, pairs)
 
 
 def on_device(tokens, expert_ids, gate_weights, w_gate, w_up, w_down):
@@ -335,34 +348,32 @@
     all_tokens = toks * group * copies
 
     size = copies * group
-    stride = 2 * group
     ids, gates = expert_ids.T, gate_weights.T
     slots, stats, tokens, gates = count(ids, gates, tokens, experts, cap)
     swap = [(i, i + group if (i // group) % 2 == 0 else i - group) for i in range(size)]
     late = lax.axis_index("dp") % 2
-    mine = lax.axis_index("expert").reshape(1)
     other = lax.ppermute(stats, AXES, swap)
     outgoing = pack(slots, tokens, experts * cap)
     pick = select(slots, experts * cap)
 
     def column_sum(value, other):
         value = value + other
-        for flip in (1, 2, 7):
-            value = add_round(value, size, flip * stride, group)
+        for partner in ROUNDS:
+            value = add_round(value, size, group, partner)
         return value
 
     stats = lax.cond(late == 1, column_sum, lambda value, other: value, stats, other)
     outgoing = note(slots, stats, outgoing, experts, cap)
-    late, mine, pick, outgoing = lax.optimization_barrier((late.reshape(1), mine, pick, outgoing))
+    pick, outgoing = lax.optimization_barrier((pick, outgoing))
     received = lax.all_to_all(outgoing, "expert", split_axis=0, concat_axis=0, tiled=True)
     hidden, loss = hidden_of(received, w_gate, w_up, experts, cap, all_tokens)
-    result = down_of(mine, slots, loss, hidden, w_down, cap)
+    result = down_of(slots, loss, hidden, w_down, cap)
     returned = lax.all_to_all(result, "expert", split_axis=0, concat_axis=0, tiled=True)
     loss = read(slots, returned, cap)
     other = lax.ppermute(loss, AXES, swap)
     mixed = combine(pick, gates, returned)
     other, mixed = lax.optimization_barrier((other, mixed))
-    return mixed, loss_of(late, loss, other).reshape(())
+    return mixed, loss_of(loss, other).reshape(())
 
 
 def solution(mesh):

time: 91.2 us -> 90.7 us (level)
  no operation moved by 1% of the time
where the time goes in v7:
time: 90.7 us; the launch traced here: 90 us
  blocking collectives  56.2 us (62%)
  starting transfers between devices  14.8 us (16%)
  Pallas kernels  12.6 us (14%)
  waiting for transfers between devices  5.6 us (6%)
    all_to_all x1, blocking collectives, on_device(): lax.all_to_all(outgoing, 'expert', split_axis=0, concat_axis=0, tiled=True)  30.3 us
    all_to_all x1, blocking collectives, on_device(): lax.all_to_all(result, 'expert', split_axis=0, concat_axis=0, tiled=True)  25.9 us
    ppermute x3, starting transfers between devices, add_round(): return value + lax.ppermute(value, AXES, pairs)  11.4 us
    ppermute x3, waiting for transfers between devices, add_round(): return value + lax.ppermute(value, AXES, pairs)  5.59 us
    pallas_call x1, Pallas kernels, hidden_of(): pl.pallas_call(functools.partial(hidden_kernel, experts, cap, tokens), in...  5.08 us
    ppermute x1, starting transfers between devices, on_device(): other = lax.ppermute(stats, AXES, swap)  3.33 us
    pallas_call x1, Pallas kernels, down_of(): pl.pallas_call(functools.partial(down_kernel, cap), in_specs=[held] * 4,...  2.63 us
  transfers between devices with their start and end apart: 5, of which 3 were waited for; matrix products, arithmetic and copies ran while one was open for 0% of the time, Pallas kernels for 3%

profile of v7, /device:TPU:1, one launch (start us, length us, event | category | flops | bytes accessed | tf_op | source)
XLA Modules:
  0.0 90.0 jit_solution(16783559819727757029)
XLA Ops:
  0.6 1.1 %count.1 = (s32[8,128]{1,0:T(8,128)S(1)}, f32[8,128]{1,0:T(8,128)S(1)}, bf16[128,2048]{1,0:T(8,128)(2,1)S(1)}, f32[2,128]{1,0:T(2,128)S(1)}) custom-call(s32[2,128]{1,0:T(2,128)} %bitcast.12, f32[2,128]{1,0:T(2,128)} %bitcast.13, bf16[128,2048]{1,0:T(8,128)(2,1)} %tok_hbm.1), custom_call_target="tpu_custom_call" | custom-call | flops 8388608 | bytes 1024 | tf_op jit(solution)/shard_map/count/pallas_call | solution.py:68
  1.7 3.3 %collective-permute-start.3 = (f32[8,128]{1,0:T(8,128)S(1)}, f32[8,128]{1,0:T(8,128)S(1)}, u32[]{:S(2)}, u32[]{:S(2)}) collective-permute-start(f32[8,128]{1,0:T(8,128)S(1)} %get-tuple-element.23), channel_id=1, source_target_pairs={{0,16},{1,17},{2,18},{3,19},{4,20},{5,21},{6,22},{7,23},{8,24},{9,... | collective-permute-start | bytes 12296 | tf_op jit(solution)/shard_map/ppermute | solution.py:355
  5.1 1.0 %pack.1.in_ref = bf16[768,2048]{1,0:T(8,128)(2,1)S(1)} custom-call(s32[8,128]{1,0:T(8,128)S(1)} %get-tuple-element.22.slot_ref, bf16[128,2048]{1,0:T(8,128)(2,1)S(1)} %get-tuple-element.24.tok_ref), custom_call_target="tpu_custom_call" | custom-call | flops 402653184 | bytes 6291456 | tf_op jit(solution)/shard_map/pack/pallas_call | solution.py:112
  6.0 0.2 select.3.pick_ref
  6.3 0.0 collective-permute-done.3
  6.3 17.1 %conditional.1 = (f32[8,128]{1,0:T(8,128)S(1)}) conditional(s32[]{:T(128)} %convert_element_type.3, f32[8,128]{1,0:T(8,128)S(1)} %get-tuple-element.23, (f32[8,128]{1,0:T(8,128)S(1)}, f32[8,128]{1,0:T(8,128)S(1)}) %tuple.16), branch_computations={%region_0.1_spmd, %region_1.2_spmd} | conditional | flops 4096 | bytes 98432 | solution.py:365
  6.3 1.9 %collective-permute-start = (f32[8,128]{1,0:T(8,128)S(1)}, f32[8,128]{1,0:T(8,128)S(1)}, u32[]{:S(2)}, u32[]{:S(2)}) collective-permute-start(f32[8,128]{1,0:T(8,128)S(1)} %add.11), channel_id=1, source_target_pairs={{16,48},{17,49},{18,50},{19,51},{20,52},{21,53},{22,54},{23,55},{2... | collective-permute-start | bytes 12296 | tf_op jit(solution)/shard_map/cond/branch_1_fun/ppermute | solution.py:338
  8.2 2.4 %collective-permute-done = f32[8,128]{1,0:T(8,128)S(1)} collective-permute-done((f32[8,128]{1,0:T(8,128)S(1)}, f32[8,128]{1,0:T(8,128)S(1)}, u32[]{:S(2)}, u32[]{:S(2)}) %collective-permute-start) | collective-permute-done | bytes 4128 | tf_op jit(solution)/shard_map/cond/branch_1_fun/ppermute | solution.py:338
  10.7 3.3 %collective-permute-start.1 = (f32[8,128]{1,0:T(8,128)S(1)}, f32[8,128]{1,0:T(8,128)S(1)}, u32[]{:S(2)}, u32[]{:S(2)}) collective-permute-start(f32[8,128]{1,0:T(8,128)S(1)} %add.12), channel_id=1, source_target_pairs={{16,80},{17,81},{18,82},{19,83},{20,84},{21,85},{22,86},{23,87},{2... | collective-permute-start | bytes 12296 | tf_op jit(solution)/shard_map/cond/branch_1_fun/ppermute | solution.py:338
  14.0 1.9 %collective-permute-done.1 = f32[8,128]{1,0:T(8,128)S(1)} collective-permute-done((f32[8,128]{1,0:T(8,128)S(1)}, f32[8,128]{1,0:T(8,128)S(1)}, u32[]{:S(2)}, u32[]{:S(2)}) %collective-permute-start.1) | collective-permute-done | bytes 4128 | tf_op jit(solution)/shard_map/cond/branch_1_fun/ppermute | solution.py:338
  15.9 6.2 %collective-permute-start.2 = (f32[8,128]{1,0:T(8,128)S(1)}, f32[8,128]{1,0:T(8,128)S(1)}, u32[]{:S(2)}, u32[]{:S(2)}) collective-permute-start(f32[8,128]{1,0:T(8,128)S(1)} %add.13), channel_id=1, source_target_pairs={{16,208},{17,209},{18,210},{19,211},{20,212},{21,213},{22,214},{23... | collective-permute-start | bytes 12296 | tf_op jit(solution)/shard_map/cond/branch_1_fun/ppermute | solution.py:338
  22.1 1.3 %collective-permute-done.2 = f32[8,128]{1,0:T(8,128)S(1)} collective-permute-done((f32[8,128]{1,0:T(8,128)S(1)}, f32[8,128]{1,0:T(8,128)S(1)}, u32[]{:S(2)}, u32[]{:S(2)}) %collective-permute-start.2) | collective-permute-done | bytes 4128 | tf_op jit(solution)/shard_map/cond/branch_1_fun/ppermute | solution.py:338
  23.4 0.1 note.1
  23.5 0.0 copy-start
  23.6 0.0 copy-start.1
  23.6 30.3 %all_to_all.22 = bf16[16,48,2048]{2,1,0:T(8,128)(2,1)S(1)} all-to-all(bf16[16,48,2048]{2,1,0:T(8,128)(2,1)S(1)} %bitcast.7), channel_id=1, replica_groups=mesh['dp'=16,'expert'=16] {'expert'}, dimensions={0} | all-to-all | bytes 6291456 | tf_op jit(solution)/shard_map/all_to_all | solution.py:368
  53.9 0.0 copy-done
  53.9 0.0 copy-done.1
  53.9 0.0 copy-start.2
  53.9 5.1 %hidden.1 = (bf16[768,768]{1,0:T(8,128)(2,1)S(1)}, f32[8,128]{1,0:T(8,128)S(1)}) custom-call(bf16[768,2048]{1,0:T(8,128)(2,1)S(1)} %bitcast.10, bf16[1,2048,768]{2,1,0:T(8,128)(2,1)S(1)} %copy-done, bf16[1,2048,768]{2,1,0:T(8,128)(2,1)S(1)} %copy-done.1), custom_call_target="tpu_custom_call" | custom-call | flops 4831838208 | bytes 9437184 | tf_op jit(solution)/shard_map/hidden/pallas_call | solution.py:180
  58.9 0.0 copy-done.2
  59.0 2.6 %down.1 = bf16[768,2048]{1,0:T(8,128)(2,1)S(1)} custom-call(s32[8,128]{1,0:T(8,128)S(1)} %get-tuple-element.22.slot_ref, f32[8,128]{1,0:T(8,128)S(1)} %get-tuple-element.26.loss_ref, bf16[768,768]{1,0:T(8,128)(2,1)S(1)} %get-tuple-element.27.x_ref, bf16[1,768,2048]{2,1,0:T(8,128)(2,1)S(1)} %copy-done.2), custom_call_target="tpu_custom_call" | custom-call | flops 2415919104 | bytes 6291456 | tf_op jit(solution)/shard_map/down/pallas_call | solution.py:214
  61.6 25.9 %all_to_all.23 = bf16[16,48,2048]{2,1,0:T(8,128)(2,1)S(1)} all-to-all(bf16[16,48,2048]{2,1,0:T(8,128)(2,1)S(1)} %bitcast.11), channel_id=1, replica_groups=mesh['dp'=16,'expert'=16] {'expert'}, dimensions={0} | all-to-all | bytes 6291456 | tf_op jit(solution)/shard_map/all_to_all | solution.py:371
  87.5 0.1 read.1.mine_ref
  87.6 0.0 collective-permute-start.4
  87.6 1.7 %combine.1 = bf16[128,2048]{1,0:T(8,128)(2,1)} custom-call(bf16[256,768]{1,0:T(8,128)(2,1)S(1)} %select.3.pick_ref, f32[2,128]{1,0:T(2,128)S(1)} %get-tuple-element.29.gates_ref, bf16[768,2048]{1,0:T(8,128)(2,1)S(1)} %bitcast.9), custom_call_target="tpu_custom_call" | custom-call | flops 805306368 | bytes 3145728 | tf_op jit(solution)/shard_map/combine/pallas_call | solution.py:319
  89.4 0.0 collective-permute-done.4.other_ref
  89.4 0.7 loss.1
  (4 shorter events, 0.0 us)
Async XLA Ops:
  1.7 4.5 %collective-permute-start.3 = (f32[8,128]{1,0:T(8,128)S(1)}, f32[8,128]{1,0:T(8,128)S(1)}, u32[]{:S(2)}, u32[]{:S(2)}) collective-permute-start(f32[8,128]{1,0:T(8,128)S(1)} %get-tuple-element.23), channel_id=1, source_target_pairs={{0,16},{1,17},{2,18},{3,19},{4,20},{5,21},{6,22},{7,23},{8,24},{9,... | collective-permute-start | bytes 12296 | tf_op jit(solution)/shard_map/ppermute | solution.py:355
  6.3 4.4 %collective-permute-start = (f32[8,128]{1,0:T(8,128)S(1)}, f32[8,128]{1,0:T(8,128)S(1)}, u32[]{:S(2)}, u32[]{:S(2)}) collective-permute-start(f32[8,128]{1,0:T(8,128)S(1)} %add.11), channel_id=1, source_target_pairs={{16,48},{17,49},{18,50},{19,51},{20,52},{21,53},{22,54},{23,55},{2... | collective-permute-start | bytes 12296 | tf_op jit(solution)/shard_map/cond/branch_1_fun/ppermute | solution.py:338
  10.7 5.2 %collective-permute-start.1 = (f32[8,128]{1,0:T(8,128)S(1)}, f32[8,128]{1,0:T(8,128)S(1)}, u32[]{:S(2)}, u32[]{:S(2)}) collective-permute-start(f32[8,128]{1,0:T(8,128)S(1)} %add.12), channel_id=1, source_target_pairs={{16,80},{17,81},{18,82},{19,83},{20,84},{21,85},{22,86},{23,87},{2... | collective-permute-start | bytes 12296 | tf_op jit(solution)/shard_map/cond/branch_1_fun/ppermute | solution.py:338
  15.9 7.5 %collective-permute-start.2 = (f32[8,128]{1,0:T(8,128)S(1)}, f32[8,128]{1,0:T(8,128)S(1)}, u32[]{:S(2)}, u32[]{:S(2)}) collective-permute-start(f32[8,128]{1,0:T(8,128)S(1)} %add.13), channel_id=1, source_target_pairs={{16,208},{17,209},{18,210},{19,211},{20,212},{21,213},{22,214},{23... | collective-permute-start | bytes 12296 | tf_op jit(solution)/shard_map/cond/branch_1_fun/ppermute | solution.py:338
  23.5 30.3 %copy-start = (bf16[1,2048,768]{2,1,0:T(8,128)(2,1)S(1)}, bf16[1,2048,768]{2,1,0:T(8,128)(2,1)}, u32[]{:S(2)}) copy-start(bf16[1,2048,768]{2,1,0:T(8,128)(2,1)} %gate_ref.1) | copy-start | bytes 9437188
  23.6 30.3 %copy-start.1 = (bf16[1,2048,768]{2,1,0:T(8,128)(2,1)S(1)}, bf16[1,2048,768]{2,1,0:T(8,128)(2,1)}, u32[]{:S(2)}) copy-start(bf16[1,2048,768]{2,1,0:T(8,128)(2,1)} %up_ref.1) | copy-start | bytes 9437188
  53.9 5.1 %copy-start.2 = (bf16[1,768,2048]{2,1,0:T(8,128)(2,1)S(1)}, bf16[1,768,2048]{2,1,0:T(8,128)(2,1)}, u32[]{:S(2)}) copy-start(bf16[1,768,2048]{2,1,0:T(8,128)(2,1)} %down_ref.1) | copy-start | bytes 9437188
  87.6 1.8 %collective-permute-start.4 = (f32[8,128]{1,0:T(8,128)S(1)}, f32[8,128]{1,0:T(8,128)S(1)}, u32[]{:S(2)}, u32[]{:S(2)}) collective-permute-start(f32[8,128]{1,0:T(8,128)S(1)} %read.1.mine_ref), channel_id=1, source_target_pairs={{0,16},{1,17},{2,18},{3,19},{4,20},{5,21},{6,22},{7,23},{8,24},{9,... | collective-permute-start | bytes 12296 | tf_op jit(solution)/shard_map/ppermute | solution.py:373

commit v8 on v7

--- a/solution.py
+++ b/solution.py
@@ -153,7 +153,7 @@
     )(slots, sums, rows)
 
 
-def hidden_kernel(experts, cap, tokens, x_ref, gate_ref, up_ref, out_ref, loss_ref):
+def hidden_kernel(experts, cap, tokens, slot_ref, x_ref, gate_ref, up_ref, out_ref, loss_ref, few_ref):
     lanes = loss_ref.shape[1]
     total = jnp.zeros((16, 5 * lanes), F32)
     for end in range(cap, x_ref.shape[0] + 1, cap):
@@ -165,23 +165,44 @@
     high, middle, low = pieces(loss, 3)
     line = jnp.where(lane == 0, high, jnp.where(lane == 1, middle, jnp.where(lane == 2, low, 0.0)))
     loss_ref[...] = line
-    x = x_ref[...]
-    for start in range(0, out_ref.shape[1], 256):
-        tile = slice(start, start + 256)
-        gate = jnp.dot(x, gate_ref[0, :, tile], preferred_element_type=F32)
-        up = jnp.dot(x, up_ref[0, :, tile], preferred_element_type=F32)
-        out_ref[:, tile] = (gate / (1.0 + jnp.exp(-gate)) * up).astype(BF16)
-
-
-def hidden_of(x, w_gate, w_up, experts, cap, tokens):
+
+    def run(rows_ref):
+        rows = rows_ref.shape[0]
+        x = rows_ref[...]
+        for start in range(0, out_ref.shape[1], 256):
+            tile = slice(start, start + 256)
+            gate = jnp.dot(x, gate_ref[0, :, tile], preferred_element_type=F32)
+            up = jnp.dot(x, up_ref[0, :, tile], preferred_element_type=F32)
+            out_ref[:rows, tile] = (gate / (1.0 + jnp.exp(-gate)) * up).astype(BF16)
+
+    free = mine_free(slot_ref)
+
+    @pl.when(free)
+    def _():
+        for chunk in range(x_ref.shape[0] // cap):
+            few_ref[chunk * 16 : chunk * 16 + 16, :] = x_ref[chunk * cap : chunk * cap + 16, :]
+        run(few_ref)
+
+    @pl.when(jnp.logical_not(free))
+    def _():
+        run(x_ref)
+
+
+def mine_free(slot_ref):
+    lane = lax.broadcasted_iota(jnp.int32, (1, slot_ref.shape[1]), 1)
+    return jnp.sum(jnp.where(lane == lax.axis_index("expert"), slot_ref[2:3, :], 0)) > 0
+
+
+def hidden_of(slots, x, w_gate, w_up, experts, cap, tokens):
     rows, width = x.shape
     middle = w_gate.shape[2]
     held = pl.BlockSpec(memory_space=pltpu.VMEM)
     return pl.pallas_call(
         functools.partial(hidden_kernel, experts, cap, tokens),
-        in_specs=[held] * 3,
+        in_specs=[held] * 4,
         out_specs=[held] * 2,
         out_shape=[jax.ShapeDtypeStruct((rows, middle), BF16), jax.ShapeDtypeStruct((8, 128), F32)],
+        scratch_shapes=[pltpu.VMEM((rows // cap * 16, width), BF16)],
         compiler_params=pltpu.CompilerParams(vmem_limit_bytes=16 * 2**20),
         cost_estimate=pl.CostEstimate(
             flops=4 * rows * width * middle,
@@ -189,22 +210,34 @@
             transcendentals=rows * middle,
         ),
         name="hidden",
-    )(x, w_gate, w_up)
+    )(slots, x, w_gate, w_up)
 
 
 def down_kernel(cap, slot_ref, loss_ref, x_ref, down_ref, out_ref):
-    for start in range(0, x_ref.shape[0], 256):
-        tile = slice(start, start + 256)
-        out_ref[tile, :] = jnp.dot(
-            x_ref[tile, :], down_ref[0], preferred_element_type=F32
-        ).astype(BF16)
-    row = lax.broadcasted_iota(jnp.int32, (16, 128), 0)
-    here = (row == 15) & is_free(slot_ref, lax.axis_index("expert"))
-    line = jnp.broadcast_to(loss_ref[0:1, :], (16, 128))
-    for end in range(cap, x_ref.shape[0] + 1, cap):
-        tile = slice(end - 16, end)
-        old = out_ref[tile, 0:128].astype(F32)
-        out_ref[tile, 0:128] = jnp.where(here, line, old).astype(BF16)
+    chunks = x_ref.shape[0] // cap
+    free = mine_free(slot_ref)
+
+    @pl.when(free)
+    def _():
+        few = chunks * 16
+        rows = jnp.dot(x_ref[:few, :], down_ref[0], preferred_element_type=F32).astype(BF16)
+        rest = jnp.zeros((cap - 16, out_ref.shape[1]), BF16)
+        last = lax.broadcasted_iota(jnp.int32, (16, 128), 0) == 15
+        line = jnp.broadcast_to(loss_ref[0:1, :], (16, 128))
+        line = jnp.where(last, line, 0.0).astype(BF16)
+        for chunk in range(chunks):
+            start = chunk * cap
+            out_ref[start : start + 16, :] = rows[chunk * 16 : chunk * 16 + 16, :]
+            out_ref[start + 16 : start + cap, :] = rest
+            out_ref[start + cap - 16 : start + cap, 0:128] = line
+
+    @pl.when(jnp.logical_not(free))
+    def _():
+        for start in range(0, x_ref.shape[0], 256):
+            tile = slice(start, start + 256)
+            out_ref[tile, :] = jnp.dot(
+                x_ref[tile, :], down_ref[0], preferred_element_type=F32
+            ).astype(BF16)
 
 
 def down_of(slots, loss, x, w_down, cap):
@@ -366,7 +399,7 @@
     outgoing = note(slots, stats, outgoing, experts, cap)
     pick, outgoing = lax.optimization_barrier((pick, outgoing))
     received = lax.all_to_all(outgoing, "expert", split_axis=0, concat_axis=0, tiled=True)
-    hidden, loss = hidden_of(received, w_gate, w_up, experts, cap, all_tokens)
+    hidden, loss = hidden_of(slots, received, w_gate, w_up, experts, cap, all_tokens)
     result = down_of(slots, loss, hidden, w_down, cap)
     returned = lax.all_to_all(result, "expert", split_axis=0, concat_axis=0, tiled=True)
     loss = read(slots, returned, cap)

time: 90.7 us -> 90.5 us (level)
  blocking collectives: 56.2 us -> 61.1 us
  Pallas kernels: 12.6 us -> 7.95 us
    all_to_all x1, blocking collectives: 25.9 us -> 30.9 us  [on_device(): lax.all_to_all(result, 'expert', split_axis=0, concat_axis=0, tiled=True)]
    pallas_call x1, Pallas kernels: 5.08 us -> 1.96 us  [hidden_of(): pl.pallas_call(functools.partial(hidden_kernel, experts, cap, tokens), in...]
    pallas_call x1, Pallas kernels: 2.63 us -> 1.11 us  [down_of(): pl.pallas_call(functools.partial(down_kernel, cap), in_specs=[held] * 4,...]
where the time goes in v8:
time: 90.5 us; the launch traced here: 90.2 us
  blocking collectives  61.1 us (68%)
  starting transfers between devices  14.8 us (16%)
  Pallas kernels  7.95 us (9%)
  waiting for transfers between devices  5.6 us (6%)
    all_to_all x1, blocking collectives, on_device(): lax.all_to_all(result, 'expert', split_axis=0, concat_axis=0, tiled=True)  30.9 us
    all_to_all x1, blocking collectives, on_device(): lax.all_to_all(outgoing, 'expert', split_axis=0, concat_axis=0, tiled=True)  30.2 us
    ppermute x3, starting transfers between devices, add_round(): return value + lax.ppermute(value, AXES, pairs)  11.4 us
    ppermute x3, waiting for transfers between devices, add_round(): return value + lax.ppermute(value, AXES, pairs)  5.59 us
    ppermute x1, starting transfers between devices, on_device(): other = lax.ppermute(stats, AXES, swap)  3.33 us
    pallas_call x1, Pallas kernels, hidden_of(): pl.pallas_call(functools.partial(hidden_kernel, experts, cap, tokens), in...  1.96 us
  transfers between devices with their start and end apart: 5, of which 3 were waited for; matrix products, arithmetic and copies ran while one was open for 0% of the time, Pallas kernels for 3%

profile of v8, /device:TPU:1, one launch (start us, length us, event | category | flops | bytes accessed | tf_op | source)
XLA Modules:
  0.0 90.2 jit_solution(11962648736335669114)
XLA Ops:
  0.6 1.1 %count.1 = (s32[8,128]{1,0:T(8,128)S(1)}, f32[8,128]{1,0:T(8,128)S(1)}, bf16[128,2048]{1,0:T(8,128)(2,1)S(1)}, f32[2,128]{1,0:T(2,128)S(1)}) custom-call(s32[2,128]{1,0:T(2,128)} %bitcast.12, f32[2,128]{1,0:T(2,128)} %bitcast.13, bf16[128,2048]{1,0:T(8,128)(2,1)} %tok_hbm.1), custom_call_target="tpu_custom_call" | custom-call | flops 8388608 | bytes 1024 | tf_op jit(solution)/shard_map/count/pallas_call | solution.py:68
  1.7 3.3 %collective-permute-start.3 = (f32[8,128]{1,0:T(8,128)S(1)}, f32[8,128]{1,0:T(8,128)S(1)}, u32[]{:S(2)}, u32[]{:S(2)}) collective-permute-start(f32[8,128]{1,0:T(8,128)S(1)} %get-tuple-element.23), channel_id=1, source_target_pairs={{0,16},{1,17},{2,18},{3,19},{4,20},{5,21},{6,22},{7,23},{8,24},{9,... | collective-permute-start | bytes 12296 | tf_op jit(solution)/shard_map/ppermute | solution.py:388
  5.1 1.0 %pack.1.in_ref = bf16[768,2048]{1,0:T(8,128)(2,1)S(1)} custom-call(s32[8,128]{1,0:T(8,128)S(1)} %get-tuple-element.22.slot_ref, bf16[128,2048]{1,0:T(8,128)(2,1)S(1)} %get-tuple-element.24.tok_ref), custom_call_target="tpu_custom_call" | custom-call | flops 402653184 | bytes 6291456 | tf_op jit(solution)/shard_map/pack/pallas_call | solution.py:112
  6.0 0.2 select.3.pick_ref
  6.3 0.0 collective-permute-done.3
  6.3 17.1 %conditional.1 = (f32[8,128]{1,0:T(8,128)S(1)}) conditional(s32[]{:T(128)} %convert_element_type.3, f32[8,128]{1,0:T(8,128)S(1)} %get-tuple-element.23, (f32[8,128]{1,0:T(8,128)S(1)}, f32[8,128]{1,0:T(8,128)S(1)}) %tuple.16), branch_computations={%region_0.1_spmd, %region_1.2_spmd} | conditional | flops 4096 | bytes 98432 | solution.py:398
  6.3 1.9 %collective-permute-start = (f32[8,128]{1,0:T(8,128)S(1)}, f32[8,128]{1,0:T(8,128)S(1)}, u32[]{:S(2)}, u32[]{:S(2)}) collective-permute-start(f32[8,128]{1,0:T(8,128)S(1)} %add.11), channel_id=1, source_target_pairs={{16,48},{17,49},{18,50},{19,51},{20,52},{21,53},{22,54},{23,55},{2... | collective-permute-start | bytes 12296 | tf_op jit(solution)/shard_map/cond/branch_1_fun/ppermute | solution.py:371
  8.2 2.4 %collective-permute-done = f32[8,128]{1,0:T(8,128)S(1)} collective-permute-done((f32[8,128]{1,0:T(8,128)S(1)}, f32[8,128]{1,0:T(8,128)S(1)}, u32[]{:S(2)}, u32[]{:S(2)}) %collective-permute-start) | collective-permute-done | bytes 4128 | tf_op jit(solution)/shard_map/cond/branch_1_fun/ppermute | solution.py:371
  10.7 3.3 %collective-permute-start.1 = (f32[8,128]{1,0:T(8,128)S(1)}, f32[8,128]{1,0:T(8,128)S(1)}, u32[]{:S(2)}, u32[]{:S(2)}) collective-permute-start(f32[8,128]{1,0:T(8,128)S(1)} %add.12), channel_id=1, source_target_pairs={{16,80},{17,81},{18,82},{19,83},{20,84},{21,85},{22,86},{23,87},{2... | collective-permute-start | bytes 12296 | tf_op jit(solution)/shard_map/cond/branch_1_fun/ppermute | solution.py:371
  14.0 1.9 %collective-permute-done.1 = f32[8,128]{1,0:T(8,128)S(1)} collective-permute-done((f32[8,128]{1,0:T(8,128)S(1)}, f32[8,128]{1,0:T(8,128)S(1)}, u32[]{:S(2)}, u32[]{:S(2)}) %collective-permute-start.1) | collective-permute-done | bytes 4128 | tf_op jit(solution)/shard_map/cond/branch_1_fun/ppermute | solution.py:371
  15.9 6.2 %collective-permute-start.2 = (f32[8,128]{1,0:T(8,128)S(1)}, f32[8,128]{1,0:T(8,128)S(1)}, u32[]{:S(2)}, u32[]{:S(2)}) collective-permute-start(f32[8,128]{1,0:T(8,128)S(1)} %add.13), channel_id=1, source_target_pairs={{16,208},{17,209},{18,210},{19,211},{20,212},{21,213},{22,214},{23... | collective-permute-start | bytes 12296 | tf_op jit(solution)/shard_map/cond/branch_1_fun/ppermute | solution.py:371
  22.1 1.3 %collective-permute-done.2 = f32[8,128]{1,0:T(8,128)S(1)} collective-permute-done((f32[8,128]{1,0:T(8,128)S(1)}, f32[8,128]{1,0:T(8,128)S(1)}, u32[]{:S(2)}, u32[]{:S(2)}) %collective-permute-start.2) | collective-permute-done | bytes 4128 | tf_op jit(solution)/shard_map/cond/branch_1_fun/ppermute | solution.py:371
  23.4 0.1 note.1
  23.5 0.0 copy-start
  23.6 0.0 copy-start.1
  23.6 30.2 %all_to_all.22 = bf16[16,48,2048]{2,1,0:T(8,128)(2,1)S(1)} all-to-all(bf16[16,48,2048]{2,1,0:T(8,128)(2,1)S(1)} %bitcast.7), channel_id=1, replica_groups=mesh['dp'=16,'expert'=16] {'expert'}, dimensions={0} | all-to-all | bytes 6291456 | tf_op jit(solution)/shard_map/all_to_all | solution.py:401
  53.8 0.0 copy-done
  53.8 0.0 copy-done.1
  53.8 0.0 copy-start.2
  53.8 2.0 %hidden.1 = (bf16[768,768]{1,0:T(8,128)(2,1)S(1)}, f32[8,128]{1,0:T(8,128)S(1)}) custom-call(s32[8,128]{1,0:T(8,128)S(1)} %get-tuple-element.22.slot_ref, bf16[768,2048]{1,0:T(8,128)(2,1)S(1)} %bitcast.10, bf16[1,2048,768]{2,1,0:T(8,128)(2,1)S(1)} %copy-done, bf16[1,2048,768]{2,1,0:T(8,128)(2,1)S(1)} %copy-done.1), custom_call_target="tpu_custom_call" | custom-call | flops 4831838208 | bytes 9437184 | tf_op jit(solution)/shard_map/hidden/pallas_call | solution.py:200
  55.7 0.0 copy-done.2
  55.7 1.1 %down.1 = bf16[768,2048]{1,0:T(8,128)(2,1)S(1)} custom-call(s32[8,128]{1,0:T(8,128)S(1)} %get-tuple-element.22.slot_ref, f32[8,128]{1,0:T(8,128)S(1)} %get-tuple-element.26.loss_ref, bf16[768,768]{1,0:T(8,128)(2,1)S(1)} %get-tuple-element.27.x_ref, bf16[1,768,2048]{2,1,0:T(8,128)(2,1)S(1)} %copy-done.2), custom_call_target="tpu_custom_call" | custom-call | flops 2415919104 | bytes 6291456 | tf_op jit(solution)/shard_map/down/pallas_call | solution.py:247
  56.9 30.9 %all_to_all.23 = bf16[16,48,2048]{2,1,0:T(8,128)(2,1)S(1)} all-to-all(bf16[16,48,2048]{2,1,0:T(8,128)(2,1)S(1)} %bitcast.11), channel_id=1, replica_groups=mesh['dp'=16,'expert'=16] {'expert'}, dimensions={0} | all-to-all | bytes 6291456 | tf_op jit(solution)/shard_map/all_to_all | solution.py:404
  87.7 0.1 read.1.mine_ref
  87.8 0.0 collective-permute-start.4
  87.9 1.7 %combine.1 = bf16[128,2048]{1,0:T(8,128)(2,1)} custom-call(bf16[256,768]{1,0:T(8,128)(2,1)S(1)} %select.3.pick_ref, f32[2,128]{1,0:T(2,128)S(1)} %get-tuple-element.29.gates_ref, bf16[768,2048]{1,0:T(8,128)(2,1)S(1)} %bitcast.9), custom_call_target="tpu_custom_call" | custom-call | flops 805306368 | bytes 3145728 | tf_op jit(solution)/shard_map/combine/pallas_call | solution.py:352
  89.6 0.0 collective-permute-done.4.other_ref
  89.6 0.7 loss.1
  (4 shorter events, 0.0 us)
Async XLA Ops:
  1.7 4.5 %collective-permute-start.3 = (f32[8,128]{1,0:T(8,128)S(1)}, f32[8,128]{1,0:T(8,128)S(1)}, u32[]{:S(2)}, u32[]{:S(2)}) collective-permute-start(f32[8,128]{1,0:T(8,128)S(1)} %get-tuple-element.23), channel_id=1, source_target_pairs={{0,16},{1,17},{2,18},{3,19},{4,20},{5,21},{6,22},{7,23},{8,24},{9,... | collective-permute-start | bytes 12296 | tf_op jit(solution)/shard_map/ppermute | solution.py:388
  6.3 4.4 %collective-permute-start = (f32[8,128]{1,0:T(8,128)S(1)}, f32[8,128]{1,0:T(8,128)S(1)}, u32[]{:S(2)}, u32[]{:S(2)}) collective-permute-start(f32[8,128]{1,0:T(8,128)S(1)} %add.11), channel_id=1, source_target_pairs={{16,48},{17,49},{18,50},{19,51},{20,52},{21,53},{22,54},{23,55},{2... | collective-permute-start | bytes 12296 | tf_op jit(solution)/shard_map/cond/branch_1_fun/ppermute | solution.py:371
  10.7 5.2 %collective-permute-start.1 = (f32[8,128]{1,0:T(8,128)S(1)}, f32[8,128]{1,0:T(8,128)S(1)}, u32[]{:S(2)}, u32[]{:S(2)}) collective-permute-start(f32[8,128]{1,0:T(8,128)S(1)} %add.12), channel_id=1, source_target_pairs={{16,80},{17,81},{18,82},{19,83},{20,84},{21,85},{22,86},{23,87},{2... | collective-permute-start | bytes 12296 | tf_op jit(solution)/shard_map/cond/branch_1_fun/ppermute | solution.py:371
  15.9 7.5 %collective-permute-start.2 = (f32[8,128]{1,0:T(8,128)S(1)}, f32[8,128]{1,0:T(8,128)S(1)}, u32[]{:S(2)}, u32[]{:S(2)}) collective-permute-start(f32[8,128]{1,0:T(8,128)S(1)} %add.13), channel_id=1, source_target_pairs={{16,208},{17,209},{18,210},{19,211},{20,212},{21,213},{22,214},{23... | collective-permute-start | bytes 12296 | tf_op jit(solution)/shard_map/cond/branch_1_fun/ppermute | solution.py:371
  23.5 30.2 %copy-start = (bf16[1,2048,768]{2,1,0:T(8,128)(2,1)S(1)}, bf16[1,2048,768]{2,1,0:T(8,128)(2,1)}, u32[]{:S(2)}) copy-start(bf16[1,2048,768]{2,1,0:T(8,128)(2,1)} %gate_ref.1) | copy-start | bytes 9437188
  23.6 30.2 %copy-start.1 = (bf16[1,2048,768]{2,1,0:T(8,128)(2,1)S(1)}, bf16[1,2048,768]{2,1,0:T(8,128)(2,1)}, u32[]{:S(2)}) copy-start(bf16[1,2048,768]{2,1,0:T(8,128)(2,1)} %up_ref.1) | copy-start | bytes 9437188
  53.8 2.0 %copy-start.2 = (bf16[1,768,2048]{2,1,0:T(8,128)(2,1)S(1)}, bf16[1,768,2048]{2,1,0:T(8,128)(2,1)}, u32[]{:S(2)}) copy-start(bf16[1,768,2048]{2,1,0:T(8,128)(2,1)} %down_ref.1) | copy-start | bytes 9437188
  87.8 1.8 %collective-permute-start.4 = (f32[8,128]{1,0:T(8,128)S(1)}, f32[8,128]{1,0:T(8,128)S(1)}, u32[]{:S(2)}, u32[]{:S(2)}) collective-permute-start(f32[8,128]{1,0:T(8,128)S(1)} %read.1.mine_ref), channel_id=1, source_target_pairs={{0,16},{1,17},{2,18},{3,19},{4,20},{5,21},{6,22},{7,23},{8,24},{9,... | collective-permute-start | bytes 12296 | tf_op jit(solution)/shard_map/ppermute | solution.py:406

commit v9 on v8

--- a/solution.py
+++ b/solution.py
@@ -387,18 +387,18 @@
     late = lax.axis_index("dp") % 2
     other = lax.ppermute(stats, AXES, swap)
     outgoing = pack(slots, tokens, experts * cap)
-    pick = select(slots, experts * cap)
-
-    def column_sum(value, other):
+
+    def column_sum(value, other, rows):
         value = value + other
         for partner in ROUNDS:
             value = add_round(value, size, group, partner)
-        return value
-
-    stats = lax.cond(late == 1, column_sum, lambda value, other: value, stats, other)
-    outgoing = note(slots, stats, outgoing, experts, cap)
-    pick, outgoing = lax.optimization_barrier((pick, outgoing))
+        return note(slots, value, rows, experts, cap)
+
+    outgoing = lax.cond(late == 1, column_sum, lambda value, other, rows: rows, stats, other, outgoing)
     received = lax.all_to_all(outgoing, "expert", split_axis=0, concat_axis=0, tiled=True)
+    slots, received = lax.optimization_barrier((slots, received))
+    pick = select(slots, experts * cap)
+    received, pick = lax.optimization_barrier((received, pick))
     hidden, loss = hidden_of(slots, received, w_gate, w_up, experts, cap, all_tokens)
     result = down_of(slots, loss, hidden, w_down, cap)
     returned = lax.all_to_all(result, "expert", split_axis=0, concat_axis=0, tiled=True)

time: 90.5 us -> 89.9 us (level)
  no operation moved by 1% of the time
where the time goes in v9:
time: 89.9 us; the launch traced here: 89.6 us
  blocking collectives  60.4 us (67%)
  starting transfers between devices  14.8 us (16%)
  Pallas kernels  7.94 us (9%)
  waiting for transfers between devices  5.6 us (6%)
    all_to_all x1, blocking collectives, on_device(): lax.all_to_all(outgoing, 'expert', split_axis=0, concat_axis=0, tiled=True)  30.2 us
    all_to_all x1, blocking collectives, on_device(): lax.all_to_all(result, 'expert', split_axis=0, concat_axis=0, tiled=True)  30.2 us
    ppermute x3, starting transfers between devices, add_round(): return value + lax.ppermute(value, AXES, pairs)  11.5 us
    ppermute x3, waiting for transfers between devices, add_round(): return value + lax.ppermute(value, AXES, pairs)  5.59 us
    ppermute x1, starting transfers between devices, on_device(): other = lax.ppermute(stats, AXES, swap)  3.33 us
    pallas_call x1, Pallas kernels, hidden_of(): pl.pallas_call(functools.partial(hidden_kernel, experts, cap, tokens), in...  1.95 us
  transfers between devices with their start and end apart: 5, of which 3 were waited for; matrix products, arithmetic and copies ran while one was open for 0% of the time, Pallas kernels for 3%

profile of v9, /device:TPU:1, one launch (start us, length us, event | category | flops | bytes accessed | tf_op | source)
XLA Modules:
  0.0 89.6 jit_solution(17358225788520614244)
XLA Ops:
  0.6 1.1 %count.1 = (s32[8,128]{1,0:T(8,128)S(1)}, f32[8,128]{1,0:T(8,128)S(1)}, bf16[128,2048]{1,0:T(8,128)(2,1)S(1)}, f32[2,128]{1,0:T(2,128)S(1)}) custom-call(s32[2,128]{1,0:T(2,128)} %bitcast.12, f32[2,128]{1,0:T(2,128)} %bitcast.13, bf16[128,2048]{1,0:T(8,128)(2,1)} %tok_hbm.1), custom_call_target="tpu_custom_call" | custom-call | flops 8388608 | bytes 1024 | tf_op jit(solution)/shard_map/count/pallas_call | solution.py:68
  1.7 3.3 %collective-permute-start.3 = (f32[8,128]{1,0:T(8,128)S(1)}, f32[8,128]{1,0:T(8,128)S(1)}, u32[]{:S(2)}, u32[]{:S(2)}) collective-permute-start(f32[8,128]{1,0:T(8,128)S(1)} %get-tuple-element.32), channel_id=1, source_target_pairs={{0,16},{1,17},{2,18},{3,19},{4,20},{5,21},{6,22},{7,23},{8,24},{9,... | collective-permute-start | bytes 12296 | tf_op jit(solution)/shard_map/ppermute | solution.py:388
  5.1 1.0 %pack.1 = bf16[768,2048]{1,0:T(8,128)(2,1)S(1)} custom-call(s32[8,128]{1,0:T(8,128)S(1)} %get-tuple-element.33.slot_ref, bf16[128,2048]{1,0:T(8,128)(2,1)S(1)} %get-tuple-element.31.tok_ref), custom_call_target="tpu_custom_call" | custom-call | flops 402653184 | bytes 6291456 | tf_op jit(solution)/shard_map/pack/pallas_call | solution.py:112
  6.0 0.0 collective-permute-done.3
  6.1 17.3 %conditional.1 = (bf16[768,2048]{1,0:T(8,128)(2,1)S(1)}) conditional(s32[]{:T(128)} %convert_element_type.3, bf16[768,2048]{1,0:T(8,128)(2,1)S(1)} %pack.1, (f32[8,128]{1,0:T(8,128)S(1)}, f32[8,128]{1,0:T(8,128)S(1)}, s32[8,128]{1,0:T(8,128)S(1)}, bf16[768,2048]{1,0:T(8,128)(2,1)S(1)}) %tuple.17), branch_computations={%region_0.1_spmd, %region_1.2_spmd} | conditional | flops 4096 | bytes 163968 | solution.py:397
  6.1 1.9 %collective-permute-start = (f32[8,128]{1,0:T(8,128)S(1)}, f32[8,128]{1,0:T(8,128)S(1)}, u32[]{:S(2)}, u32[]{:S(2)}) collective-permute-start(f32[8,128]{1,0:T(8,128)S(1)} %add.11), channel_id=1, source_target_pairs={{16,48},{17,49},{18,50},{19,51},{20,52},{21,53},{22,54},{23,55},{2... | collective-permute-start | bytes 12296 | tf_op jit(solution)/shard_map/cond/branch_1_fun/ppermute | solution.py:371
  8.0 2.4 %collective-permute-done = f32[8,128]{1,0:T(8,128)S(1)} collective-permute-done((f32[8,128]{1,0:T(8,128)S(1)}, f32[8,128]{1,0:T(8,128)S(1)}, u32[]{:S(2)}, u32[]{:S(2)}) %collective-permute-start) | collective-permute-done | bytes 4128 | tf_op jit(solution)/shard_map/cond/branch_1_fun/ppermute | solution.py:371
  10.4 3.3 %collective-permute-start.1 = (f32[8,128]{1,0:T(8,128)S(1)}, f32[8,128]{1,0:T(8,128)S(1)}, u32[]{:S(2)}, u32[]{:S(2)}) collective-permute-start(f32[8,128]{1,0:T(8,128)S(1)} %add.12), channel_id=1, source_target_pairs={{16,80},{17,81},{18,82},{19,83},{20,84},{21,85},{22,86},{23,87},{2... | collective-permute-start | bytes 12296 | tf_op jit(solution)/shard_map/cond/branch_1_fun/ppermute | solution.py:371
  13.8 1.9 %collective-permute-done.1 = f32[8,128]{1,0:T(8,128)S(1)} collective-permute-done((f32[8,128]{1,0:T(8,128)S(1)}, f32[8,128]{1,0:T(8,128)S(1)}, u32[]{:S(2)}, u32[]{:S(2)}) %collective-permute-start.1) | collective-permute-done | bytes 4128 | tf_op jit(solution)/shard_map/cond/branch_1_fun/ppermute | solution.py:371
  15.7 6.2 %collective-permute-start.2 = (f32[8,128]{1,0:T(8,128)S(1)}, f32[8,128]{1,0:T(8,128)S(1)}, u32[]{:S(2)}, u32[]{:S(2)}) collective-permute-start(f32[8,128]{1,0:T(8,128)S(1)} %add.13), channel_id=1, source_target_pairs={{16,208},{17,209},{18,210},{19,211},{20,212},{21,213},{22,214},{23... | collective-permute-start | bytes 12296 | tf_op jit(solution)/shard_map/cond/branch_1_fun/ppermute | solution.py:371
  21.9 1.3 %collective-permute-done.2 = f32[8,128]{1,0:T(8,128)S(1)} collective-permute-done((f32[8,128]{1,0:T(8,128)S(1)}, f32[8,128]{1,0:T(8,128)S(1)}, u32[]{:S(2)}, u32[]{:S(2)}) %collective-permute-start.2) | collective-permute-done | bytes 4128 | tf_op jit(solution)/shard_map/cond/branch_1_fun/ppermute | solution.py:371
  23.2 0.1 note.1
  23.3 0.0 copy-start
  23.3 0.0 copy-start.1
  23.3 30.2 %all_to_all.23 = bf16[16,48,2048]{2,1,0:T(8,128)(2,1)S(1)} all-to-all(bf16[16,48,2048]{2,1,0:T(8,128)(2,1)S(1)} %bitcast.11), channel_id=1, replica_groups=mesh['dp'=16,'expert'=16] {'expert'}, dimensions={0} | all-to-all | bytes 6291456 | tf_op jit(solution)/shard_map/all_to_all | solution.py:398
  53.6 0.2 select.3.pick_ref
  53.8 0.0 copy-done
  53.8 0.0 copy-done.1
  53.8 0.0 copy-start.2
  53.8 1.9 %hidden.1 = (bf16[768,768]{1,0:T(8,128)(2,1)S(1)}, f32[8,128]{1,0:T(8,128)S(1)}) custom-call(s32[8,128]{1,0:T(8,128)S(1)} %get-tuple-element.33.slot_ref, bf16[768,2048]{1,0:T(8,128)(2,1)S(1)} %bitcast.9, bf16[1,2048,768]{2,1,0:T(8,128)(2,1)S(1)} %copy-done, bf16[1,2048,768]{2,1,0:T(8,128)(2,1)S(1)} %copy-done.1), custom_call_target="tpu_custom_call" | custom-call | flops 4831838208 | bytes 9437184 | tf_op jit(solution)/shard_map/hidden/pallas_call | solution.py:200
  55.8 0.0 copy-done.2
  55.8 1.1 %down.1 = bf16[768,2048]{1,0:T(8,128)(2,1)S(1)} custom-call(s32[8,128]{1,0:T(8,128)S(1)} %get-tuple-element.33.slot_ref, f32[8,128]{1,0:T(8,128)S(1)} %get-tuple-element.36.loss_ref, bf16[768,768]{1,0:T(8,128)(2,1)S(1)} %get-tuple-element.37.x_ref, bf16[1,768,2048]{2,1,0:T(8,128)(2,1)S(1)} %copy-done.2), custom_call_target="tpu_custom_call" | custom-call | flops 2415919104 | bytes 6291456 | tf_op jit(solution)/shard_map/down/pallas_call | solution.py:247
  56.9 30.2 %all_to_all.24 = bf16[16,48,2048]{2,1,0:T(8,128)(2,1)S(1)} all-to-all(bf16[16,48,2048]{2,1,0:T(8,128)(2,1)S(1)} %bitcast.10), channel_id=1, replica_groups=mesh['dp'=16,'expert'=16] {'expert'}, dimensions={0} | all-to-all | bytes 6291456 | tf_op jit(solution)/shard_map/all_to_all | solution.py:404
  87.1 0.1 read.1.mine_ref
  87.2 0.0 collective-permute-start.4
  87.2 1.7 %combine.1 = bf16[128,2048]{1,0:T(8,128)(2,1)} custom-call(bf16[256,768]{1,0:T(8,128)(2,1)S(1)} %select.3.pick_ref, f32[2,128]{1,0:T(2,128)S(1)} %get-tuple-element.39.gates_ref, bf16[768,2048]{1,0:T(8,128)(2,1)S(1)} %bitcast.8), custom_call_target="tpu_custom_call" | custom-call | flops 805306368 | bytes 3145728 | tf_op jit(solution)/shard_map/combine/pallas_call | solution.py:352
  88.9 0.0 collective-permute-done.4.other_ref
  88.9 0.7 loss.1
  (4 shorter events, 0.0 us)
Async XLA Ops:
  1.7 4.3 %collective-permute-start.3 = (f32[8,128]{1,0:T(8,128)S(1)}, f32[8,128]{1,0:T(8,128)S(1)}, u32[]{:S(2)}, u32[]{:S(2)}) collective-permute-start(f32[8,128]{1,0:T(8,128)S(1)} %get-tuple-element.32), channel_id=1, source_target_pairs={{0,16},{1,17},{2,18},{3,19},{4,20},{5,21},{6,22},{7,23},{8,24},{9,... | collective-permute-start | bytes 12296 | tf_op jit(solution)/shard_map/ppermute | solution.py:388
  6.1 4.4 %collective-permute-start = (f32[8,128]{1,0:T(8,128)S(1)}, f32[8,128]{1,0:T(8,128)S(1)}, u32[]{:S(2)}, u32[]{:S(2)}) collective-permute-start(f32[8,128]{1,0:T(8,128)S(1)} %add.11), channel_id=1, source_target_pairs={{16,48},{17,49},{18,50},{19,51},{20,52},{21,53},{22,54},{23,55},{2... | collective-permute-start | bytes 12296 | tf_op jit(solution)/shard_map/cond/branch_1_fun/ppermute | solution.py:371
  10.4 5.2 %collective-permute-start.1 = (f32[8,128]{1,0:T(8,128)S(1)}, f32[8,128]{1,0:T(8,128)S(1)}, u32[]{:S(2)}, u32[]{:S(2)}) collective-permute-start(f32[8,128]{1,0:T(8,128)S(1)} %add.12), channel_id=1, source_target_pairs={{16,80},{17,81},{18,82},{19,83},{20,84},{21,85},{22,86},{23,87},{2... | collective-permute-start | bytes 12296 | tf_op jit(solution)/shard_map/cond/branch_1_fun/ppermute | solution.py:371
  15.7 7.5 %collective-permute-start.2 = (f32[8,128]{1,0:T(8,128)S(1)}, f32[8,128]{1,0:T(8,128)S(1)}, u32[]{:S(2)}, u32[]{:S(2)}) collective-permute-start(f32[8,128]{1,0:T(8,128)S(1)} %add.13), channel_id=1, source_target_pairs={{16,208},{17,209},{18,210},{19,211},{20,212},{21,213},{22,214},{23... | collective-permute-start | bytes 12296 | tf_op jit(solution)/shard_map/cond/branch_1_fun/ppermute | solution.py:371
  23.3 30.5 %copy-start = (bf16[1,2048,768]{2,1,0:T(8,128)(2,1)S(1)}, bf16[1,2048,768]{2,1,0:T(8,128)(2,1)}, u32[]{:S(2)}) copy-start(bf16[1,2048,768]{2,1,0:T(8,128)(2,1)} %gate_ref.1) | copy-start | bytes 9437188
  23.3 30.5 %copy-start.1 = (bf16[1,2048,768]{2,1,0:T(8,128)(2,1)S(1)}, bf16[1,2048,768]{2,1,0:T(8,128)(2,1)}, u32[]{:S(2)}) copy-start(bf16[1,2048,768]{2,1,0:T(8,128)(2,1)} %up_ref.1) | copy-start | bytes 9437188
  53.8 2.0 %copy-start.2 = (bf16[1,768,2048]{2,1,0:T(8,128)(2,1)S(1)}, bf16[1,768,2048]{2,1,0:T(8,128)(2,1)}, u32[]{:S(2)}) copy-start(bf16[1,768,2048]{2,1,0:T(8,128)(2,1)} %down_ref.1) | copy-start | bytes 9437188
  87.2 1.8 %collective-permute-start.4 = (f32[8,128]{1,0:T(8,128)S(1)}, f32[8,128]{1,0:T(8,128)S(1)}, u32[]{:S(2)}, u32[]{:S(2)}) collective-permute-start(f32[8,128]{1,0:T(8,128)S(1)} %read.1.mine_ref), channel_id=1, source_target_pairs={{0,16},{1,17},{2,18},{3,19},{4,20},{5,21},{6,22},{7,23},{8,24},{9,... | collective-permute-start | bytes 12296 | tf_op jit(solution)/shard_map/ppermute | solution.py:406

commit v10 on v9

--- a/solution.py
+++ b/solution.py
@@ -93,24 +93,37 @@
     return parts
 
 
-def pack_kernel(slot_ref, tok_ref, out_ref):
+def pack_kernel(experts, cap, slot_ref, tok_ref, out_ref):
     toks = tok_ref.shape[0]
-    rows = out_ref.shape[0] // PARTS
-    tokens = tok_ref[...]
+    few, rest = experts * 16, cap - 16
     first_slot, second_slot = slot_ref[0:1, :], slot_ref[1:2, :]
-    for part in range(PARTS):
-        slot = lax.broadcasted_iota(jnp.int32, (rows, toks), 0) + part * rows
+    lane = lax.broadcasted_iota(jnp.int32, (1, toks), 1)
+    full = (lane < experts) & (slot_ref[2:3, :] == 0)
+    low = jnp.min(jnp.where(full, lane, experts - 1))
+    high = jnp.max(jnp.where(full, lane, 0))
+    row = lax.broadcasted_iota(jnp.int32, (few, toks), 0)
+    slot = (row >> 4) * cap + (row & 15)
+    pick = ((slot == first_slot) | (slot == second_slot)).astype(F32).astype(BF16)
+    rows = jnp.dot(pick, tok_ref[...], preferred_element_type=F32).astype(BF16)
+    none = jnp.zeros((rest, out_ref.shape[1]), BF16)
+    for e in range(experts):
+        out_ref[e * cap : e * cap + 16, :] = rows[e * 16 : e * 16 + 16, :]
+        out_ref[e * cap + 16 : (e + 1) * cap, :] = none
+    for expert in (low, high):
+        start = pl.multiple_of(expert * cap + 16, 16)
+        slot = lax.broadcasted_iota(jnp.int32, (rest, toks), 0) + start
         pick = ((slot == first_slot) | (slot == second_slot)).astype(F32).astype(BF16)
-        out_ref[part * rows : (part + 1) * rows, :] = jnp.dot(
-            pick, tokens, preferred_element_type=F32
+        out_ref[pl.ds(start, rest), :] = jnp.dot(
+            pick, tok_ref[...], preferred_element_type=F32
         ).astype(BF16)
 
 
-def pack(slots, tokens, count):
+def pack(slots, tokens, experts, cap):
     toks, width = tokens.shape
-    held = pl.BlockSpec(memory_space=pltpu.VMEM)
-    return pl.pallas_call(
-        pack_kernel,
+    count = experts * cap
+    held = pl.BlockSpec(memory_space=pltpu.VMEM)
+    return pl.pallas_call(
+        functools.partial(pack_kernel, experts, cap),
         in_specs=[held] * 2,
         out_specs=held,
         out_shape=jax.ShapeDtypeStruct((count, width), BF16),
@@ -386,7 +399,7 @@
     swap = [(i, i + group if (i // group) % 2 == 0 else i - group) for i in range(size)]
     late = lax.axis_index("dp") % 2
     other = lax.ppermute(stats, AXES, swap)
-    outgoing = pack(slots, tokens, experts * cap)
+    outgoing = pack(slots, tokens, experts, cap)
 
     def column_sum(value, other, rows):
         value = value + other

time: 89.9 us -> 90.4 us (level)
  transfers between devices with their start and end apart: 5 -> 5, of which waited for: 3 -> 4; matrix products, arithmetic and copies ran while one was open for 0% -> 0% of each run, Pallas kernels for 3% -> 3%
where the time goes in v10:
time: 90.4 us; the launch traced here: 89.3 us
  blocking collectives  60.3 us (67%)
  starting transfers between devices  14.8 us (16%)
  Pallas kernels  7.64 us (8%)
  waiting for transfers between devices  5.74 us (6%)
    all_to_all x1, blocking collectives, on_device(): lax.all_to_all(outgoing, 'expert', split_axis=0, concat_axis=0, tiled=True)  30.2 us
    all_to_all x1, blocking collectives, on_device(): lax.all_to_all(result, 'expert', split_axis=0, concat_axis=0, tiled=True)  30.1 us
    ppermute x3, starting transfers between devices, add_round(): return value + lax.ppermute(value, AXES, pairs)  11.4 us
    ppermute x3, waiting for transfers between devices, add_round(): return value + lax.ppermute(value, AXES, pairs)  5.6 us
    ppermute x1, starting transfers between devices, on_device(): other = lax.ppermute(stats, AXES, swap)  3.33 us
    pallas_call x1, Pallas kernels, hidden_of(): pl.pallas_call(functools.partial(hidden_kernel, experts, cap, tokens), in...  1.95 us
  transfers between devices with their start and end apart: 5, of which 4 were waited for; matrix products, arithmetic and copies ran while one was open for 0% of the time, Pallas kernels for 3%

profile of v10, /device:TPU:1, one launch (start us, length us, event | category | flops | bytes accessed | tf_op | source)
XLA Modules:
  0.0 89.3 jit_solution(8782712129237572785)
XLA Ops:
  0.6 1.1 %count.1 = (s32[8,128]{1,0:T(8,128)S(1)}, f32[8,128]{1,0:T(8,128)S(1)}, bf16[128,2048]{1,0:T(8,128)(2,1)S(1)}, f32[2,128]{1,0:T(2,128)S(1)}) custom-call(s32[2,128]{1,0:T(2,128)} %bitcast.12, f32[2,128]{1,0:T(2,128)} %bitcast.13, bf16[128,2048]{1,0:T(8,128)(2,1)} %tok_hbm.1), custom_call_target="tpu_custom_call" | custom-call | flops 8388608 | bytes 1024 | tf_op jit(solution)/shard_map/count/pallas_call | solution.py:68
  1.7 3.3 %collective-permute-start.3 = (f32[8,128]{1,0:T(8,128)S(1)}, f32[8,128]{1,0:T(8,128)S(1)}, u32[]{:S(2)}, u32[]{:S(2)}) collective-permute-start(f32[8,128]{1,0:T(8,128)S(1)} %get-tuple-element.32), channel_id=1, source_target_pairs={{0,16},{1,17},{2,18},{3,19},{4,20},{5,21},{6,22},{7,23},{8,24},{9,... | collective-permute-start | bytes 12296 | tf_op jit(solution)/shard_map/ppermute | solution.py:401
  5.1 0.7 pack.1
  5.7 0.1 collective-permute-done.3
  5.9 17.2 %conditional.1 = (bf16[768,2048]{1,0:T(8,128)(2,1)S(1)}) conditional(s32[]{:T(128)} %convert_element_type.3, bf16[768,2048]{1,0:T(8,128)(2,1)S(1)} %pack.1, (f32[8,128]{1,0:T(8,128)S(1)}, f32[8,128]{1,0:T(8,128)S(1)}, s32[8,128]{1,0:T(8,128)S(1)}, bf16[768,2048]{1,0:T(8,128)(2,1)S(1)}) %tuple.17), branch_computations={%region_0.1_spmd, %region_1.2_spmd} | conditional | flops 4096 | bytes 163968 | solution.py:410
  5.9 1.9 %collective-permute-start = (f32[8,128]{1,0:T(8,128)S(1)}, f32[8,128]{1,0:T(8,128)S(1)}, u32[]{:S(2)}, u32[]{:S(2)}) collective-permute-start(f32[8,128]{1,0:T(8,128)S(1)} %add.11), channel_id=1, source_target_pairs={{16,48},{17,49},{18,50},{19,51},{20,52},{21,53},{22,54},{23,55},{2... | collective-permute-start | bytes 12296 | tf_op jit(solution)/shard_map/cond/branch_1_fun/ppermute | solution.py:384
  7.8 2.4 %collective-permute-done = f32[8,128]{1,0:T(8,128)S(1)} collective-permute-done((f32[8,128]{1,0:T(8,128)S(1)}, f32[8,128]{1,0:T(8,128)S(1)}, u32[]{:S(2)}, u32[]{:S(2)}) %collective-permute-start) | collective-permute-done | bytes 4128 | tf_op jit(solution)/shard_map/cond/branch_1_fun/ppermute | solution.py:384
  10.2 3.3 %collective-permute-start.1 = (f32[8,128]{1,0:T(8,128)S(1)}, f32[8,128]{1,0:T(8,128)S(1)}, u32[]{:S(2)}, u32[]{:S(2)}) collective-permute-start(f32[8,128]{1,0:T(8,128)S(1)} %add.12), channel_id=1, source_target_pairs={{16,80},{17,81},{18,82},{19,83},{20,84},{21,85},{22,86},{23,87},{2... | collective-permute-start | bytes 12296 | tf_op jit(solution)/shard_map/cond/branch_1_fun/ppermute | solution.py:384
  13.6 1.9 %collective-permute-done.1 = f32[8,128]{1,0:T(8,128)S(1)} collective-permute-done((f32[8,128]{1,0:T(8,128)S(1)}, f32[8,128]{1,0:T(8,128)S(1)}, u32[]{:S(2)}, u32[]{:S(2)}) %collective-permute-start.1) | collective-permute-done | bytes 4128 | tf_op jit(solution)/shard_map/cond/branch_1_fun/ppermute | solution.py:384
  15.5 6.2 %collective-permute-start.2 = (f32[8,128]{1,0:T(8,128)S(1)}, f32[8,128]{1,0:T(8,128)S(1)}, u32[]{:S(2)}, u32[]{:S(2)}) collective-permute-start(f32[8,128]{1,0:T(8,128)S(1)} %add.13), channel_id=1, source_target_pairs={{16,208},{17,209},{18,210},{19,211},{20,212},{21,213},{22,214},{23... | collective-permute-start | bytes 12296 | tf_op jit(solution)/shard_map/cond/branch_1_fun/ppermute | solution.py:384
  21.7 1.3 %collective-permute-done.2 = f32[8,128]{1,0:T(8,128)S(1)} collective-permute-done((f32[8,128]{1,0:T(8,128)S(1)}, f32[8,128]{1,0:T(8,128)S(1)}, u32[]{:S(2)}, u32[]{:S(2)}) %collective-permute-start.2) | collective-permute-done | bytes 4128 | tf_op jit(solution)/shard_map/cond/branch_1_fun/ppermute | solution.py:384
  23.0 0.1 note.1
  23.1 0.0 copy-start
  23.1 0.0 copy-start.1
  23.1 30.2 %all_to_all.23 = bf16[16,48,2048]{2,1,0:T(8,128)(2,1)S(1)} all-to-all(bf16[16,48,2048]{2,1,0:T(8,128)(2,1)S(1)} %bitcast.11), channel_id=1, replica_groups=mesh['dp'=16,'expert'=16] {'expert'}, dimensions={0} | all-to-all | bytes 6291456 | tf_op jit(solution)/shard_map/all_to_all | solution.py:411
  53.3 0.2 select.3.pick_ref
  53.5 0.0 copy-done
  53.6 0.0 copy-done.1
  53.6 0.0 copy-start.2
  53.6 1.9 %hidden.1 = (bf16[768,768]{1,0:T(8,128)(2,1)S(1)}, f32[8,128]{1,0:T(8,128)S(1)}) custom-call(s32[8,128]{1,0:T(8,128)S(1)} %get-tuple-element.33.slot_ref, bf16[768,2048]{1,0:T(8,128)(2,1)S(1)} %bitcast.9, bf16[1,2048,768]{2,1,0:T(8,128)(2,1)S(1)} %copy-done, bf16[1,2048,768]{2,1,0:T(8,128)(2,1)S(1)} %copy-done.1), custom_call_target="tpu_custom_call" | custom-call | flops 4831838208 | bytes 9437184 | tf_op jit(solution)/shard_map/hidden/pallas_call | solution.py:213
  55.5 0.0 copy-done.2
  55.5 1.1 %down.1 = bf16[768,2048]{1,0:T(8,128)(2,1)S(1)} custom-call(s32[8,128]{1,0:T(8,128)S(1)} %get-tuple-element.33.slot_ref, f32[8,128]{1,0:T(8,128)S(1)} %get-tuple-element.36.loss_ref, bf16[768,768]{1,0:T(8,128)(2,1)S(1)} %get-tuple-element.37.x_ref, bf16[1,768,2048]{2,1,0:T(8,128)(2,1)S(1)} %copy-done.2), custom_call_target="tpu_custom_call" | custom-call | flops 2415919104 | bytes 6291456 | tf_op jit(solution)/shard_map/down/pallas_call | solution.py:260
  56.7 30.1 %all_to_all.24 = bf16[16,48,2048]{2,1,0:T(8,128)(2,1)S(1)} all-to-all(bf16[16,48,2048]{2,1,0:T(8,128)(2,1)S(1)} %bitcast.10), channel_id=1, replica_groups=mesh['dp'=16,'expert'=16] {'expert'}, dimensions={0} | all-to-all | bytes 6291456 | tf_op jit(solution)/shard_map/all_to_all | solution.py:417
  86.8 0.1 read.1.mine_ref
  86.8 0.0 collective-permute-start.4
  86.9 1.7 %combine.1 = bf16[128,2048]{1,0:T(8,128)(2,1)} custom-call(bf16[256,768]{1,0:T(8,128)(2,1)S(1)} %select.3.pick_ref, f32[2,128]{1,0:T(2,128)S(1)} %get-tuple-element.39.gates_ref, bf16[768,2048]{1,0:T(8,128)(2,1)S(1)} %bitcast.8), custom_call_target="tpu_custom_call" | custom-call | flops 805306368 | bytes 3145728 | tf_op jit(solution)/shard_map/combine/pallas_call | solution.py:365
  88.6 0.0 collective-permute-done.4.other_ref
  88.6 0.7 loss.1
  (4 shorter events, 0.0 us)
Async XLA Ops:
  1.7 4.2 %collective-permute-start.3 = (f32[8,128]{1,0:T(8,128)S(1)}, f32[8,128]{1,0:T(8,128)S(1)}, u32[]{:S(2)}, u32[]{:S(2)}) collective-permute-start(f32[8,128]{1,0:T(8,128)S(1)} %get-tuple-element.32), channel_id=1, source_target_pairs={{0,16},{1,17},{2,18},{3,19},{4,20},{5,21},{6,22},{7,23},{8,24},{9,... | collective-permute-start | bytes 12296 | tf_op jit(solution)/shard_map/ppermute | solution.py:401
  5.9 4.3 %collective-permute-start = (f32[8,128]{1,0:T(8,128)S(1)}, f32[8,128]{1,0:T(8,128)S(1)}, u32[]{:S(2)}, u32[]{:S(2)}) collective-permute-start(f32[8,128]{1,0:T(8,128)S(1)} %add.11), channel_id=1, source_target_pairs={{16,48},{17,49},{18,50},{19,51},{20,52},{21,53},{22,54},{23,55},{2... | collective-permute-start | bytes 12296 | tf_op jit(solution)/shard_map/cond/branch_1_fun/ppermute | solution.py:384
  10.2 5.2 %collective-permute-start.1 = (f32[8,128]{1,0:T(8,128)S(1)}, f32[8,128]{1,0:T(8,128)S(1)}, u32[]{:S(2)}, u32[]{:S(2)}) collective-permute-start(f32[8,128]{1,0:T(8,128)S(1)} %add.12), channel_id=1, source_target_pairs={{16,80},{17,81},{18,82},{19,83},{20,84},{21,85},{22,86},{23,87},{2... | collective-permute-start | bytes 12296 | tf_op jit(solution)/shard_map/cond/branch_1_fun/ppermute | solution.py:384
  15.5 7.5 %collective-permute-start.2 = (f32[8,128]{1,0:T(8,128)S(1)}, f32[8,128]{1,0:T(8,128)S(1)}, u32[]{:S(2)}, u32[]{:S(2)}) collective-permute-start(f32[8,128]{1,0:T(8,128)S(1)} %add.13), channel_id=1, source_target_pairs={{16,208},{17,209},{18,210},{19,211},{20,212},{21,213},{22,214},{23... | collective-permute-start | bytes 12296 | tf_op jit(solution)/shard_map/cond/branch_1_fun/ppermute | solution.py:384
  23.1 30.4 %copy-start = (bf16[1,2048,768]{2,1,0:T(8,128)(2,1)S(1)}, bf16[1,2048,768]{2,1,0:T(8,128)(2,1)}, u32[]{:S(2)}) copy-start(bf16[1,2048,768]{2,1,0:T(8,128)(2,1)} %gate_ref.1) | copy-start | bytes 9437188
  23.1 30.4 %copy-start.1 = (bf16[1,2048,768]{2,1,0:T(8,128)(2,1)S(1)}, bf16[1,2048,768]{2,1,0:T(8,128)(2,1)}, u32[]{:S(2)}) copy-start(bf16[1,2048,768]{2,1,0:T(8,128)(2,1)} %up_ref.1) | copy-start | bytes 9437188
  53.6 2.0 %copy-start.2 = (bf16[1,768,2048]{2,1,0:T(8,128)(2,1)S(1)}, bf16[1,768,2048]{2,1,0:T(8,128)(2,1)}, u32[]{:S(2)}) copy-start(bf16[1,768,2048]{2,1,0:T(8,128)(2,1)} %down_ref.1) | copy-start | bytes 9437188
  86.8 1.8 %collective-permute-start.4 = (f32[8,128]{1,0:T(8,128)S(1)}, f32[8,128]{1,0:T(8,128)S(1)}, u32[]{:S(2)}, u32[]{:S(2)}) collective-permute-start(f32[8,128]{1,0:T(8,128)S(1)} %read.1.mine_ref), channel_id=1, source_target_pairs={{0,16},{1,17},{2,18},{3,19},{4,20},{5,21},{6,22},{7,23},{8,24},{9,... | collective-permute-start | bytes 12296 | tf_op jit(solution)/shard_map/ppermute | solution.py:419

commit v11 on v9

--- a/solution.py
+++ b/solution.py
@@ -259,29 +259,35 @@
     )(slots, loss, x, w_down)
 
 
-def select_kernel(slot_ref, pick_ref):
+def select_kernel(slot_ref, gates_ref, pick_ref, weight_ref):
     toks, slots = slot_ref.shape[1], pick_ref.shape[1]
     labels = lax.broadcasted_iota(jnp.int32, (toks, toks), 0)
     first_slot, second_slot = slot_ref[0:1, :].astype(F32), slot_ref[1:2, :].astype(F32)
-    lines = jnp.where(labels == 0, first_slot, jnp.where(labels == 1, second_slot, 0.0)).T
+    gates = gates_ref[...]
+    lines = jnp.where(labels == 0, first_slot, jnp.where(labels == 1, second_slot, 0.0))
+    lines = jnp.where(labels == 2, gates[0:1, :], jnp.where(labels == 3, gates[1:2, :], lines)).T
+    weight_ref[...] = lines
     dest = lines[:, 0:2].astype(jnp.int32)
     lane = lax.broadcasted_iota(jnp.int32, (toks, slots), 1)
     pick_ref[:toks, :] = (lane == dest[:, 0:1]).astype(F32).astype(BF16)
     pick_ref[toks:, :] = (lane == dest[:, 1:2]).astype(F32).astype(BF16)
 
 
-def select(slots, count):
+def select(slots, gates, count):
     toks = slots.shape[1]
     held = pl.BlockSpec(memory_space=pltpu.VMEM)
     return pl.pallas_call(
         select_kernel,
-        in_specs=[held],
-        out_specs=held,
-        out_shape=jax.ShapeDtypeStruct((2 * toks, count), BF16),
+        in_specs=[held] * 2,
+        out_specs=[held] * 2,
+        out_shape=[
+            jax.ShapeDtypeStruct((2 * toks, count), BF16),
+            jax.ShapeDtypeStruct((toks, toks), F32),
+        ],
         compiler_params=pltpu.CompilerParams(vmem_limit_bytes=4 * 2**20),
         cost_estimate=pl.CostEstimate(flops=0, bytes_accessed=4 * toks * count, transcendentals=0),
         name="select",
-    )(slots)
+    )(slots, gates)
 
 
 def read_kernel(cap, slot_ref, rows_ref, out_ref):
@@ -325,12 +331,9 @@
     )(mine, other)
 
 
-def combine_kernel(pick_ref, gates_ref, rows_ref, out_hbm, out_ref, sems):
+def combine_kernel(pick_ref, weight_ref, rows_ref, out_hbm, out_ref, sems):
     toks, width = out_ref.shape
-    gates = gates_ref[...]
-    labels = lax.broadcasted_iota(jnp.int32, (toks, toks), 0)
-    lines = jnp.where(labels == 0, gates[0:1, :], jnp.where(labels == 1, gates[1:2, :], 0.0)).T
-    first, second = lines[:, 0:1], lines[:, 1:2]
+    first, second = weight_ref[:, 2:3], weight_ref[:, 3:4]
     block = width // PARTS
     copies = []
     for part in range(PARTS):
@@ -345,8 +348,8 @@
         copy.wait()
 
 
-def combine(pick, gates, rows):
-    toks = gates.shape[1]
+def combine(pick, weights, rows):
+    toks = weights.shape[0]
     slots, width = rows.shape
     held = pl.BlockSpec(memory_space=pltpu.VMEM)
     return pl.pallas_call(
@@ -360,7 +363,7 @@
             flops=4 * toks * slots * width, bytes_accessed=2 * slots * width, transcendentals=0
         ),
         name="combine",
-    )(pick, gates, rows)
+    )(pick, weights, rows)
 
 
 def add_round(value, size, step, partner):
@@ -397,14 +400,14 @@
     outgoing = lax.cond(late == 1, column_sum, lambda value, other, rows: rows, stats, other, outgoing)
     received = lax.all_to_all(outgoing, "expert", split_axis=0, concat_axis=0, tiled=True)
     slots, received = lax.optimization_barrier((slots, received))
-    pick = select(slots, experts * cap)
-    received, pick = lax.optimization_barrier((received, pick))
+    pick, weights = select(slots, gates, experts * cap)
+    received, pick, weights = lax.optimization_barrier((received, pick, weights))
     hidden, loss = hidden_of(slots, received, w_gate, w_up, experts, cap, all_tokens)
     result = down_of(slots, loss, hidden, w_down, cap)
     returned = lax.all_to_all(result, "expert", split_axis=0, concat_axis=0, tiled=True)
     loss = read(slots, returned, cap)
     other = lax.ppermute(loss, AXES, swap)
-    mixed = combine(pick, gates, returned)
+    mixed = combine(pick, weights, returned)
     other, mixed = lax.optimization_barrier((other, mixed))
     return mixed, loss_of(loss, other).reshape(())
 

time: 89.9 us -> 89.8 us (level)
  no operation moved by 1% of the time
where the time goes in v11:
time: 89.8 us; the launch traced here: 89.5 us
  blocking collectives  60.3 us (67%)
  starting transfers between devices  14.8 us (16%)
  Pallas kernels  7.94 us (9%)
  waiting for transfers between devices  5.6 us (6%)
    all_to_all x1, blocking collectives, on_device(): lax.all_to_all(outgoing, 'expert', split_axis=0, concat_axis=0, tiled=True)  30.2 us
    all_to_all x1, blocking collectives, on_device(): lax.all_to_all(result, 'expert', split_axis=0, concat_axis=0, tiled=True)  30.1 us
    ppermute x3, starting transfers between devices, add_round(): return value + lax.ppermute(value, AXES, pairs)  11.5 us
    ppermute x3, waiting for transfers between devices, add_round(): return value + lax.ppermute(value, AXES, pairs)  5.59 us
    ppermute x1, starting transfers between devices, on_device(): other = lax.ppermute(stats, AXES, swap)  3.33 us
    pallas_call x1, Pallas kernels, hidden_of(): pl.pallas_call(functools.partial(hidden_kernel, experts, cap, tokens), in...  1.95 us
  transfers between devices with their start and end apart: 5, of which 3 were waited for; matrix products, arithmetic and copies ran while one was open for 0% of the time, Pallas kernels for 3%

profile of v11, /device:TPU:1, one launch (start us, length us, event | category | flops | bytes accessed | tf_op | source)
XLA Modules:
  0.0 89.5 jit_solution(18150634542201603913)
XLA Ops:
  0.6 1.1 %count.1 = (s32[8,128]{1,0:T(8,128)S(1)}, f32[8,128]{1,0:T(8,128)S(1)}, bf16[128,2048]{1,0:T(8,128)(2,1)S(1)}, f32[2,128]{1,0:T(2,128)S(1)}) custom-call(s32[2,128]{1,0:T(2,128)} %bitcast.12, f32[2,128]{1,0:T(2,128)} %bitcast.13, bf16[128,2048]{1,0:T(8,128)(2,1)} %tok_hbm.1), custom_call_target="tpu_custom_call" | custom-call | flops 8388608 | bytes 1024 | tf_op jit(solution)/shard_map/count/pallas_call | solution.py:68
  1.7 3.3 %collective-permute-start.3 = (f32[8,128]{1,0:T(8,128)S(1)}, f32[8,128]{1,0:T(8,128)S(1)}, u32[]{:S(2)}, u32[]{:S(2)}) collective-permute-start(f32[8,128]{1,0:T(8,128)S(1)} %get-tuple-element.35), channel_id=1, source_target_pairs={{0,16},{1,17},{2,18},{3,19},{4,20},{5,21},{6,22},{7,23},{8,24},{9,... | collective-permute-start | bytes 12296 | tf_op jit(solution)/shard_map/ppermute | solution.py:391
  5.1 1.0 %pack.1 = bf16[768,2048]{1,0:T(8,128)(2,1)S(1)} custom-call(s32[8,128]{1,0:T(8,128)S(1)} %get-tuple-element.36.slot_ref, bf16[128,2048]{1,0:T(8,128)(2,1)S(1)} %get-tuple-element.34.tok_ref), custom_call_target="tpu_custom_call" | custom-call | flops 402653184 | bytes 6291456 | tf_op jit(solution)/shard_map/pack/pallas_call | solution.py:112
  6.0 0.0 collective-permute-done.3
  6.1 17.3 %conditional.1 = (bf16[768,2048]{1,0:T(8,128)(2,1)S(1)}) conditional(s32[]{:T(128)} %convert_element_type.3, bf16[768,2048]{1,0:T(8,128)(2,1)S(1)} %pack.1, (f32[8,128]{1,0:T(8,128)S(1)}, f32[8,128]{1,0:T(8,128)S(1)}, s32[8,128]{1,0:T(8,128)S(1)}, bf16[768,2048]{1,0:T(8,128)(2,1)S(1)}) %tuple.17), branch_computations={%region_0.1_spmd, %region_1.2_spmd} | conditional | flops 4096 | bytes 163968 | solution.py:400
  6.1 1.9 %collective-permute-start = (f32[8,128]{1,0:T(8,128)S(1)}, f32[8,128]{1,0:T(8,128)S(1)}, u32[]{:S(2)}, u32[]{:S(2)}) collective-permute-start(f32[8,128]{1,0:T(8,128)S(1)} %add.11), channel_id=1, source_target_pairs={{16,48},{17,49},{18,50},{19,51},{20,52},{21,53},{22,54},{23,55},{2... | collective-permute-start | bytes 12296 | tf_op jit(solution)/shard_map/cond/branch_1_fun/ppermute | solution.py:374
  8.0 2.4 %collective-permute-done = f32[8,128]{1,0:T(8,128)S(1)} collective-permute-done((f32[8,128]{1,0:T(8,128)S(1)}, f32[8,128]{1,0:T(8,128)S(1)}, u32[]{:S(2)}, u32[]{:S(2)}) %collective-permute-start) | collective-permute-done | bytes 4128 | tf_op jit(solution)/shard_map/cond/branch_1_fun/ppermute | solution.py:374
  10.4 3.3 %collective-permute-start.1 = (f32[8,128]{1,0:T(8,128)S(1)}, f32[8,128]{1,0:T(8,128)S(1)}, u32[]{:S(2)}, u32[]{:S(2)}) collective-permute-start(f32[8,128]{1,0:T(8,128)S(1)} %add.12), channel_id=1, source_target_pairs={{16,80},{17,81},{18,82},{19,83},{20,84},{21,85},{22,86},{23,87},{2... | collective-permute-start | bytes 12296 | tf_op jit(solution)/shard_map/cond/branch_1_fun/ppermute | solution.py:374
  13.8 1.9 %collective-permute-done.1 = f32[8,128]{1,0:T(8,128)S(1)} collective-permute-done((f32[8,128]{1,0:T(8,128)S(1)}, f32[8,128]{1,0:T(8,128)S(1)}, u32[]{:S(2)}, u32[]{:S(2)}) %collective-permute-start.1) | collective-permute-done | bytes 4128 | tf_op jit(solution)/shard_map/cond/branch_1_fun/ppermute | solution.py:374
  15.7 6.2 %collective-permute-start.2 = (f32[8,128]{1,0:T(8,128)S(1)}, f32[8,128]{1,0:T(8,128)S(1)}, u32[]{:S(2)}, u32[]{:S(2)}) collective-permute-start(f32[8,128]{1,0:T(8,128)S(1)} %add.13), channel_id=1, source_target_pairs={{16,208},{17,209},{18,210},{19,211},{20,212},{21,213},{22,214},{23... | collective-permute-start | bytes 12296 | tf_op jit(solution)/shard_map/cond/branch_1_fun/ppermute | solution.py:374
  21.9 1.3 %collective-permute-done.2 = f32[8,128]{1,0:T(8,128)S(1)} collective-permute-done((f32[8,128]{1,0:T(8,128)S(1)}, f32[8,128]{1,0:T(8,128)S(1)}, u32[]{:S(2)}, u32[]{:S(2)}) %collective-permute-start.2) | collective-permute-done | bytes 4128 | tf_op jit(solution)/shard_map/cond/branch_1_fun/ppermute | solution.py:374
  23.2 0.1 note.1
  23.3 0.0 copy-start
  23.3 0.0 copy-start.1
  23.3 30.2 %all_to_all.23 = bf16[16,48,2048]{2,1,0:T(8,128)(2,1)S(1)} all-to-all(bf16[16,48,2048]{2,1,0:T(8,128)(2,1)S(1)} %bitcast.11), channel_id=1, replica_groups=mesh['dp'=16,'expert'=16] {'expert'}, dimensions={0} | all-to-all | bytes 6291456 | tf_op jit(solution)/shard_map/all_to_all | solution.py:401
  53.6 0.2 select.3
  53.8 0.0 copy-done
  53.8 0.0 copy-done.1
  53.8 0.0 copy-start.2
  53.8 1.9 %hidden.1 = (bf16[768,768]{1,0:T(8,128)(2,1)S(1)}, f32[8,128]{1,0:T(8,128)S(1)}) custom-call(s32[8,128]{1,0:T(8,128)S(1)} %get-tuple-element.36.slot_ref, bf16[768,2048]{1,0:T(8,128)(2,1)S(1)} %bitcast.9, bf16[1,2048,768]{2,1,0:T(8,128)(2,1)S(1)} %copy-done, bf16[1,2048,768]{2,1,0:T(8,128)(2,1)S(1)} %copy-done.1), custom_call_target="tpu_custom_call" | custom-call | flops 4831838208 | bytes 9437184 | tf_op jit(solution)/shard_map/hidden/pallas_call | solution.py:200
  55.8 0.0 copy-done.2
  55.8 1.1 %down.1 = bf16[768,2048]{1,0:T(8,128)(2,1)S(1)} custom-call(s32[8,128]{1,0:T(8,128)S(1)} %get-tuple-element.36.slot_ref, f32[8,128]{1,0:T(8,128)S(1)} %get-tuple-element.42.loss_ref, bf16[768,768]{1,0:T(8,128)(2,1)S(1)} %get-tuple-element.43.x_ref, bf16[1,768,2048]{2,1,0:T(8,128)(2,1)S(1)} %copy-done.2), custom_call_target="tpu_custom_call" | custom-call | flops 2415919104 | bytes 6291456 | tf_op jit(solution)/shard_map/down/pallas_call | solution.py:247
  56.9 30.1 %all_to_all.24 = bf16[16,48,2048]{2,1,0:T(8,128)(2,1)S(1)} all-to-all(bf16[16,48,2048]{2,1,0:T(8,128)(2,1)S(1)} %bitcast.10), channel_id=1, replica_groups=mesh['dp'=16,'expert'=16] {'expert'}, dimensions={0} | all-to-all | bytes 6291456 | tf_op jit(solution)/shard_map/all_to_all | solution.py:407
  87.0 0.1 read.1.mine_ref
  87.1 0.0 collective-permute-start.4
  87.1 1.7 %combine.1 = bf16[128,2048]{1,0:T(8,128)(2,1)} custom-call(bf16[256,768]{1,0:T(8,128)(2,1)S(1)} %get-tuple-element.44.pick_ref, f32[128,128]{1,0:T(8,128)S(1)} %get-tuple-element.45.weight_ref, bf16[768,2048]{1,0:T(8,128)(2,1)S(1)} %bitcast.8), custom_call_target="tpu_custom_call" | custom-call | flops 805306368 | bytes 3145728 | tf_op jit(solution)/shard_map/combine/pallas_call | solution.py:355
  88.8 0.0 collective-permute-done.4.other_ref
  88.8 0.7 loss.1
  (4 shorter events, 0.0 us)
Async XLA Ops:
  1.7 4.3 %collective-permute-start.3 = (f32[8,128]{1,0:T(8,128)S(1)}, f32[8,128]{1,0:T(8,128)S(1)}, u32[]{:S(2)}, u32[]{:S(2)}) collective-permute-start(f32[8,128]{1,0:T(8,128)S(1)} %get-tuple-element.35), channel_id=1, source_target_pairs={{0,16},{1,17},{2,18},{3,19},{4,20},{5,21},{6,22},{7,23},{8,24},{9,... | collective-permute-start | bytes 12296 | tf_op jit(solution)/shard_map/ppermute | solution.py:391
  6.1 4.4 %collective-permute-start = (f32[8,128]{1,0:T(8,128)S(1)}, f32[8,128]{1,0:T(8,128)S(1)}, u32[]{:S(2)}, u32[]{:S(2)}) collective-permute-start(f32[8,128]{1,0:T(8,128)S(1)} %add.11), channel_id=1, source_target_pairs={{16,48},{17,49},{18,50},{19,51},{20,52},{21,53},{22,54},{23,55},{2... | collective-permute-start | bytes 12296 | tf_op jit(solution)/shard_map/cond/branch_1_fun/ppermute | solution.py:374
  10.4 5.2 %collective-permute-start.1 = (f32[8,128]{1,0:T(8,128)S(1)}, f32[8,128]{1,0:T(8,128)S(1)}, u32[]{:S(2)}, u32[]{:S(2)}) collective-permute-start(f32[8,128]{1,0:T(8,128)S(1)} %add.12), channel_id=1, source_target_pairs={{16,80},{17,81},{18,82},{19,83},{20,84},{21,85},{22,86},{23,87},{2... | collective-permute-start | bytes 12296 | tf_op jit(solution)/shard_map/cond/branch_1_fun/ppermute | solution.py:374
  15.7 7.5 %collective-permute-start.2 = (f32[8,128]{1,0:T(8,128)S(1)}, f32[8,128]{1,0:T(8,128)S(1)}, u32[]{:S(2)}, u32[]{:S(2)}) collective-permute-start(f32[8,128]{1,0:T(8,128)S(1)} %add.13), channel_id=1, source_target_pairs={{16,208},{17,209},{18,210},{19,211},{20,212},{21,213},{22,214},{23... | collective-permute-start | bytes 12296 | tf_op jit(solution)/shard_map/cond/branch_1_fun/ppermute | solution.py:374
  23.3 30.5 %copy-start = (bf16[1,2048,768]{2,1,0:T(8,128)(2,1)S(1)}, bf16[1,2048,768]{2,1,0:T(8,128)(2,1)}, u32[]{:S(2)}) copy-start(bf16[1,2048,768]{2,1,0:T(8,128)(2,1)} %gate_ref.1) | copy-start | bytes 9437188
  23.3 30.5 %copy-start.1 = (bf16[1,2048,768]{2,1,0:T(8,128)(2,1)S(1)}, bf16[1,2048,768]{2,1,0:T(8,128)(2,1)}, u32[]{:S(2)}) copy-start(bf16[1,2048,768]{2,1,0:T(8,128)(2,1)} %up_ref.1) | copy-start | bytes 9437188
  53.8 2.0 %copy-start.2 = (bf16[1,768,2048]{2,1,0:T(8,128)(2,1)S(1)}, bf16[1,768,2048]{2,1,0:T(8,128)(2,1)}, u32[]{:S(2)}) copy-start(bf16[1,768,2048]{2,1,0:T(8,128)(2,1)} %down_ref.1) | copy-start | bytes 9437188
  87.1 1.8 %collective-permute-start.4 = (f32[8,128]{1,0:T(8,128)S(1)}, f32[8,128]{1,0:T(8,128)S(1)}, u32[]{:S(2)}, u32[]{:S(2)}) collective-permute-start(f32[8,128]{1,0:T(8,128)S(1)} %read.1.mine_ref), channel_id=1, source_target_pairs={{0,16},{1,17},{2,18},{3,19},{4,20},{5,21},{6,22},{7,23},{8,24},{9,... | collective-permute-start | bytes 12296 | tf_op jit(solution)/shard_map/ppermute | solution.py:409
